TPU v7x, 32 devices: a whole 2x2x4 slice. The times are simulated.
32 devices in a mesh: ctx: 16 (over z, x, core), mp: 2 (over y).
Axes of the slice: x: 2, y: 2, z: 4, core: 2. Of those that a mesh axis runs over, the one named last changes fastest.
Arguments:
- byte_qkv: bfloat16 [8192, 3, 4096], P('ctx', None, 'mp'), may hold values from -14 to 14
- kv_weight: bfloat16 [4096, 2, 4096], P(None, None, 'mp'), may hold values from -4 to 4
- patch_bounds: int32 [16, 161], replicated, may hold values from 0 to 8192, as said below
Outputs:
- mixed: bfloat16 [2560, 4096], P('ctx', 'mp')
Inputs may be any that keep to these rules, and one draw needn't show every extreme that they name: `patch_bounds`: row c lists in increasing order the first bytes of the patches that begin in bytes c * 512 to (c + 1) * 512 - 1, then the end of its last patch, repeated to the end of the row. The patches cover all 8192 bytes, each is 1 to 16 bytes long, one is exactly 16 long, and some row lists exactly 160 patches.
All inputs are finite; a program needn't handle non-finite values.
Results may differ from a plain program's by a relative error of at most 0.002.
The roundings to bfloat16 on the way count: a program that leaves them out, or rounds other values in their place, can miss the bound.
Values may be sent and summed in bfloat16 or wider, within the bound.
No kernel may reach another device: no remote copies, remote signals or barrier semaphores. Data moves between devices by JAX's collectives and lax.ppermute only.
A program may use at most 192 MiB of HBM per device.

v0:
```python
import math

import jax
import jax.numpy as jnp
from jax import lax
from jax.sharding import PartitionSpec as P

D = 4096
HEADS = 32
WIN = 16


masked_score = -1e30


def passed_along(value, axis, steps):
    count = lax.axis_size(axis)
    initial, last = (max(0, -steps), min(count, count - steps))
    return lax.ppermute(value, axis, [(source, source + steps) for source in range(initial, last)])


def shards(byte_qkv, kv_weight, patch_bounds):
    byte_rows = byte_qkv.shape[0]
    col_width = byte_qkv.shape[2]
    head_dim = D // HEADS
    heads_here = col_width // head_dim
    slot_count = patch_bounds.shape[1] - 1
    score_scale = 1.0 / math.sqrt(head_dim)
    ctx_place = lax.axis_index("ctx")
    my_bounds = lax.dynamic_index_in_dim(patch_bounds, ctx_place, 0, keepdims=False)
    starts = my_bounds[:slot_count]
    lengths = my_bounds[1:] - starts
    live_slot = lengths > 0
    edge_rows = passed_along(byte_qkv[:WIN], "ctx", -1)
    extended = jnp.concatenate([byte_qkv, edge_rows], axis=0)
    offsets = jnp.arange(WIN, dtype=jnp.int32)
    local_start = jnp.clip(starts - ctx_place * byte_rows, 0, byte_rows)
    window = extended[local_start[:, None] + offsets[None, :]]
    window = window.reshape(slot_count, WIN, 3, heads_here, head_dim)
    inside = offsets[None, :] < lengths[:, None]
    queries = jnp.max(jnp.where(inside[:, :, None, None], window[:, :, 0], -jnp.inf), axis=1)
    queries = jnp.where(live_slot[:, None, None], queries, 0)
    scores = (
        jnp.einsum("shd,swhd->shw", queries, window[:, :, 1], preferred_element_type=jnp.float32)
        * score_scale
    )
    scores = jnp.where(inside[:, None, :], scores, masked_score)
    scores = scores - jnp.max(scores, axis=2, keepdims=True)
    exp_terms = jnp.exp(scores)
    weights = (exp_terms / jnp.sum(exp_terms, axis=2, keepdims=True)).astype(jnp.bfloat16)
    pooled = jnp.einsum(
        "shw,swhd->shd", weights, window[:, :, 2], preferred_element_type=jnp.float32
    )
    patch_state = (
        jnp.where(live_slot[:, None, None], pooled, 0.0)
        .astype(jnp.bfloat16)
        .reshape(slot_count, col_width)
    )
    flat_weight = kv_weight.reshape(kv_weight.shape[0], 2 * col_width)
    projected = jnp.dot(
        lax.all_gather(patch_state, "mp", axis=1, tiled=True),
        flat_weight,
        preferred_element_type=jnp.float32,
    )
    key_value = projected.astype(jnp.bfloat16)
    query_heads = patch_state.reshape(slot_count, heads_here, head_dim)
    query_slot = ctx_place * slot_count + jnp.arange(slot_count, dtype=jnp.int32)
    valid_all = (patch_bounds[:, 1:] > patch_bounds[:, :-1]).reshape(-1)
    shard_piece = lax.all_gather(key_value, "ctx", axis=0, tiled=True)
    top_score = jnp.full((heads_here, slot_count), masked_score, jnp.float32)
    piece_rows = shard_piece.shape[0]
    key_part = shard_piece[:, :col_width].reshape(piece_rows, heads_here, head_dim)
    value_part = shard_piece[:, col_width:].reshape(piece_rows, heads_here, head_dim)
    key_slot = jnp.arange(piece_rows, dtype=jnp.int32)
    visible = (key_slot[None, :] <= query_slot[:, None]) & valid_all[None, :]
    global_scores = (
        jnp.einsum("qhd,khd->hqk", query_heads, key_part, preferred_element_type=jnp.float32)
        * score_scale
    )
    global_scores = jnp.where(visible[None], global_scores, masked_score)
    new_top = jnp.maximum(top_score, jnp.max(global_scores, axis=2))
    exp_part = jnp.where(visible[None], jnp.exp(global_scores - new_top[:, :, None]), 0.0)
    denom_sum = jnp.sum(exp_part, axis=2)
    weighted = jnp.einsum(
        "hqk,khd->hqd", exp_part, value_part.astype(jnp.float32), precision=lax.Precision.HIGHEST
    )
    fold_state = (new_top, denom_sum, weighted)
    top_score, denom_sum, weighted = fold_state
    safe_total = jnp.where(denom_sum > 0, denom_sum, 1.0)
    attended = (weighted / safe_total[:, :, None]).transpose(1, 0, 2).reshape(slot_count, col_width)
    attended = jnp.where(live_slot[:, None], attended, 0.0)
    return (patch_state.astype(jnp.float32) + attended).astype(jnp.bfloat16)


def solution(mesh):
    return jax.shard_map(
        shards,
        mesh=mesh,
        in_specs=(P("ctx", None, "mp"), P(None, None, "mp"), P()),
        out_specs=P("ctx", "mp"),
        check_vma=False,
    )
```

profile of v0, /device:TPU:0, one launch (start us, length us, event | category | flops | bytes accessed | tf_op | source)
XLA Modules:
  0.0 464.5 jit_solution(7453595683164272935)
XLA Ops:
  6.5 11.4 %copy.29 = bf16[512,3,2048]{2,1,0:T(4,128)(2,1)} copy(bf16[512,3,2048]{2,0,1:T(8,128)(2,1)} %param.3) | data formatting | bytes 12582912 | tf_op args[0]
  17.9 1.0 slice.44
  19.0 1.5 collective-permute-start
  20.5 0.1 dynamic-slice_subtract_fusion
  20.6 0.1 compare_select_fusion
  20.7 0.1 reshape.193
  20.8 0.1 iota_compare_fusion.1
  21.0 1.5 collective-permute-done
  22.4 8.5 %pad_maximum_fusion = bf16[528,3,2048]{2,1,0:T(4,128)(2,1)} fusion(bf16[16,3,2048]{2,1,0:T(4,128)(2,1)S(1)} %collective-permute-done, bf16[512,3,2048]{2,1,0:T(4,128)(2,1)} %copy.29), kind=kLoop, calls=%fused_computation.29 | loop fusion | flops 3244032 | bytes 12976128 | tf_op jit(solution)/shard_map/concatenate | solution.py:35
  31.0 79.1 %gather_fusion = bf16[2560,3,2048]{2,1,0:T(4,128)(2,1)} fusion(bf16[528,3,2048]{2,1,0:T(4,128)(2,1)} %pad_maximum_fusion, s32[3072]{0:T(1024)S(1)} %pad_clamp_fusion), kind=kCustom, calls=%fused_computation | custom fusion | bytes 62924800 | tf_op jit(solution)/shard_map/gather | solution.py:38
  110.1 82.1 %reshape.205 = bf16[160,16,3,16,128]{4,3,2,1,0:T(8,128)(2,1)} reshape(bf16[2560,3,2048]{2,1,0:T(4,128)(2,1)} %gather_fusion) | data formatting | bytes 62914560 | tf_op jit(solution)/shard_map/reshape | solution.py:39
  192.2 5.7 %fusion.16 = bf16[160,16,128]{2,1,0:T(8,128)(2,1)S(1)} fusion(bf16[160,16,3,16,128]{4,3,2,1,0:T(8,128)(2,1)} %reshape.205, pred[160,16]{1,0:T(8,128)(4,1)S(1)} %iota_compare_fusion.1), kind=kLoop, calls=%fused_computation.24 | loop fusion | flops 10158080 | bytes 11143680 | tf_op jit(solution)/shard_map/reduce_max | solution.py:41
  197.9 18.7 %slice_bitcast_fusion.2 = (bf16[160,16,16,128]{3,2,1,0:T(8,128)(2,1)}, bf16[160,16,16,128]{3,2,1,0:T(8,128)(2,1)}) fusion(bf16[160,16,3,16,128]{4,3,2,1,0:T(8,128)(2,1)} %reshape.205), kind=kLoop, calls=%fused_computation.20 | loop fusion | bytes 41943040 | tf_op jit(solution)/shard_map/squeeze | solution.py:52
  216.7 0.2 select_bitcast_fusion
  216.9 8.1 %fusion.19 = f32[160,16,1,16]{3,2,1,0:T(1,128)S(1)} fusion(bf16[160,16,16,128]{3,2,1,0:T(8,128)(2,1)} %get-tuple-element.6, bf16[160,16,128,1]{2,1,0,3:T(8,128)(2,1)S(1)} %select_bitcast_fusion), kind=kOutput, calls=%fused_computation.27 | convolution fusion | flops 10485760 | bytes 11304960 | tf_op jit(solution)/shard_map/shd,swhd->shw/dot_general | solution.py:44
  225.1 0.9 copy.37
  226.0 0.1 fusion.32
  226.2 1.1 copy.38
  227.2 7.1 %fusion.17 = f32[160,16,1,128]{3,2,1,0:T(1,128)S(1)} fusion(bf16[160,16,16,1]{2,3,1,0:T(2,128)(2,1)S(1)} %copy.38, bf16[160,16,16,128]{3,2,1,0:T(8,128)(2,1)} %get-tuple-element.5), kind=kOutput, calls=%fused_computation.25 | convolution fusion | flops 10485760 | bytes 11878400 | tf_op jit(solution)/shard_map/shw,swhd->shd/dot_general | solution.py:51
  234.3 0.2 select_convert_fusion
  234.6 1.0 copy.78
  235.7 23.5 %copy.49 = bf16[512,8,2,2048]{3,1,2,0:T(8,128)(2,1)} copy(bf16[512,8,2,2048]{3,2,1,0:T(2,128)(2,1)} %bitcast.76) | data formatting | bytes 67108864
  259.1 6.6 %all-gather.3.cloned.1.call-done = bf16[160,4096]{1,0:T(8,128)(2,1)} async-done(((bf16[160,2048]{1,0:T(8,128)(2,1)}), bf16[160,4096]{1,0:T(8,128)(2,1)}) %all-gather.3.cloned.1.call-update) | async-done | bytes 1310736 | tf_op jit(solution)/shard_map/all_gather | solution.py:61
  265.8 14.9 %convolution_convert_fusion = bf16[160,4096]{1,0:T(8,128)(2,1)} fusion(bf16[160,4096]{1,0:T(8,128)(2,1)} %all-gather.3.cloned.1.call-done, bf16[4096,4096]{1,0:T(8,128)(2,1)} %bitcast.77), kind=kOutput, calls=%fused_computation.30 | convolution fusion | flops 5369364480 | bytes 36175872 | tf_op jit(solution)/shard_map/dot_general | solution.py:60
  280.7 0.1 and.15
  280.8 0.3 fusion.21
  281.2 108.5 %all-gather.5.cloned.1.call-done = bf16[2560,4096]{1,0:T(8,128)(2,1)} async-done(((bf16[160,4096]{1,0:T(8,128)(2,1)}), bf16[2560,4096]{1,0:T(8,128)(2,1)}) %all-gather.5.cloned.1.call-update) | async-done | bytes 20971536 | tf_op jit(solution)/shard_map/all_gather | solution.py:69
  389.7 16.5 %slice_bitcast_fusion = (bf16[320,16,8,128]{3,2,1,0:T(8,128)(2,1)}, bf16[320,16,8,128]{3,2,1,0:T(8,128)(2,1)}) fusion(bf16[2560,4096]{1,0:T(8,128)(2,1)} %all-gather.5.cloned.1.call-done), kind=kLoop, calls=%fused_computation.18 | loop fusion | bytes 41943040
  406.1 14.6 %fusion.2 = (f32[16,160]{1,0:T(8,128)S(1)}, f32[16,160,2560]{2,1,0:T(8,128)}) fusion(pred[160,2560]{1,0:T(8,128)(4,1)S(1)} %fusion.21, bf16[320,16,8,128]{3,2,1,0:T(8,128)(2,1)} %get-tuple-element.8, bf16[160,16,128]{2,1,0:T(8,128)(2,1)S(1)} %select_convert_fusion), kind=kOutput, calls=%fused_computation.5 | convolution fusion | flops 1697379840 | bytes 37775360 | tf_op jit(solution)/shard_map/qhd,khd->hqk/dot_general | solution.py:77
  420.7 13.8 %fusion.3 = f32[16,160]{1,0:T(8,128)S(1)} fusion(f32[16,160,2560]{2,1,0:T(8,128)} %get-tuple-element.12, f32[16,160]{1,0:T(8,128)S(1)} %broadcast_maximum_fusion, pred[160,2560]{1,0:T(8,128)(4,1)S(1)} %fusion.21), kind=kLoop, calls=%fused_computation.6 | loop fusion | flops 32765440 | bytes 26644480 | tf_op jit(solution)/shard_map/reduce_sum | solution.py:83
  434.5 22.0 %divide_bitcast_fusion = f32[16,20,8,128]{3,2,1,0:T(8,128)S(1)} fusion(f32[160,16]{0,1:T(8,128)S(1)} %compare_select_fusion.1, bf16[320,16,8,128]{3,2,1,0:T(8,128)(2,1)} %get-tuple-element.7, f32[16,160,2560]{2,1,0:T(8,128)} %get-tuple-element.12, f32[16,160]{1,0:T(8,128)S(1)} %broadcast_maximum_fusion, pred[160,2560]{1,0:T(8,128)(4,1)S(1)} %fusion.21), kind=kOutput, calls=%fused_computation.38 | convolution fusion | flops 10092871680 | bytes 38440960 | tf_op jit(solution)/shard_map/hqk,khd->hqd/dot_general | solution.py:84
  456.6 1.1 fusion.26
  (13 shorter events, 0.3 us)
Async XLA Ops:
  6.5 14.0 %copy-start = (s32[16,161]{1,0:T(8,128)S(1)}, s32[16,161]{1,0:T(8,128)}, u32[]{:S(2)}) copy-start(s32[16,161]{1,0:T(8,128)} %param.5) | copy-start | bytes 30916
  6.5 259.2 %all-gather.3.cloned.1.call-start = ((), (), s32[]{:S(2)}) async-start(), calls=%async_computation | async-start | bytes 1966080 | tf_op jit(solution)/shard_map/all_gather | solution.py:61
  19.0 3.4 collective-permute-start
  235.6 154.1 %all-gather.5.cloned.1.call-start = ((), (), s32[]{:S(2)}) async-start(), calls=%async_computation.1 | async-start | bytes 22282240 | tf_op jit(solution)/shard_map/all_gather | solution.py:69
Sparse Core Ops, SparseCore 0:
  235.7 30.0 all-gather.2
  280.8 108.8 all-gather.4
where the time goes:
time: 467 us; the launch traced here: 464 us
  local copies, waits for them, and re-layouts  236 us (51%)
  waiting for transfers between devices  117 us (25%)
  matrix products  66.7 us (14%)
  other arithmetic  30.5 us (7%)
  between operations  13.6 us (3%)
    all_gather x1, waiting for transfers between devices, shards(): shard_piece = lax.all_gather(key_value, 'ctx', axis=0, tiled=True)  108 us
    reshape x1, local copies, waits for them, and re-layouts, shards(): window = window.reshape(slot_count, WIN, 3, heads_here, head_dim)  82.1 us
    gather x1, local copies, waits for them, and re-layouts, shards(): window = extended[local_start[:, None] + offsets[None, :]]  79.1 us
    unnamed x6, local copies, waits for them, and re-layouts  52.4 us
    dot_general x1, matrix products, shards(): jnp.einsum('hqk,khd->hqd', exp_part, value_part.astype(jnp.float32), prec...  22 us
    squeeze x1, local copies, waits for them, and re-layouts, shards(): window[:, :, 2]  18.7 us
    dot_general x1, matrix products, shards(): jnp.dot(lax.all_gather(patch_state, 'mp', axis=1, tiled=True), flat_weigh...  14.9 us
    dot_general x1, matrix products, shards(): jnp.einsum('qhd,khd->hqk', query_heads, key_part, preferred_element_type=...  14.6 us
  transfers between devices with their start and end apart: 3, of which 3 were waited for; matrix products, arithmetic and copies ran while one was open for 5% of the time, Pallas kernels for 0%

commit v1 on v0

v1 whole, which is shorter than its diff:
```python
import functools
import math

import jax
import jax.numpy as jnp
from jax import lax
from jax.experimental import pallas as pl
from jax.experimental.pallas import tpu as pltpu
from jax.sharding import PartitionSpec as P

D = 4096
HEADS = 32
WIN = 16
HEAD = D // HEADS
SCALE = 1.0 / math.sqrt(HEAD)
MASKED = -1e30
VMEM_LIMIT = 56 * 1024 * 1024


def params():
    return pltpu.CompilerParams(vmem_limit_bytes=VMEM_LIMIT)


def dot_f32(left, right, right_dim=0):
    return lax.dot_general(
        left, right, (((1,), (right_dim,)), ((), ())), preferred_element_type=jnp.float32
    )


def patch_body(heads, place_ref, bounds_ref, main_ref, edge_ref, out_ref, pens, bias, pick, live):
    byte_rows = main_ref.shape[1]
    slots = out_ref.shape[0]
    rows = byte_rows + WIN
    entries = bounds_ref.shape[1]

    @pl.when(pl.program_id(0) == 0)
    def _():
        place = place_ref[0]
        local = (bounds_ref[pl.ds(place, 1), :] - place * byte_rows).astype(jnp.float32)
        entry = lax.broadcasted_iota(jnp.int32, (slots, entries), 1)
        slot = lax.broadcasted_iota(jnp.int32, (slots, entries), 0)
        first = jnp.sum(jnp.where(entry == slot, local, 0.0), axis=1, keepdims=True)
        after = jnp.sum(jnp.where(entry == slot + 1, local, 0.0), axis=1, keepdims=True)
        byte = lax.broadcasted_iota(jnp.int32, (slots, rows), 1).astype(jnp.float32)
        inside = (byte >= first) & (byte < after)
        bias[...] = jnp.where(inside, 0.0, MASKED)
        pick[...] = jnp.where(inside & (byte == first), 1.0, 0.0).astype(jnp.bfloat16)
        live[...] = jnp.where(after > first, 1.0, 0.0)
        at = lax.broadcasted_iota(jnp.int32, (rows, entries), 0).astype(jnp.float32)
        begins = jnp.max(jnp.where(at == local, 1.0, 0.0), axis=1, keepdims=True)
        pen = jnp.broadcast_to(jnp.where(begins > 0.0, -jnp.inf, 0.0), (rows, HEAD))
        pen = pltpu.roll(pen, rows - 1, 0)
        pens[0] = pen
        for level in range(1, 4):
            pen = pen + pltpu.roll(pen, rows - (1 << (level - 1)), 0)
            pens[level] = pen

    for head in range(heads):
        cols = slice(head * HEAD, (head + 1) * HEAD)
        top = jnp.concatenate([main_ref[0, :, cols], edge_ref[0, :, cols]], axis=0).astype(jnp.float32)
        for level in range(4):
            top = jnp.maximum(top, pltpu.roll(top, rows - (1 << level), 0) + pens[level])
        query = dot_f32(pick[...], top.astype(jnp.bfloat16)).astype(jnp.bfloat16)
        keys = jnp.concatenate([main_ref[1, :, cols], edge_ref[1, :, cols]], axis=0)
        values = jnp.concatenate([main_ref[2, :, cols], edge_ref[2, :, cols]], axis=0)
        scores = dot_f32(query, keys, 1) * SCALE + bias[...]
        terms = jnp.exp(scores - jnp.max(scores, axis=1, keepdims=True))
        total = jnp.sum(terms, axis=1, keepdims=True)
        weights = (terms * (live[...] / total)).astype(jnp.bfloat16)
        out_ref[:, cols] = dot_f32(weights, values).astype(jnp.bfloat16)


def patch_states(place, bounds, parts, edge, first_head, head_count, slots):
    byte_rows = parts.shape[1]
    rows = byte_rows + WIN
    group = 2 if head_count % 2 == 0 else 1
    skip = first_head // group
    width = group * HEAD
    return pl.pallas_call(
        functools.partial(patch_body, group),
        grid=(head_count // group,),
        in_specs=[
            pl.BlockSpec(memory_space=pltpu.SMEM),
            pl.BlockSpec(bounds.shape, lambda i: (0, 0)),
            pl.BlockSpec((3, byte_rows, width), lambda i: (0, 0, i + skip)),
            pl.BlockSpec((3, WIN, width), lambda i: (0, 0, i + skip)),
        ],
        out_specs=pl.BlockSpec((slots, width), lambda i: (0, i)),
        out_shape=jax.ShapeDtypeStruct((slots, head_count * HEAD), jnp.bfloat16),
        scratch_shapes=[
            pltpu.VMEM((4, rows, HEAD), jnp.float32),
            pltpu.VMEM((slots, rows), jnp.float32),
            pltpu.VMEM((slots, rows), jnp.bfloat16),
            pltpu.VMEM((slots, 1), jnp.float32),
        ],
        compiler_params=params(),
        name="patch_states",
    )(place, bounds, parts, edge)


def project_body(start_ref, states_ref, weight_ref, sums_ref):
    width = weight_ref.shape[2]

    @pl.when(pl.program_id(0) == 0)
    def _():
        sums_ref[...] = jnp.zeros_like(sums_ref)

    states = states_ref[...]
    sums_ref[:, :width] += dot_f32(states, weight_ref[:, 0, :])
    sums_ref[:, width:] += dot_f32(states, weight_ref[:, 1, :])


def project_more_body(start_ref, states_ref, weight_ref, before_ref, own_ref, out_ref, sums):
    width = weight_ref.shape[2]

    @pl.when(pl.program_id(0) == 0)
    def _():
        sums[...] = before_ref[...]

    states = states_ref[...]
    sums[:, :width] += dot_f32(states, weight_ref[:, 0, :])
    sums[:, width:] += dot_f32(states, weight_ref[:, 1, :])

    @pl.when(pl.program_id(0) == pl.num_programs(0) - 1)
    def _():
        for head in range(width // HEAD):
            cols = slice(head * HEAD, (head + 1) * HEAD)
            out_ref[head, :, :HEAD] = own_ref[:, cols]
            out_ref[head, :, HEAD : 2 * HEAD] = sums[:, cols].astype(jnp.bfloat16)
            out_ref[head, :, 2 * HEAD :] = sums[:, width + head * HEAD : width + (head + 1) * HEAD].astype(
                jnp.bfloat16
            )


def feature_chunk(count):
    return next(c for c in (512, 256, 128) if count % c == 0)


def project(start, states, weight):
    slots, count = states.shape
    width = weight.shape[2]
    chunk = feature_chunk(count)
    return pl.pallas_call(
        project_body,
        grid_spec=pltpu.PrefetchScalarGridSpec(
            num_scalar_prefetch=1,
            grid=(count // chunk,),
            in_specs=[
                pl.BlockSpec((slots, chunk), lambda i, start: (0, i)),
                pl.BlockSpec((chunk, 2, width), lambda i, start: (start[0] * (count // chunk) + i, 0, 0)),
            ],
            out_specs=pl.BlockSpec((slots, 2 * width), lambda i, start: (0, 0)),
        ),
        out_shape=jax.ShapeDtypeStruct((slots, 2 * width), jnp.float32),
        compiler_params=params(),
        name="project",
    )(start, states, weight)


def project_more(start, states, weight, before, own):
    slots, count = states.shape
    width = weight.shape[2]
    chunk = feature_chunk(count)
    heads = width // HEAD
    return pl.pallas_call(
        project_more_body,
        grid_spec=pltpu.PrefetchScalarGridSpec(
            num_scalar_prefetch=1,
            grid=(count // chunk,),
            in_specs=[
                pl.BlockSpec((slots, chunk), lambda i, start: (0, i)),
                pl.BlockSpec((chunk, 2, width), lambda i, start: (start[0] * (count // chunk) + i, 0, 0)),
                pl.BlockSpec((slots, 2 * width), lambda i, start: (0, 0)),
                pl.BlockSpec((slots, width), lambda i, start: (0, 0)),
            ],
            out_specs=pl.BlockSpec((heads, slots, 3 * HEAD), lambda i, start: (0, 0, 0)),
            scratch_shapes=[pltpu.VMEM((slots, 2 * width), jnp.float32)],
        ),
        out_shape=jax.ShapeDtypeStruct((heads, slots, 3 * HEAD), jnp.bfloat16),
        compiler_params=params(),
        name="project_more",
    )(start, states, weight, before, own)


def attend_body(block, bias_ref, qkv_ref, out_ref, values):
    slots = qkv_ref.shape[0]
    values[:, :HEAD] = qkv_ref[:, 2 * HEAD :]
    values[:, HEAD:] = jnp.ones((slots, HEAD), jnp.bfloat16)
    row = lax.broadcasted_iota(jnp.int32, (block, block), 0)
    col = lax.broadcasted_iota(jnp.int32, (block, block), 1)
    later = jnp.where(col <= row, 0.0, MASKED)
    for at in range(0, slots, block):
        seen = at + block
        query = qkv_ref[at:seen, :HEAD]
        scores = dot_f32(query, qkv_ref[:seen, HEAD : 2 * HEAD], 1) * SCALE + bias_ref[:, :seen]
        last = scores[:, at:] + later
        scores = last if at == 0 else jnp.concatenate([scores[:, :at], last], axis=1)
        terms = jnp.exp(scores - jnp.max(scores, axis=1, keepdims=True))
        high = terms.astype(jnp.bfloat16)
        low = (terms - high.astype(jnp.float32)).astype(jnp.bfloat16)
        summed = dot_f32(high, values[:seen]) + dot_f32(low, values[:seen])
        mixed = query.astype(jnp.float32) + summed[:, :HEAD] / summed[:, HEAD:]
        out_ref[at:seen] = mixed.astype(jnp.bfloat16)


def attend(bias, qkv):
    slots = qkv.shape[0]
    block = next(b for b in (256, 128) if slots % b == 0)
    return pl.pallas_call(
        functools.partial(attend_body, block),
        out_shape=jax.ShapeDtypeStruct((slots, HEAD), jnp.bfloat16),
        scratch_shapes=[pltpu.VMEM((slots, 2 * HEAD), jnp.bfloat16)],
        compiler_params=params(),
        name="attend",
    )(bias, qkv)


def attend_gathered(place, valid, queries, keys, values):
    slots, width = queries.shape
    heads = width // HEAD
    keys = lax.all_gather(keys, "ctx", axis=0, tiled=True)
    values = lax.all_gather(values, "ctx", axis=0, tiled=True)
    total = keys.shape[0]
    query_slot = place * slots + jnp.arange(slots, dtype=jnp.int32)
    visible = (jnp.arange(total, dtype=jnp.int32)[None, :] <= query_slot[:, None]) & valid[None, :]
    scores = jnp.einsum(
        "qhd,khd->hqk",
        queries.reshape(slots, heads, HEAD),
        keys.reshape(total, heads, HEAD),
        preferred_element_type=jnp.float32,
    )
    scores = jnp.where(visible[None], scores * SCALE, MASKED)
    terms = jnp.where(visible[None], jnp.exp(scores - jnp.max(scores, axis=2, keepdims=True)), 0.0)
    sums = jnp.sum(terms, axis=2)
    attended = jnp.einsum(
        "hqk,khd->hqd",
        terms,
        values.reshape(total, heads, HEAD).astype(jnp.float32),
        precision=lax.Precision.HIGHEST,
    )
    attended = attended / jnp.where(sums > 0, sums, 1.0)[:, :, None]
    attended = attended.transpose(1, 0, 2).reshape(slots, width)
    return (queries.astype(jnp.float32) + attended).astype(jnp.bfloat16)


def shards(byte_qkv, kv_weight, patch_bounds):
    width = byte_qkv.shape[2]
    heads = width // HEAD
    slots = patch_bounds.shape[1] - 1
    ctx_count, mp_count = lax.axis_size("ctx"), lax.axis_size("mp")
    place = lax.axis_index("ctx").astype(jnp.int32)
    half = lax.axis_index("mp").astype(jnp.int32)

    edge = lax.ppermute(byte_qkv[:WIN], "ctx", [(i + 1, i) for i in range(ctx_count - 1)])
    parts = byte_qkv.transpose(1, 0, 2)
    edge = edge.transpose(1, 0, 2)
    states = patch_states(place[None], patch_bounds, parts, edge, 0, heads, slots)

    if mp_count == 2:
        others = lax.ppermute(states, "mp", [(0, 1), (1, 0)])
        before = project(half[None], states, kv_weight)
        other_half = 1 - half
    else:
        others = lax.all_gather(states, "mp", axis=1, tiled=True)
        before = jnp.zeros((slots, 2 * width), jnp.float32)
        other_half = jnp.zeros_like(half)
    qkv = project_more(other_half[None], others, kv_weight, before, states)

    valid = patch_bounds[:, 1:] > patch_bounds[:, :-1]
    if ctx_count == heads:
        bias = jnp.where(valid, 0.0, MASKED).astype(jnp.float32).reshape(1, ctx_count * slots)
        mine = lax.all_to_all(qkv, "ctx", 0, 0, tiled=True).reshape(ctx_count * slots, 3 * HEAD)
        mixed = attend(bias, mine).reshape(ctx_count, slots, HEAD)
        mixed = lax.all_to_all(mixed, "ctx", 0, 0, tiled=True)
        mixed = mixed.transpose(1, 0, 2).reshape(slots, width)
    else:
        keys = qkv[:, :, HEAD : 2 * HEAD].transpose(1, 0, 2).reshape(slots, width)
        values = qkv[:, :, 2 * HEAD :].transpose(1, 0, 2).reshape(slots, width)
        mixed = attend_gathered(place, valid.reshape(-1), states, keys, values)
    live = lax.dynamic_index_in_dim(valid, place, 0, keepdims=False)
    return jnp.where(live[:, None], mixed, jnp.zeros_like(mixed))


def solution(mesh):
    return jax.shard_map(
        shards,
        mesh=mesh,
        in_specs=(P("ctx", None, "mp"), P(None, None, "mp"), P()),
        out_specs=P("ctx", "mp"),
        check_vma=False,
    )
```

time: 467 us -> 201 us (0.43)
  local copies, waits for them, and re-layouts: 236 us -> 4.46 us
  Pallas kernels: 0 us -> 115 us
  matrix products: 66.7 us -> 0 us
  waiting for transfers between devices: 117 us -> 56.6 us
  other arithmetic: 30.5 us -> 1.1 us
  starting transfers between devices: 1.52 us -> 23.7 us
  between operations: 13.6 us -> 0.05 us
    all_gather x2 -> x0, waiting for transfers between devices: 115 us -> none  [the longest x1 108 us: shards(): shard_piece = lax.all_gather(key_value, 'ctx', axis=0, tiled=True)]
    pallas_call x0 -> x4, Pallas kernels: none -> 115 us  [the longest x1 44.5 us: project_more(): pl.pallas_call(project_more_body, grid_spec=pltpu.PrefetchScalarGridSpec(...]
    reshape x1, local copies, waits for them, and re-layouts: 82.1 us -> 0.68 us  [shards(): jnp.where(valid, 0.0, MASKED).astype(jnp.float32)]
    gather x1 -> x0, local copies, waits for them, and re-layouts: 79.1 us -> none  [shards(): window = extended[local_start[:, None] + offsets[None, :]]]
    dot_general x5 -> x0, matrix products: 66.7 us -> none  [the longest x1 22 us: shards(): jnp.einsum('hqk,khd->hqd', exp_part, value_part.astype(jnp.float32), prec...]
    all_to_all x0 -> x2, waiting for transfers between devices: none -> 54.6 us  [the longest x1 38 us: shards(): lax.all_to_all(qkv, 'ctx', 0, 0, tiled=True)]
    unnamed x6 -> x8, local copies, waits for them, and re-layouts: 52.4 us -> 2.81 us
    all_to_all x0 -> x2, starting transfers between devices: none -> 19.4 us  [the longest x1 10.7 us: shards(): mixed = lax.all_to_all(mixed, 'ctx', 0, 0, tiled=True)]
  transfers between devices with their start and end apart: 3 -> 4, of which waited for: 3 -> 3; matrix products, arithmetic and copies ran while one was open for 5% -> 0% of each run, Pallas kernels for 0% -> 22%
where the time goes in v1:
time: 201 us
  Pallas kernels  115 us (57%)
  waiting for transfers between devices  56.6 us (28%)
  starting transfers between devices  23.7 us (12%)
  local copies, waits for them, and re-layouts  4.46 us (2%)
    pallas_call x1, Pallas kernels, project_more(): pl.pallas_call(project_more_body, grid_spec=pltpu.PrefetchScalarGridSpec(...  44.5 us
    pallas_call x1, Pallas kernels, project(): pl.pallas_call(project_body, grid_spec=pltpu.PrefetchScalarGridSpec(num_s...  43.5 us
    all_to_all x1, waiting for transfers between devices, shards(): lax.all_to_all(qkv, 'ctx', 0, 0, tiled=True)  38 us
    all_to_all x1, waiting for transfers between devices, shards(): mixed = lax.all_to_all(mixed, 'ctx', 0, 0, tiled=True)  16.6 us
    pallas_call x1, Pallas kernels, patch_states(): pl.pallas_call(functools.partial(patch_body, group), grid=(head_count //...  15.5 us
    pallas_call x1, Pallas kernels, attend(): pl.pallas_call(functools.partial(attend_body, block), out_shape=jax.Shape...  11.6 us
    all_to_all x1, starting transfers between devices, shards(): mixed = lax.all_to_all(mixed, 'ctx', 0, 0, tiled=True)  10.7 us
    all_to_all x1, starting transfers between devices, shards(): lax.all_to_all(qkv, 'ctx', 0, 0, tiled=True)  8.74 us
  transfers between devices with their start and end apart: 4, of which 3 were waited for; matrix products, arithmetic and copies ran while one was open for 0% of the time, Pallas kernels for 22%

profile of v1, /device:TPU:0, one launch (start us, length us, event | category | flops | bytes accessed | tf_op | source)
XLA Modules:
  0.0 201.1 jit_solution(4203274335556126184)
XLA Ops:
  0.0 0.9 slice.11
  0.9 1.3 collective-permute-start
  2.2 2.0 %collective-permute-done = bf16[16,3,2048]{2,0,1:T(8,128)(2,1)S(1)} collective-permute-done((bf16[16,3,2048]{2,0,1:T(8,128)(2,1)S(1)}, bf16[16,3,2048]{2,0,1:T(8,128)(2,1)S(1)}, u32[]{:S(2)}, u32[]{:S(2)}) %collective-permute-start) | collective-permute-done | bytes 196640 | tf_op jit(solution)/shard_map/ppermute | solution.py:254
  4.3 0.0 copy-start.2
  4.3 0.7 copy-done.2
  4.9 15.5 %patch_states.1.states_ref.own_ref = bf16[160,2048]{1,0:T(8,128)(2,1)} custom-call(s32[1]{0:T(128)} %bitcast.1.place_ref, s32[16,161]{1,0:T(8,128)} %bounds_ref.1, bf16[3,512,2048]{2,1,0:T(8,128)(2,1)} %bitcast.14, bf16[3,16,2048]{2,1,0:T(8,128)(2,1)} %bitcast.16), custom_call_target="tpu_custom_call" | custom-call | tf_op jit(solution)/shard_map/patch_states/pallas_call | solution.py:79
  20.4 3.0 %collective-permute-start.1 = (bf16[160,2048]{1,0:T(8,128)(2,1)}, bf16[160,2048]{1,0:T(8,128)(2,1)S(1)}, u32[]{:S(2)}, u32[]{:S(2)}) collective-permute-start(bf16[160,2048]{1,0:T(8,128)(2,1)} %patch_states.1.states_ref.own_ref), channel_id=1, source_target_pairs={{0,1},{1,0},{2,3},{3,2},{4,5},{5,4},{6,7},{7,6},{8,9},{9,8},{10,11... | collective-permute-start | bytes 1966088 | tf_op jit(solution)/shard_map/ppermute | solution.py:260
  23.4 43.5 %project.1.before_ref = f32[160,4096]{1,0:T(8,128)} custom-call(s32[1]{0:T(128)} %bitcast.4.start_ref, bf16[160,2048]{1,0:T(8,128)(2,1)} %patch_states.1.states_ref.own_ref, bf16[4096,2,2048]{2,1,0:T(2,128)(2,1)} %weight_ref.3), custom_call_target="tpu_custom_call" | custom-call | tf_op jit(solution)/shard_map/project/pallas_call | solution.py:143
  66.9 0.0 collective-permute-done.1.states_ref
  66.9 0.0 copy-start.1
  66.9 0.8 copy-done.1
  67.7 44.5 %project_more.1 = bf16[16,160,384]{2,1,0:T(8,128)(2,1)} custom-call(s32[1]{0:T(128)} %bitcast.start_ref, bf16[160,2048]{1,0:T(8,128)(2,1)} %copy-done.1, bf16[4096,2,2048]{2,1,0:T(2,128)(2,1)} %weight_ref.3, f32[160,4096]{1,0:T(8,128)} %project.1.before_ref, bf16[160,2048]{1,0:T(8,128)(2,1)} %patch_states.1.states_ref.own_ref), custom_call_target="tpu_custom_call" | custom-call | tf_op jit(solution)/shard_map/project_more/pallas_call | solution.py:165
  112.2 0.0 copy-start.3
  112.2 8.7 %all-to-all-start = ((bf16[16,160,384]{2,1,0:T(8,128)(2,1)}), bf16[16,160,384]{2,1,0:T(8,128)(2,1)S(1)}, u32[]{:S(2)}, u32[]{:S(2)}) async-start(bf16[16,160,384]{2,1,0:T(8,128)(2,1)} %project_more.1), calls=%async_computation | async-start | bytes 3932160 | tf_op jit(solution)/shard_map/all_to_all | solution.py:272
  121.0 0.0 copy-done.3
  121.0 0.1 broadcast_select_fusion
  121.1 0.7 reshape.14.bias_ref
  121.7 38.0 %all-to-all-done = bf16[16,160,384]{2,1,0:T(8,128)(2,1)S(1)} async-done(((bf16[16,160,384]{2,1,0:T(8,128)(2,1)}), bf16[16,160,384]{2,1,0:T(8,128)(2,1)S(1)}, u32[]{:S(2)}, u32[]{:S(2)}) %all-to-all-start) | async-done | bytes 1966112 | tf_op jit(solution)/shard_map/all_to_all | solution.py:272
  159.8 0.0 copy-start
  159.8 1.3 copy-done
  161.1 11.6 %attend.1 = bf16[2560,128]{1,0:T(8,128)(2,1)} custom-call(f32[1,2560]{1,0:T(1,128)} %reshape.14.bias_ref, bf16[2560,384]{1,0:T(8,128)(2,1)} %bitcast.13), custom_call_target="tpu_custom_call" | custom-call | tf_op jit(solution)/shard_map/attend/pallas_call | solution.py:209
  172.7 10.7 %all-to-all-start.1 = ((bf16[16,160,128]{2,1,0:T(8,128)(2,1)}), bf16[16,160,128]{2,1,0:T(8,128)(2,1)S(1)}, u32[]{:S(2)}, u32[]{:S(2)}) async-start(bf16[16,160,128]{2,1,0:T(8,128)(2,1)} %bitcast.15), calls=%async_computation.1 | async-start | bytes 1310720 | tf_op jit(solution)/shard_map/all_to_all | solution.py:274
  183.5 16.6 %all-to-all-done.1 = bf16[16,160,128]{2,1,0:T(8,128)(2,1)S(1)} async-done(((bf16[16,160,128]{2,1,0:T(8,128)(2,1)}), bf16[16,160,128]{2,1,0:T(8,128)(2,1)S(1)}, u32[]{:S(2)}, u32[]{:S(2)}) %all-to-all-start.1) | async-done | bytes 655392 | tf_op jit(solution)/shard_map/all_to_all | solution.py:274
  200.0 1.0 bitcast_select_fusion
  (1 shorter events, 0.0 us)
Async XLA Ops:
  0.9 3.3 %collective-permute-start = (bf16[16,3,2048]{2,0,1:T(8,128)(2,1)S(1)}, bf16[16,3,2048]{2,0,1:T(8,128)(2,1)S(1)}, u32[]{:S(2)}, u32[]{:S(2)}) collective-permute-start(bf16[16,3,2048]{2,0,1:T(8,128)(2,1)S(1)} %slice.11), channel_id=1, source_target_pairs={{2,0},{4,2},{6,4},{8,6},{10,8},{12,10},{14,12},{16,14},{18,16},{20... | collective-permute-start | bytes 589832 | tf_op jit(solution)/shard_map/ppermute | solution.py:254
  4.3 0.7 copy-start.2
  20.4 46.5 %collective-permute-start.1 = (bf16[160,2048]{1,0:T(8,128)(2,1)}, bf16[160,2048]{1,0:T(8,128)(2,1)S(1)}, u32[]{:S(2)}, u32[]{:S(2)}) collective-permute-start(bf16[160,2048]{1,0:T(8,128)(2,1)} %patch_states.1.states_ref.own_ref), channel_id=1, source_target_pairs={{0,1},{1,0},{2,3},{3,2},{4,5},{5,4},{6,7},{7,6},{8,9},{9,8},{10,11... | collective-permute-start | bytes 1966088 | tf_op jit(solution)/shard_map/ppermute | solution.py:260
  66.9 0.8 copy-start.1
  112.2 8.8 %copy-start.3 = (s32[16,161]{1,0:T(8,128)S(1)}, s32[16,161]{1,0:T(8,128)}, u32[]{:S(2)}) copy-start(s32[16,161]{1,0:T(8,128)} %bounds_ref.1) | copy-start | bytes 30916
  112.2 47.6 %all-to-all-start = ((bf16[16,160,384]{2,1,0:T(8,128)(2,1)}), bf16[16,160,384]{2,1,0:T(8,128)(2,1)S(1)}, u32[]{:S(2)}, u32[]{:S(2)}) async-start(bf16[16,160,384]{2,1,0:T(8,128)(2,1)} %project_more.1), calls=%async_computation | async-start | bytes 3932160 | tf_op jit(solution)/shard_map/all_to_all | solution.py:272
  159.8 1.3 copy-start
  172.7 27.3 %all-to-all-start.1 = ((bf16[16,160,128]{2,1,0:T(8,128)(2,1)}), bf16[16,160,128]{2,1,0:T(8,128)(2,1)S(1)}, u32[]{:S(2)}, u32[]{:S(2)}) async-start(bf16[16,160,128]{2,1,0:T(8,128)(2,1)} %bitcast.15), calls=%async_computation.1 | async-start | bytes 1310720 | tf_op jit(solution)/shard_map/all_to_all | solution.py:274

commit v2 on v1

--- a/solution.py
+++ b/solution.py
@@ -29,7 +29,7 @@
 
 def patch_body(heads, place_ref, bounds_ref, main_ref, edge_ref, out_ref, pens, bias, pick, live):
     byte_rows = main_ref.shape[1]
-    slots = out_ref.shape[0]
+    slots = out_ref.shape[1]
     rows = byte_rows + WIN
     entries = bounds_ref.shape[1]
 
@@ -67,13 +67,13 @@
         terms = jnp.exp(scores - jnp.max(scores, axis=1, keepdims=True))
         total = jnp.sum(terms, axis=1, keepdims=True)
         weights = (terms * (live[...] / total)).astype(jnp.bfloat16)
-        out_ref[:, cols] = dot_f32(weights, values).astype(jnp.bfloat16)
+        out_ref[head] = dot_f32(weights, values).astype(jnp.bfloat16)
 
 
 def patch_states(place, bounds, parts, edge, first_head, head_count, slots):
     byte_rows = parts.shape[1]
     rows = byte_rows + WIN
-    group = 2 if head_count % 2 == 0 else 1
+    group = next(g for g in (4, 2, 1) if head_count % g == 0)
     skip = first_head // group
     width = group * HEAD
     return pl.pallas_call(
@@ -85,8 +85,8 @@
             pl.BlockSpec((3, byte_rows, width), lambda i: (0, 0, i + skip)),
             pl.BlockSpec((3, WIN, width), lambda i: (0, 0, i + skip)),
         ],
-        out_specs=pl.BlockSpec((slots, width), lambda i: (0, i)),
-        out_shape=jax.ShapeDtypeStruct((slots, head_count * HEAD), jnp.bfloat16),
+        out_specs=pl.BlockSpec((group, slots, HEAD), lambda i: (i, 0, 0)),
+        out_shape=jax.ShapeDtypeStruct((head_count, slots, HEAD), jnp.bfloat16),
         scratch_shapes=[
             pltpu.VMEM((4, rows, HEAD), jnp.float32),
             pltpu.VMEM((slots, rows), jnp.float32),
@@ -98,101 +98,102 @@
     )(place, bounds, parts, edge)
 
 
-def project_body(start_ref, states_ref, weight_ref, sums_ref):
-    width = weight_ref.shape[2]
-
-    @pl.when(pl.program_id(0) == 0)
-    def _():
-        sums_ref[...] = jnp.zeros_like(sums_ref)
-
-    states = states_ref[...]
-    sums_ref[:, :width] += dot_f32(states, weight_ref[:, 0, :])
-    sums_ref[:, width:] += dot_f32(states, weight_ref[:, 1, :])
-
-
-def project_more_body(start_ref, states_ref, weight_ref, before_ref, own_ref, out_ref, sums):
-    width = weight_ref.shape[2]
-
-    @pl.when(pl.program_id(0) == 0)
-    def _():
-        sums[...] = before_ref[...]
-
-    states = states_ref[...]
-    sums[:, :width] += dot_f32(states, weight_ref[:, 0, :])
-    sums[:, width:] += dot_f32(states, weight_ref[:, 1, :])
-
-    @pl.when(pl.program_id(0) == pl.num_programs(0) - 1)
-    def _():
-        for head in range(width // HEAD):
-            cols = slice(head * HEAD, (head + 1) * HEAD)
-            out_ref[head, :, :HEAD] = own_ref[:, cols]
-            out_ref[head, :, HEAD : 2 * HEAD] = sums[:, cols].astype(jnp.bfloat16)
-            out_ref[head, :, 2 * HEAD :] = sums[:, width + head * HEAD : width + (head + 1) * HEAD].astype(
-                jnp.bfloat16
-            )
-
-
-def feature_chunk(count):
-    return next(c for c in (512, 256, 128) if count % c == 0)
+def column_block(width):
+    return next(c for c in (512, 256, 128) if width % c == 0)
+
+
+def spread_products(start_ref, states_ref, weight_ref, spread, blocks, arrived, emit):
+    heads, slots = states_ref.shape[:2]
+    count = heads * HEAD
+    steps, _, _, block = blocks.shape
+    rows = pl.ds(pl.multiple_of(start_ref[0] * count, count), count)
+    copies = [
+        pltpu.make_async_copy(
+            weight_ref.at[rows, :, pl.ds(step * block, block)], blocks.at[step], arrived.at[step]
+        )
+        for step in range(steps)
+    ]
+    for copy in copies:
+        copy.start()
+    feature = lax.broadcasted_iota(jnp.int32, (HEAD, 2 * HEAD), 0)
+    row = lax.broadcasted_iota(jnp.int32, (HEAD, 2 * HEAD), 1)
+    for part in range(2):
+        place = jnp.where(row == 2 * feature + part, 1.0, 0.0).astype(jnp.bfloat16)
+        for head in range(heads):
+            spread[part * slots : (part + 1) * slots, 2 * head * HEAD : 2 * (head + 1) * HEAD] = dot_f32(
+                states_ref[head], place
+            ).astype(jnp.bfloat16)
+    for step in range(steps):
+        copies[step].wait()
+        emit(step * block, block, dot_f32(spread[...], blocks.at[step].reshape(2 * count, block)[...]))
+
+
+def project_body(start_ref, states_ref, weight_ref, sums_ref, spread, blocks, arrived):
+    def emit(at, block, product):
+        sums_ref[:, at : at + block] = product
+
+    spread_products(start_ref, states_ref, weight_ref, spread, blocks, arrived, emit)
+
+
+def project_more_body(start_ref, states_ref, weight_ref, before_ref, out_ref, spread, blocks, arrived):
+    slots = out_ref.shape[1]
+
+    def emit(at, block, product):
+        total = (before_ref[:, at : at + block] + product).astype(jnp.bfloat16)
+        for col in range(0, block, HEAD):
+            head = (at + col) // HEAD
+            out_ref[head, :, :HEAD] = total[:slots, col : col + HEAD]
+            out_ref[head, :, HEAD:] = total[slots:, col : col + HEAD]
+
+    spread_products(start_ref, states_ref, weight_ref, spread, blocks, arrived, emit)
+
+
+def project_call(body, name, out_shape, start, states, weight, *before):
+    heads, slots, _ = states.shape
+    width = weight.shape[2]
+    block = column_block(width)
+    count = heads * HEAD
+    in_vmem = pl.BlockSpec(memory_space=pltpu.VMEM)
+    return pl.pallas_call(
+        body,
+        in_specs=[pl.BlockSpec(memory_space=pltpu.SMEM), in_vmem, pl.BlockSpec(memory_space=pl.ANY)]
+        + [in_vmem] * len(before),
+        out_specs=in_vmem,
+        out_shape=out_shape,
+        scratch_shapes=[
+            pltpu.VMEM((2 * slots, 2 * count), jnp.bfloat16),
+            pltpu.VMEM((width // block, count, 2, block), jnp.bfloat16),
+            pltpu.SemaphoreType.DMA((width // block,)),
+        ],
+        compiler_params=params(),
+        cost_estimate=pl.CostEstimate(
+            flops=8 * slots * count * width, bytes_accessed=4 * count * width, transcendentals=0
+        ),
+        name=name,
+    )(start, states, weight, *before)
 
 
 def project(start, states, weight):
-    slots, count = states.shape
-    width = weight.shape[2]
-    chunk = feature_chunk(count)
-    return pl.pallas_call(
-        project_body,
-        grid_spec=pltpu.PrefetchScalarGridSpec(
-            num_scalar_prefetch=1,
-            grid=(count // chunk,),
-            in_specs=[
-                pl.BlockSpec((slots, chunk), lambda i, start: (0, i)),
-                pl.BlockSpec((chunk, 2, width), lambda i, start: (start[0] * (count // chunk) + i, 0, 0)),
-            ],
-            out_specs=pl.BlockSpec((slots, 2 * width), lambda i, start: (0, 0)),
-        ),
-        out_shape=jax.ShapeDtypeStruct((slots, 2 * width), jnp.float32),
-        compiler_params=params(),
-        name="project",
-    )(start, states, weight)
-
-
-def project_more(start, states, weight, before, own):
-    slots, count = states.shape
-    width = weight.shape[2]
-    chunk = feature_chunk(count)
-    heads = width // HEAD
-    return pl.pallas_call(
-        project_more_body,
-        grid_spec=pltpu.PrefetchScalarGridSpec(
-            num_scalar_prefetch=1,
-            grid=(count // chunk,),
-            in_specs=[
-                pl.BlockSpec((slots, chunk), lambda i, start: (0, i)),
-                pl.BlockSpec((chunk, 2, width), lambda i, start: (start[0] * (count // chunk) + i, 0, 0)),
-                pl.BlockSpec((slots, 2 * width), lambda i, start: (0, 0)),
-                pl.BlockSpec((slots, width), lambda i, start: (0, 0)),
-            ],
-            out_specs=pl.BlockSpec((heads, slots, 3 * HEAD), lambda i, start: (0, 0, 0)),
-            scratch_shapes=[pltpu.VMEM((slots, 2 * width), jnp.float32)],
-        ),
-        out_shape=jax.ShapeDtypeStruct((heads, slots, 3 * HEAD), jnp.bfloat16),
-        compiler_params=params(),
-        name="project_more",
-    )(start, states, weight, before, own)
-
-
-def attend_body(block, bias_ref, qkv_ref, out_ref, values):
-    slots = qkv_ref.shape[0]
-    values[:, :HEAD] = qkv_ref[:, 2 * HEAD :]
+    shape = jax.ShapeDtypeStruct((2 * states.shape[1], weight.shape[2]), jnp.float32)
+    return project_call(project_body, "project", shape, start, states, weight)
+
+
+def project_more(start, states, weight, before):
+    shape = jax.ShapeDtypeStruct((weight.shape[2] // HEAD, states.shape[1], 2 * HEAD), jnp.bfloat16)
+    return project_call(project_more_body, "project_more", shape, start, states, weight, before)
+
+
+def attend_body(block, bias_ref, query_ref, kv_ref, out_ref, values):
+    slots = kv_ref.shape[0]
+    values[:, :HEAD] = kv_ref[:, HEAD:]
     values[:, HEAD:] = jnp.ones((slots, HEAD), jnp.bfloat16)
     row = lax.broadcasted_iota(jnp.int32, (block, block), 0)
     col = lax.broadcasted_iota(jnp.int32, (block, block), 1)
     later = jnp.where(col <= row, 0.0, MASKED)
     for at in range(0, slots, block):
         seen = at + block
-        query = qkv_ref[at:seen, :HEAD]
-        scores = dot_f32(query, qkv_ref[:seen, HEAD : 2 * HEAD], 1) * SCALE + bias_ref[:, :seen]
+        query = query_ref[at:seen]
+        scores = dot_f32(query, kv_ref[:seen, :HEAD], 1) * SCALE + bias_ref[:, :seen]
         last = scores[:, at:] + later
         scores = last if at == 0 else jnp.concatenate([scores[:, :at], last], axis=1)
         terms = jnp.exp(scores - jnp.max(scores, axis=1, keepdims=True))
@@ -203,8 +204,8 @@
         out_ref[at:seen] = mixed.astype(jnp.bfloat16)
 
 
-def attend(bias, qkv):
-    slots = qkv.shape[0]
+def attend(bias, query, kv):
+    slots = kv.shape[0]
     block = next(b for b in (256, 128) if slots % b == 0)
     return pl.pallas_call(
         functools.partial(attend_body, block),
@@ -212,7 +213,7 @@
         scratch_shapes=[pltpu.VMEM((slots, 2 * HEAD), jnp.bfloat16)],
         compiler_params=params(),
         name="attend",
-    )(bias, qkv)
+    )(bias, query, kv)
 
 
 def attend_gathered(place, valid, queries, keys, values):
@@ -256,27 +257,32 @@
     edge = edge.transpose(1, 0, 2)
     states = patch_states(place[None], patch_bounds, parts, edge, 0, heads, slots)
 
+    paired = ctx_count == heads
     if mp_count == 2:
         others = lax.ppermute(states, "mp", [(0, 1), (1, 0)])
         before = project(half[None], states, kv_weight)
         other_half = 1 - half
     else:
-        others = lax.all_gather(states, "mp", axis=1, tiled=True)
-        before = jnp.zeros((slots, 2 * width), jnp.float32)
+        others = lax.all_gather(states, "mp", axis=0, tiled=True)
+        before = jnp.zeros((2 * slots, width), jnp.float32)
         other_half = jnp.zeros_like(half)
-    qkv = project_more(other_half[None], others, kv_weight, before, states)
+    if paired:
+        query = lax.all_to_all(states, "ctx", 0, 0, tiled=True).reshape(ctx_count * slots, HEAD)
+    kv = project_more(other_half[None], others, kv_weight, before)
 
     valid = patch_bounds[:, 1:] > patch_bounds[:, :-1]
-    if ctx_count == heads:
+    if paired:
         bias = jnp.where(valid, 0.0, MASKED).astype(jnp.float32).reshape(1, ctx_count * slots)
-        mine = lax.all_to_all(qkv, "ctx", 0, 0, tiled=True).reshape(ctx_count * slots, 3 * HEAD)
-        mixed = attend(bias, mine).reshape(ctx_count, slots, HEAD)
+        kv = lax.all_to_all(kv, "ctx", 0, 0, tiled=True).reshape(ctx_count * slots, 2 * HEAD)
+        mixed = attend(bias, query, kv).reshape(ctx_count, slots, HEAD)
         mixed = lax.all_to_all(mixed, "ctx", 0, 0, tiled=True)
         mixed = mixed.transpose(1, 0, 2).reshape(slots, width)
     else:
-        keys = qkv[:, :, HEAD : 2 * HEAD].transpose(1, 0, 2).reshape(slots, width)
-        values = qkv[:, :, 2 * HEAD :].transpose(1, 0, 2).reshape(slots, width)
-        mixed = attend_gathered(place, valid.reshape(-1), states, keys, values)
+        query, keys, values = (
+            part.transpose(1, 0, 2).reshape(slots, width)
+            for part in (states, kv[:, :, :HEAD], kv[:, :, HEAD:])
+        )
+        mixed = attend_gathered(place, valid.reshape(-1), query, keys, values)
     live = lax.dynamic_index_in_dim(valid, place, 0, keepdims=False)
     return jnp.where(live[:, None], mixed, jnp.zeros_like(mixed))
 

time: 201 us -> 132 us (0.66)
  Pallas kernels: 115 us -> 48.5 us
  waiting for transfers between devices: 56.6 us -> 50 us
  starting transfers between devices: 23.7 us -> 27 us
    pallas_call x2, Pallas kernels: 88 us -> 22.3 us  [project_call(): pl.pallas_call(body, in_specs=[pl.BlockSpec(memory_space=pltpu.SMEM), in_...]
    all_to_all x1 -> x2, waiting for transfers between devices: 38 us -> 26.6 us  [the longest x1 26.6 us: shards(): lax.all_to_all(kv, 'ctx', 0, 0, tiled=True)]
    all_to_all x1 -> x2, starting transfers between devices: 8.74 us -> 16.1 us  [the longest x1 10.3 us: shards(): lax.all_to_all(states, 'ctx', 0, 0, tiled=True)]
    ppermute x1, waiting for transfers between devices: 0.01 us -> 4.78 us  [shards(): others = lax.ppermute(states, 'mp', [(0, 1), (1, 0)])]
    all_to_all x1, starting transfers between devices: 10.7 us -> 8.01 us  [shards(): mixed = lax.all_to_all(mixed, 'ctx', 0, 0, tiled=True)]
  transfers between devices with their start and end apart: 4 -> 5, of which waited for: 3 -> 4; matrix products, arithmetic and copies ran while one was open for 0% -> 1% of each run, Pallas kernels for 22% -> 17%
where the time goes in v2:
time: 132 us; the launch traced here: 131 us
  waiting for transfers between devices  50 us (38%)
  Pallas kernels  48.5 us (37%)
  starting transfers between devices  27 us (20%)
  local copies, waits for them, and re-layouts  4.28 us (3%)
    all_to_all x1, waiting for transfers between devices, shards(): lax.all_to_all(kv, 'ctx', 0, 0, tiled=True)  26.6 us
    pallas_call x2, Pallas kernels, project_call(): pl.pallas_call(body, in_specs=[pl.BlockSpec(memory_space=pltpu.SMEM), in_...  22.3 us
    all_to_all x1, waiting for transfers between devices, shards(): mixed = lax.all_to_all(mixed, 'ctx', 0, 0, tiled=True)  16.6 us
    pallas_call x1, Pallas kernels, patch_states(): pl.pallas_call(functools.partial(patch_body, group), grid=(head_count //...  14.6 us
    pallas_call x1, Pallas kernels, attend(): pl.pallas_call(functools.partial(attend_body, block), out_shape=jax.Shape...  11.6 us
    all_to_all x1, starting transfers between devices, shards(): lax.all_to_all(states, 'ctx', 0, 0, tiled=True)  10.3 us
    all_to_all x1, starting transfers between devices, shards(): mixed = lax.all_to_all(mixed, 'ctx', 0, 0, tiled=True)  8.01 us
    all_to_all x1, starting transfers between devices, shards(): lax.all_to_all(kv, 'ctx', 0, 0, tiled=True)  5.74 us
  transfers between devices with their start and end apart: 5, of which 4 were waited for; matrix products, arithmetic and copies ran while one was open for 1% of the time, Pallas kernels for 17%

profile of v2, /device:TPU:0, one launch (start us, length us, event | category | flops | bytes accessed | tf_op | source)
XLA Modules:
  0.0 130.9 jit_solution(10957365533327461944)
XLA Ops:
  0.0 0.9 slice.11
  0.9 1.3 collective-permute-start
  2.2 2.0 %collective-permute-done = bf16[16,3,2048]{2,0,1:T(8,128)(2,1)S(1)} collective-permute-done((bf16[16,3,2048]{2,0,1:T(8,128)(2,1)S(1)}, bf16[16,3,2048]{2,0,1:T(8,128)(2,1)S(1)}, u32[]{:S(2)}, u32[]{:S(2)}) %collective-permute-start) | collective-permute-done | bytes 196640 | tf_op jit(solution)/shard_map/ppermute | solution.py:255
  4.3 0.0 copy-start.3
  4.3 0.7 copy-done.3
  5.0 14.6 %patch_states.1.states_ref = bf16[16,160,128]{2,1,0:T(8,128)(2,1)} custom-call(s32[1]{0:T(128)} %bitcast.place_ref, s32[16,161]{1,0:T(8,128)} %bounds_ref.1, bf16[3,512,2048]{2,1,0:T(8,128)(2,1)} %bitcast.14, bf16[3,16,2048]{2,1,0:T(8,128)(2,1)} %bitcast.18), custom_call_target="tpu_custom_call" | custom-call | tf_op jit(solution)/shard_map/patch_states/pallas_call | solution.py:79
  19.5 10.3 %all-to-all-start = ((bf16[16,160,128]{2,1,0:T(8,128)(2,1)}), bf16[16,160,128]{2,1,0:T(8,128)(2,1)S(1)}, u32[]{:S(2)}, u32[]{:S(2)}) async-start(bf16[16,160,128]{2,1,0:T(8,128)(2,1)} %patch_states.1.states_ref), calls=%async_computation | async-start | bytes 1310720 | tf_op jit(solution)/shard_map/all_to_all | solution.py:270
  29.9 1.6 %collective-permute-start.1 = (bf16[16,160,128]{2,1,0:T(8,128)(2,1)}, bf16[16,160,128]{2,1,0:T(8,128)(2,1)S(1)}, u32[]{:S(2)}, u32[]{:S(2)}) collective-permute-start(bf16[16,160,128]{2,1,0:T(8,128)(2,1)} %patch_states.1.states_ref), channel_id=1, source_target_pairs={{0,1},{1,0},{2,3},{3,2},{4,5},{5,4},{6,7},{7,6},{8,9},{9,8},{10,11... | collective-permute-start | bytes 1966088 | tf_op jit(solution)/shard_map/ppermute | solution.py:262
  31.5 11.0 %project.1.before_ref = f32[320,2048]{1,0:T(8,128)} custom-call(s32[1]{0:T(128)} %bitcast.5.start_ref, bf16[16,160,128]{2,1,0:T(8,128)(2,1)} %patch_states.1.states_ref, bf16[4096,2,2048]{2,1,0:T(2,128)(2,1)} %weight_ref.3), custom_call_target="tpu_custom_call" | custom-call | flops 5368709120 | bytes 16777216 | tf_op jit(solution)/shard_map/project/pallas_call | solution.py:157
  42.4 4.8 %collective-permute-done.1.states_ref = bf16[16,160,128]{2,1,0:T(8,128)(2,1)S(1)} collective-permute-done((bf16[16,160,128]{2,1,0:T(8,128)(2,1)}, bf16[16,160,128]{2,1,0:T(8,128)(2,1)S(1)}, u32[]{:S(2)}, u32[]{:S(2)}) %collective-permute-start.1) | collective-permute-done | bytes 655392 | tf_op jit(solution)/shard_map/ppermute | solution.py:262
  47.2 0.0 copy-start.2
  47.2 0.8 copy-done.2
  48.1 11.3 %project_more.1 = bf16[16,160,256]{2,1,0:T(8,128)(2,1)} custom-call(s32[1]{0:T(128)} %bitcast.4.start_ref, bf16[16,160,128]{2,1,0:T(8,128)(2,1)} %copy-done.2, bf16[4096,2,2048]{2,1,0:T(2,128)(2,1)} %weight_ref.3, f32[320,2048]{1,0:T(8,128)} %project.1.before_ref), custom_call_target="tpu_custom_call" | custom-call | flops 5368709120 | bytes 16777216 | tf_op jit(solution)/shard_map/project_more/pallas_call | solution.py:157
  59.4 0.0 copy-start.4
  59.4 0.0 all-to-all-done
  59.4 0.0 copy-start.1
  59.4 5.7 %all-to-all-start.1 = ((bf16[16,160,256]{2,1,0:T(8,128)(2,1)}), bf16[16,160,256]{2,1,0:T(8,128)(2,1)S(1)}, u32[]{:S(2)}, u32[]{:S(2)}) async-start(bf16[16,160,256]{2,1,0:T(8,128)(2,1)} %project_more.1), calls=%async_computation.1 | async-start | bytes 2621440 | tf_op jit(solution)/shard_map/all_to_all | solution.py:276
  65.2 0.0 copy-done.4
  65.2 0.1 broadcast_select_fusion
  65.3 0.7 reshape.17.bias_ref
  65.9 26.6 %all-to-all-done.1 = bf16[16,160,256]{2,1,0:T(8,128)(2,1)S(1)} async-done(((bf16[16,160,256]{2,1,0:T(8,128)(2,1)}), bf16[16,160,256]{2,1,0:T(8,128)(2,1)S(1)}, u32[]{:S(2)}, u32[]{:S(2)}) %all-to-all-start.1) | async-done | bytes 1310752 | tf_op jit(solution)/shard_map/all_to_all | solution.py:276
  92.6 0.0 copy-start
  92.6 0.0 copy-done.1
  92.6 1.1 copy-done
  93.7 11.6 %attend.1 = bf16[2560,128]{1,0:T(8,128)(2,1)} custom-call(f32[1,2560]{1,0:T(1,128)} %reshape.17.bias_ref, bf16[2560,128]{1,0:T(8,128)(2,1)} %bitcast.16, bf16[2560,256]{1,0:T(8,128)(2,1)} %bitcast.15), custom_call_target="tpu_custom_call" | custom-call | tf_op jit(solution)/shard_map/attend/pallas_call | solution.py:210
  105.3 8.0 %all-to-all-start.2 = ((bf16[16,160,128]{2,1,0:T(8,128)(2,1)}), bf16[16,160,128]{2,1,0:T(8,128)(2,1)S(1)}, u32[]{:S(2)}, u32[]{:S(2)}) async-start(bf16[16,160,128]{2,1,0:T(8,128)(2,1)} %bitcast.17), calls=%async_computation.2 | async-start | bytes 1310720 | tf_op jit(solution)/shard_map/all_to_all | solution.py:278
  113.3 16.6 %all-to-all-done.2 = bf16[16,160,128]{2,1,0:T(8,128)(2,1)S(1)} async-done(((bf16[16,160,128]{2,1,0:T(8,128)(2,1)}), bf16[16,160,128]{2,1,0:T(8,128)(2,1)S(1)}, u32[]{:S(2)}, u32[]{:S(2)}) %all-to-all-start.2) | async-done | bytes 655392 | tf_op jit(solution)/shard_map/all_to_all | solution.py:278
  129.9 1.0 bitcast_select_fusion
  (1 shorter events, 0.0 us)
Async XLA Ops:
  0.9 3.3 %collective-permute-start = (bf16[16,3,2048]{2,0,1:T(8,128)(2,1)S(1)}, bf16[16,3,2048]{2,0,1:T(8,128)(2,1)S(1)}, u32[]{:S(2)}, u32[]{:S(2)}) collective-permute-start(bf16[16,3,2048]{2,0,1:T(8,128)(2,1)S(1)} %slice.11), channel_id=1, source_target_pairs={{2,0},{4,2},{6,4},{8,6},{10,8},{12,10},{14,12},{16,14},{18,16},{20... | collective-permute-start | bytes 589832 | tf_op jit(solution)/shard_map/ppermute | solution.py:255
  4.3 0.7 copy-start.3
  19.5 39.9 %all-to-all-start = ((bf16[16,160,128]{2,1,0:T(8,128)(2,1)}), bf16[16,160,128]{2,1,0:T(8,128)(2,1)S(1)}, u32[]{:S(2)}, u32[]{:S(2)}) async-start(bf16[16,160,128]{2,1,0:T(8,128)(2,1)} %patch_states.1.states_ref), calls=%async_computation | async-start | bytes 1310720 | tf_op jit(solution)/shard_map/all_to_all | solution.py:270
  29.9 17.3 %collective-permute-start.1 = (bf16[16,160,128]{2,1,0:T(8,128)(2,1)}, bf16[16,160,128]{2,1,0:T(8,128)(2,1)S(1)}, u32[]{:S(2)}, u32[]{:S(2)}) collective-permute-start(bf16[16,160,128]{2,1,0:T(8,128)(2,1)} %patch_states.1.states_ref), channel_id=1, source_target_pairs={{0,1},{1,0},{2,3},{3,2},{4,5},{5,4},{6,7},{7,6},{8,9},{9,8},{10,11... | collective-permute-start | bytes 1966088 | tf_op jit(solution)/shard_map/ppermute | solution.py:262
  47.2 0.8 copy-start.2
  59.4 5.8 %copy-start.4 = (s32[16,161]{1,0:T(8,128)S(1)}, s32[16,161]{1,0:T(8,128)}, u32[]{:S(2)}) copy-start(s32[16,161]{1,0:T(8,128)} %bounds_ref.1) | copy-start | bytes 30916
  59.4 33.2 %copy-start.1 = (bf16[16,160,128]{2,1,0:T(8,128)(2,1)}, bf16[16,160,128]{2,1,0:T(8,128)(2,1)S(1)}, u32[]{:S(2)}) copy-start(bf16[16,160,128]{2,1,0:T(8,128)(2,1)S(1)} %all-to-all-done) | copy-start | bytes 1966084
  59.4 33.2 %all-to-all-start.1 = ((bf16[16,160,256]{2,1,0:T(8,128)(2,1)}), bf16[16,160,256]{2,1,0:T(8,128)(2,1)S(1)}, u32[]{:S(2)}, u32[]{:S(2)}) async-start(bf16[16,160,256]{2,1,0:T(8,128)(2,1)} %project_more.1), calls=%async_computation.1 | async-start | bytes 2621440 | tf_op jit(solution)/shard_map/all_to_all | solution.py:276
  92.6 1.1 copy-start
  105.3 24.6 %all-to-all-start.2 = ((bf16[16,160,128]{2,1,0:T(8,128)(2,1)}), bf16[16,160,128]{2,1,0:T(8,128)(2,1)S(1)}, u32[]{:S(2)}, u32[]{:S(2)}) async-start(bf16[16,160,128]{2,1,0:T(8,128)(2,1)} %bitcast.17), calls=%async_computation.2 | async-start | bytes 1310720 | tf_op jit(solution)/shard_map/all_to_all | solution.py:278

commit v3 on v2

v3 whole, which is shorter than its diff:
```python
import functools
import math

import jax
import jax.numpy as jnp
from jax import lax
from jax.experimental import pallas as pl
from jax.experimental.pallas import tpu as pltpu
from jax.sharding import PartitionSpec as P

D = 4096
HEADS = 32
WIN = 16
HEAD = D // HEADS
SCALE = 1.0 / math.sqrt(HEAD)
MASKED = -1e30


def params(mebibytes):
    return pltpu.CompilerParams(vmem_limit_bytes=mebibytes * 1024 * 1024)


def dot_f32(left, right, right_dim=0):
    return lax.dot_general(
        left, right, (((1,), (right_dim,)), ((), ())), preferred_element_type=jnp.float32
    )


def ahead(row, steps):
    return pltpu.roll(row, row.shape[1] - steps, 1)


def patch_body(heads, joins, place_ref, bounds_ref, main_ref, edge_ref, *refs):
    if joins:
        earlier_ref, out_ref, whole_ref, pens, cuts, inside, pick = refs
    else:
        out_ref, pens, cuts, inside, pick = refs
    byte_rows = main_ref.shape[1]
    slots = out_ref.shape[1]
    rows = byte_rows + WIN
    lanes = inside.shape[1]
    entries = bounds_ref.shape[1]

    @pl.when(pl.program_id(0) == 0)
    def _():
        place = place_ref[0]
        local = (bounds_ref[pl.ds(place, 1), :] - place * byte_rows).astype(jnp.float32)
        entry = lax.broadcasted_iota(jnp.int32, (slots, entries), 1)
        slot = lax.broadcasted_iota(jnp.int32, (slots, entries), 0)
        first = jnp.sum(jnp.where(entry == slot, local, 0.0), axis=1, keepdims=True)
        after = jnp.sum(jnp.where(entry == slot + 1, local, 0.0), axis=1, keepdims=True)
        byte = lax.broadcasted_iota(jnp.int32, (slots, lanes), 1).astype(jnp.float32)
        member = (byte >= first) & (byte < after)
        inside[...] = jnp.where(member, 1.0, 0.0)
        pick[...] = jnp.where(member & (byte == first), 1.0, 0.0)[:, :rows].astype(jnp.bfloat16)
        edges = jnp.where((byte == first) | (byte == after), 1.0, 0.0)
        cut = jnp.where(jnp.max(edges, axis=0, keepdims=True) > 0.0, -jnp.inf, 0.0)
        cut = ahead(jnp.broadcast_to(cut, (8, lanes)), 1)
        cuts[0] = cut
        at = lax.broadcasted_iota(jnp.int32, (rows, entries), 0).astype(jnp.float32)
        begins = jnp.max(jnp.where(at == local, 1.0, 0.0), axis=1, keepdims=True)
        pen = jnp.broadcast_to(jnp.where(begins > 0.0, -jnp.inf, 0.0), (rows, HEAD))
        pen = pltpu.roll(pen, rows - 1, 0)
        pens[0] = pen
        for level in range(1, 4):
            steps = 1 << (level - 1)
            cut = cut + ahead(cut, steps)
            cuts[level] = cut
            pen = pen + pltpu.roll(pen, rows - steps, 0)
            pens[level] = pen

    score_rows = []
    for head in range(heads):
        cols = slice(head * HEAD, (head + 1) * HEAD)
        top = jnp.concatenate([main_ref[0, :, cols], edge_ref[0, :, cols]], axis=0).astype(jnp.float32)
        for level in range(4):
            top = jnp.maximum(top, pltpu.roll(top, rows - (1 << level), 0) + pens[level])
        query = dot_f32(pick[...], top.astype(jnp.bfloat16)).astype(jnp.bfloat16)
        spare = jnp.zeros((lanes - rows, HEAD), jnp.bfloat16)
        keys = jnp.concatenate([main_ref[1, :, cols], edge_ref[1, :, cols], spare], axis=0)
        scores = dot_f32(query, keys, 1) * inside[...]
        score_rows.append(jnp.sum(scores, axis=0, keepdims=True))
    scores = jnp.concatenate(score_rows + [jnp.zeros((8 - heads, lanes), jnp.float32)] * (heads < 8), axis=0)
    fore = back = scores
    for level in range(4):
        steps = 1 << level
        cut = cuts[level]
        fore = jnp.maximum(fore, ahead(fore, steps) + cut)
        back = jnp.maximum(back, pltpu.roll(back + cut, steps, 1))
    terms = jnp.exp((scores - jnp.maximum(fore, back)) * SCALE)
    fore = back = terms
    for level in range(4):
        steps = 1 << level
        keep = jnp.where(cuts[level] < 0.0, 0.0, 1.0)
        fore = fore + ahead(fore, steps) * keep
        back = back + pltpu.roll(back * keep, steps, 1)
    weights = terms / (fore + back - terms)
    for head in range(heads):
        cols = slice(head * HEAD, (head + 1) * HEAD)
        spare = jnp.zeros((lanes - rows, HEAD), jnp.bfloat16)
        values = jnp.concatenate([main_ref[2, :, cols], edge_ref[2, :, cols], spare], axis=0)
        spread = (inside[...] * weights[head : head + 1]).astype(jnp.bfloat16)
        out_ref[head] = dot_f32(spread, values).astype(jnp.bfloat16)
    if joins:
        whole_ref[: heads] = earlier_ref[...]
        whole_ref[heads:] = out_ref[...]


def patch_states(place, bounds, parts, edge, slots, first_head, heads, earlier=None):
    byte_rows = parts.shape[1]
    rows = byte_rows + WIN
    lanes = -(-rows // 128) * 128
    width = heads * HEAD
    run = first_head // heads
    joins = earlier is not None
    states = jax.ShapeDtypeStruct((heads, slots, HEAD), jnp.bfloat16)
    states_spec = pl.BlockSpec((heads, slots, HEAD), lambda i: (0, 0, 0))
    whole = jax.ShapeDtypeStruct((2 * heads, slots, HEAD), jnp.bfloat16)
    whole_spec = pl.BlockSpec((2 * heads, slots, HEAD), lambda i: (0, 0, 0))
    return pl.pallas_call(
        functools.partial(patch_body, heads, joins),
        grid=(1,),
        in_specs=[
            pl.BlockSpec(memory_space=pltpu.SMEM),
            pl.BlockSpec(bounds.shape, lambda i: (0, 0)),
            pl.BlockSpec((3, byte_rows, width), lambda i: (0, 0, run)),
            pl.BlockSpec((3, WIN, width), lambda i: (0, 0, run)),
        ]
        + [states_spec] * joins,
        out_specs=[states_spec, whole_spec] if joins else states_spec,
        out_shape=[states, whole] if joins else states,
        scratch_shapes=[
            pltpu.VMEM((4, rows, HEAD), jnp.float32),
            pltpu.VMEM((4, 8, lanes), jnp.float32),
            pltpu.VMEM((slots, lanes), jnp.float32),
            pltpu.VMEM((slots, rows), jnp.bfloat16),
        ],
        compiler_params=params(20),
        name="patch_states",
    )(place, bounds, parts, edge, *([earlier] if joins else []))


def column_block(width):
    return next(c for c in (512, 256, 128) if width % c == 0)


def spread_states(states_refs, spread):
    slots = states_refs[0].shape[1]
    feature = lax.broadcasted_iota(jnp.int32, (HEAD, 2 * HEAD), 0)
    row = lax.broadcasted_iota(jnp.int32, (HEAD, 2 * HEAD), 1)
    for part in range(2):
        place = jnp.where(row == 2 * feature + part, 1.0, 0.0).astype(jnp.bfloat16)
        at = 0
        for states_ref in states_refs:
            for head in range(states_ref.shape[0]):
                spread[part * slots : (part + 1) * slots, at : at + 2 * HEAD] = dot_f32(
                    states_ref[head], place
                ).astype(jnp.bfloat16)
                at += 2 * HEAD


def project_body(half_ref, states_ref, weight_ref, sums_ref, held_ref, spread, blocks, arrived, held_arrived):
    count = states_ref.shape[0] * HEAD
    steps, _, _, block = blocks.shape

    def rows(half):
        return pl.ds(pl.multiple_of(half * count, count), count)

    half = half_ref[0]
    copies = [
        pltpu.make_async_copy(
            weight_ref.at[rows(half), :, pl.ds(step * block, block)], blocks.at[step], arrived.at[step]
        )
        for step in range(steps)
    ]
    hold = pltpu.make_async_copy(weight_ref.at[rows(1 - half)], held_ref, held_arrived)
    for copy in copies:
        copy.start()
    hold.start()
    spread_states([states_ref], spread)
    for step in range(steps):
        copies[step].wait()
        weights = blocks.at[step].reshape(2 * count, block)[...]
        sums_ref[:, step * block : (step + 1) * block] = dot_f32(spread[...], weights)
    hold.wait()


def project(half, states, weight):
    heads, slots, _ = states.shape
    width = weight.shape[2]
    block = column_block(width)
    count = heads * HEAD
    in_vmem = pl.BlockSpec(memory_space=pltpu.VMEM)
    return pl.pallas_call(
        project_body,
        in_specs=[pl.BlockSpec(memory_space=pltpu.SMEM), in_vmem, pl.BlockSpec(memory_space=pl.ANY)],
        out_specs=[in_vmem, pl.BlockSpec(memory_space=pl.ANY)],
        out_shape=[
            jax.ShapeDtypeStruct((2 * slots, width), jnp.float32),
            pltpu.VMEM((count, 2, width), weight.dtype),
        ],
        scratch_shapes=[
            pltpu.VMEM((2 * slots, 2 * count), jnp.bfloat16),
            pltpu.VMEM((width // block, count, 2, block), jnp.bfloat16),
            pltpu.SemaphoreType.DMA((width // block,)),
            pltpu.SemaphoreType.DMA,
        ],
        compiler_params=params(28),
        cost_estimate=pl.CostEstimate(
            flops=8 * slots * count * width, bytes_accessed=8 * count * width, transcendentals=0
        ),
        name="project",
    )(half, states, weight)


def project_more_body(parts, *refs):
    states_refs, (weight_ref, before_ref, out_ref, spread) = refs[:parts], refs[parts:]
    slots = out_ref.shape[1]
    count, _, width = weight_ref.shape
    block = column_block(width)
    spread_states(states_refs, spread)
    flat = weight_ref.reshape(2 * count, width)
    for at in range(0, width, block):
        product = dot_f32(spread[...], flat[:, at : at + block])
        total = (before_ref[:, at : at + block] + product).astype(jnp.bfloat16)
        for col in range(0, block, HEAD):
            head = (at + col) // HEAD
            out_ref[head, :, :HEAD] = total[:slots, col : col + HEAD]
            out_ref[head, :, HEAD:] = total[slots:, col : col + HEAD]


def project_more(states, weight, before):
    slots = states[0].shape[1]
    count, _, width = weight.shape
    in_vmem = pl.BlockSpec(memory_space=pltpu.VMEM)
    return pl.pallas_call(
        functools.partial(project_more_body, len(states)),
        in_specs=[in_vmem] * (len(states) + 2),
        out_specs=in_vmem,
        out_shape=jax.ShapeDtypeStruct((width // HEAD, slots, 2 * HEAD), jnp.bfloat16),
        scratch_shapes=[pltpu.VMEM((2 * slots, 2 * count), jnp.bfloat16)],
        compiler_params=params(24),
        cost_estimate=pl.CostEstimate(
            flops=8 * slots * count * width, bytes_accessed=4 * count * width, transcendentals=0
        ),
        name="project_more",
    )(*states, pltpu.with_memory_space_constraint(weight, pltpu.VMEM), before)


def attend_body(block, bias_ref, query_ref, kv_ref, out_ref, values):
    slots = kv_ref.shape[0]
    values[:, :HEAD] = kv_ref[:, HEAD:]
    values[:, HEAD:] = jnp.ones((slots, HEAD), jnp.bfloat16)
    row = lax.broadcasted_iota(jnp.int32, (block, block), 0)
    col = lax.broadcasted_iota(jnp.int32, (block, block), 1)
    later = jnp.where(col <= row, 0.0, MASKED)
    for at in range(0, slots, block):
        seen = at + block
        query = query_ref[at:seen]
        scores = dot_f32(query, kv_ref[:seen, :HEAD], 1) * SCALE + bias_ref[:, :seen]
        last = scores[:, at:] + later
        scores = last if at == 0 else jnp.concatenate([scores[:, :at], last], axis=1)
        terms = jnp.exp(scores - jnp.max(scores, axis=1, keepdims=True))
        high = terms.astype(jnp.bfloat16)
        low = (terms - high.astype(jnp.float32)).astype(jnp.bfloat16)
        summed = dot_f32(high, values[:seen]) + dot_f32(low, values[:seen])
        mixed = query.astype(jnp.float32) + summed[:, :HEAD] / summed[:, HEAD:]
        out_ref[at:seen] = mixed.astype(jnp.bfloat16)


def attend(bias, query, kv):
    slots = kv.shape[0]
    block = next(b for b in (256, 128) if slots % b == 0)
    return pl.pallas_call(
        functools.partial(attend_body, block),
        out_shape=jax.ShapeDtypeStruct((slots, HEAD), jnp.bfloat16),
        scratch_shapes=[pltpu.VMEM((slots, 2 * HEAD), jnp.bfloat16)],
        compiler_params=params(24),
        name="attend",
    )(bias, query, kv)


def attend_gathered(place, valid, queries, keys, values):
    slots, width = queries.shape
    heads = width // HEAD
    keys = lax.all_gather(keys, "ctx", axis=0, tiled=True)
    values = lax.all_gather(values, "ctx", axis=0, tiled=True)
    total = keys.shape[0]
    query_slot = place * slots + jnp.arange(slots, dtype=jnp.int32)
    visible = (jnp.arange(total, dtype=jnp.int32)[None, :] <= query_slot[:, None]) & valid[None, :]
    scores = jnp.einsum(
        "qhd,khd->hqk",
        queries.reshape(slots, heads, HEAD),
        keys.reshape(total, heads, HEAD),
        preferred_element_type=jnp.float32,
    )
    scores = jnp.where(visible[None], scores * SCALE, MASKED)
    terms = jnp.where(visible[None], jnp.exp(scores - jnp.max(scores, axis=2, keepdims=True)), 0.0)
    sums = jnp.sum(terms, axis=2)
    attended = jnp.einsum(
        "hqk,khd->hqd",
        terms,
        values.reshape(total, heads, HEAD).astype(jnp.float32),
        precision=lax.Precision.HIGHEST,
    )
    attended = attended / jnp.where(sums > 0, sums, 1.0)[:, :, None]
    attended = attended.transpose(1, 0, 2).reshape(slots, width)
    return (queries.astype(jnp.float32) + attended).astype(jnp.bfloat16)


def shards(byte_qkv, kv_weight, patch_bounds):
    width = byte_qkv.shape[2]
    heads = width // HEAD
    slots = patch_bounds.shape[1] - 1
    ctx_count, mp_count = lax.axis_size("ctx"), lax.axis_size("mp")
    place = lax.axis_index("ctx").astype(jnp.int32)
    half = lax.axis_index("mp").astype(jnp.int32)

    edge = lax.ppermute(byte_qkv[:WIN], "ctx", [(i + 1, i) for i in range(ctx_count - 1)])
    parts = byte_qkv.transpose(1, 0, 2)
    edge = edge.transpose(1, 0, 2)
    in_hbm = functools.partial(pltpu.with_memory_space_constraint, memory_space=pltpu.HBM)
    byte_phase = functools.partial(
        patch_states, place[None], in_hbm(patch_bounds), in_hbm(parts), edge, slots
    )
    run = max(heads // 2, 1)
    first = byte_phase(0, run)
    states = first
    if heads > run:
        second, states = byte_phase(run, run, first)

    paired = ctx_count == heads
    if mp_count == 2:
        others = [lax.ppermute(run_states, "mp", [(0, 1), (1, 0)]) for run_states in (first, second)]
        before, held = project(half[None], states, kv_weight)
    else:
        others = [lax.all_gather(states, "mp", axis=0, tiled=True)]
        before, held = jnp.zeros((2 * slots, width), jnp.float32), kv_weight
    if paired:
        sent, others[0] = lax.optimization_barrier((states, others[0]))
        query = lax.all_to_all(sent, "ctx", 0, 0, tiled=True).reshape(ctx_count * slots, HEAD)
    kv = project_more(others, held, before)

    valid = patch_bounds[:, 1:] > patch_bounds[:, :-1]
    if paired:
        bias = jnp.where(valid, 0.0, MASKED).astype(jnp.float32).reshape(1, ctx_count * slots)
        kv = lax.all_to_all(kv, "ctx", 0, 0, tiled=True).reshape(ctx_count * slots, 2 * HEAD)
        mixed = attend(bias, query, kv).reshape(ctx_count, slots, HEAD)
        mixed = lax.all_to_all(mixed, "ctx", 0, 0, tiled=True)
        mixed = mixed.transpose(1, 0, 2).reshape(slots, width)
    else:
        query, keys, values = (
            part.transpose(1, 0, 2).reshape(slots, width)
            for part in (states, kv[:, :, :HEAD], kv[:, :, HEAD:])
        )
        mixed = attend_gathered(place, valid.reshape(-1), query, keys, values)
    live = lax.dynamic_index_in_dim(valid, place, 0, keepdims=False)
    return jnp.where(live[:, None], mixed, jnp.zeros_like(mixed))


def solution(mesh):
    return jax.shard_map(
        shards,
        mesh=mesh,
        in_specs=(P("ctx", None, "mp"), P(None, None, "mp"), P()),
        out_specs=P("ctx", "mp"),
        check_vma=False,
    )
```

time: 132 us -> 120 us (0.909)
  Pallas kernels: 48.5 us -> 42 us
  waiting for transfers between devices: 50 us -> 45.8 us
  local copies, waits for them, and re-layouts: 4.28 us -> 1.06 us
  starting transfers between devices: 27 us -> 29.8 us
    pallas_call x3 -> x4, Pallas kernels: 36.9 us -> 31.9 us  [the longest x2 12.6 us: patch_states(): pl.pallas_call(functools.partial(patch_body, heads, joins), grid=(1,), in...]
    ppermute x1 -> x2, waiting for transfers between devices: 4.78 us -> 0.01 us  [shards(): lax.ppermute(run_states, 'mp', [(0, 1), (1, 0)])]
    ppermute x1 -> x2, starting transfers between devices: 1.58 us -> 4.65 us  [shards(): lax.ppermute(run_states, 'mp', [(0, 1), (1, 0)])]
    unnamed x10 -> x2, local copies, waits for them, and re-layouts: 2.62 us -> 0.01 us
    pallas_call x1, Pallas kernels: 11.6 us -> 10.1 us  [attend(): pl.pallas_call(functools.partial(attend_body, block), out_shape=jax.Shape...]
  transfers between devices with their start and end apart: 5 -> 6, of which waited for: 4 -> 3; matrix products, arithmetic and copies ran while one was open for 1% -> 0% of each run, Pallas kernels for 17% -> 22%
where the time goes in v3:
time: 120 us
  waiting for transfers between devices  45.8 us (38%)
  Pallas kernels  42 us (35%)
  starting transfers between devices  29.8 us (25%)
    all_to_all x1, waiting for transfers between devices, shards(): lax.all_to_all(kv, 'ctx', 0, 0, tiled=True)  27.2 us
    all_to_all x1, waiting for transfers between devices, shards(): mixed = lax.all_to_all(mixed, 'ctx', 0, 0, tiled=True)  16.6 us
    pallas_call x2, Pallas kernels, patch_states(): pl.pallas_call(functools.partial(patch_body, heads, joins), grid=(1,), in...  12.6 us
    pallas_call x1, Pallas kernels, project(): pl.pallas_call(project_body, in_specs=[pl.BlockSpec(memory_space=pltpu.SM...  11.8 us
    pallas_call x1, Pallas kernels, attend(): pl.pallas_call(functools.partial(attend_body, block), out_shape=jax.Shape...  10.1 us
    all_to_all x1, starting transfers between devices, shards(): lax.all_to_all(sent, 'ctx', 0, 0, tiled=True)  9.87 us
    all_to_all x1, starting transfers between devices, shards(): mixed = lax.all_to_all(mixed, 'ctx', 0, 0, tiled=True)  8.01 us
    pallas_call x1, Pallas kernels, project_more(): pl.pallas_call(functools.partial(project_more_body, len(states)), in_spec...  7.45 us
  transfers between devices with their start and end apart: 6, of which 3 were waited for; matrix products, arithmetic and copies ran while one was open for 0% of the time, Pallas kernels for 22%

profile of v3, /device:TPU:0, one launch (start us, length us, event | category | flops | bytes accessed | tf_op | source)
XLA Modules:
  0.0 119.8 jit_solution(4434380037994806980)
XLA Ops:
  0.0 0.9 slice.11
  0.9 1.3 %collective-permute-start = (bf16[16,3,2048]{2,0,1:T(8,128)(2,1)S(1)}, bf16[16,3,2048]{2,0,1:T(8,128)(2,1)S(1)}, u32[]{:S(2)}, u32[]{:S(2)}) collective-permute-start(bf16[16,3,2048]{2,0,1:T(8,128)(2,1)S(1)} %slice.11), channel_id=1, source_target_pairs={{2,0},{4,2},{6,4},{8,6},{10,8},{12,10},{14,12},{16,14},{18,16},{20... | collective-permute-start | bytes 589832 | tf_op jit(solution)/shard_map/ppermute | solution.py:319
  2.2 2.0 %collective-permute-done = bf16[16,3,2048]{2,0,1:T(8,128)(2,1)S(1)} collective-permute-done((bf16[16,3,2048]{2,0,1:T(8,128)(2,1)S(1)}, bf16[16,3,2048]{2,0,1:T(8,128)(2,1)S(1)}, u32[]{:S(2)}, u32[]{:S(2)}) %collective-permute-start) | collective-permute-done | bytes 196640 | tf_op jit(solution)/shard_map/ppermute | solution.py:319
  4.3 5.8 %patch_states.2.refs_0_ = bf16[8,160,128]{2,1,0:T(8,128)(2,1)S(1)} custom-call(s32[1]{0:T(128)} %bitcast.place_ref, s32[16,161]{1,0:T(8,128)} %bounds_ref.3, bf16[3,512,2048]{2,1,0:T(8,128)(2,1)} %bitcast.17, bf16[3,16,2048]{2,1,0:T(8,128)(2,1)S(1)} %bitcast.15), custom_call_target="tpu_custom_call" | custom-call | tf_op jit(solution)/shard_map/patch_states/pallas_call | solution.py:120
  10.1 3.0 %collective-permute-start.1 = (bf16[8,160,128]{2,1,0:T(8,128)(2,1)S(1)}, bf16[8,160,128]{2,1,0:T(8,128)(2,1)S(1)}, u32[]{:S(2)}, u32[]{:S(2)}) collective-permute-start(bf16[8,160,128]{2,1,0:T(8,128)(2,1)S(1)} %patch_states.2.refs_0_), channel_id=1, source_target_pairs={{0,1},{1,0},{2,3},{3,2},{4,5},{5,4},{6,7},{7,6},{8,9},{9,8},{10,11... | collective-permute-start | bytes 983048 | tf_op jit(solution)/shard_map/ppermute | solution.py:334
  13.1 6.7 %patch_states.3 = (bf16[8,160,128]{2,1,0:T(8,128)(2,1)S(1)}, bf16[16,160,128]{2,1,0:T(8,128)(2,1)}) custom-call(s32[1]{0:T(128)} %bitcast.place_ref, s32[16,161]{1,0:T(8,128)} %bounds_ref.3, bf16[3,512,2048]{2,1,0:T(8,128)(2,1)} %bitcast.18, bf16[3,16,2048]{2,1,0:T(8,128)(2,1)S(1)} %bitcast.16, bf16[8,160,128]{2,1,0:T(8,128)(2,1)S(1)} %patch_states.2.refs_0_), custom_call_target="tpu_custom_call" | custom-call | tf_op jit(solution)/shard_map/patch_states/pallas_call | solution.py:120
  19.9 0.0 collective-permute-done.1.refs_0_
  19.9 9.9 %all-to-all-start = ((bf16[16,160,128]{2,1,0:T(8,128)(2,1)}), bf16[16,160,128]{2,1,0:T(8,128)(2,1)S(1)}, u32[]{:S(2)}, u32[]{:S(2)}) async-start(bf16[16,160,128]{2,1,0:T(8,128)(2,1)} %get-tuple-element.12.states_ref), calls=%async_computation | async-start | bytes 1310720 | tf_op jit(solution)/shard_map/all_to_all | solution.py:341
  29.8 1.6 %collective-permute-start.2 = (bf16[8,160,128]{2,1,0:T(8,128)(2,1)S(1)}, bf16[8,160,128]{2,1,0:T(8,128)(2,1)S(1)}, u32[]{:S(2)}, u32[]{:S(2)}) collective-permute-start(bf16[8,160,128]{2,1,0:T(8,128)(2,1)S(1)} %get-tuple-element.14), channel_id=1, source_target_pairs={{0,1},{1,0},{2,3},{3,2},{4,5},{5,4},{6,7},{7,6},{8,9},{9,8},{10,11... | collective-permute-start | bytes 983048 | tf_op jit(solution)/shard_map/ppermute | solution.py:334
  31.4 11.8 %project.1 = (f32[320,2048]{1,0:T(8,128)S(1)}, bf16[2048,2,2048]{2,1,0:T(2,128)(2,1)S(1)}) custom-call(s32[1]{0:T(128)} %bitcast.4.half_ref, bf16[16,160,128]{2,1,0:T(8,128)(2,1)} %get-tuple-element.12.states_ref, bf16[4096,2,2048]{2,1,0:T(2,128)(2,1)} %weight_ref.1), custom_call_target="tpu_custom_call" | custom-call | flops 5368709120 | bytes 33554432 | tf_op jit(solution)/shard_map/project/pallas_call | solution.py:194
  43.2 0.0 collective-permute-done.2.refs_1_
  43.2 0.0 copy-start
  43.3 7.5 %project_more.1 = bf16[16,160,256]{2,1,0:T(8,128)(2,1)} custom-call(bf16[8,160,128]{2,1,0:T(8,128)(2,1)S(1)} %collective-permute-done.1.refs_0_, bf16[8,160,128]{2,1,0:T(8,128)(2,1)S(1)} %collective-permute-done.2.refs_1_, bf16[2048,2,2048]{2,1,0:T(2,128)(2,1)S(1)} %get-tuple-element.15.refs_2_, f32[320,2048]{1,0:T(8,128)S(1)} %get-tuple-element.16.refs_3_), custom_call_target="tpu_custom_call" | custom-call | flops 5368709120 | bytes 16777216 | tf_op jit(solution)/shard_map/project_more/pallas_call | solution.py:236
  50.7 0.0 all-to-all-done
  50.7 6.0 %all-to-all-start.1 = ((bf16[16,160,256]{2,1,0:T(8,128)(2,1)}), bf16[16,160,256]{2,1,0:T(8,128)(2,1)S(1)}, u32[]{:S(2)}, u32[]{:S(2)}) async-start(bf16[16,160,256]{2,1,0:T(8,128)(2,1)} %project_more.1), calls=%async_computation.1 | async-start | bytes 2621440 | tf_op jit(solution)/shard_map/all_to_all | solution.py:347
  56.7 0.0 copy-done
  56.7 0.1 broadcast_select_fusion
  56.8 0.1 reshape.17.bias_ref
  56.9 27.2 %all-to-all-done.1 = bf16[16,160,256]{2,1,0:T(8,128)(2,1)S(1)} async-done(((bf16[16,160,256]{2,1,0:T(8,128)(2,1)}), bf16[16,160,256]{2,1,0:T(8,128)(2,1)S(1)}, u32[]{:S(2)}, u32[]{:S(2)}) %all-to-all-start.1) | async-done | bytes 1310752 | tf_op jit(solution)/shard_map/all_to_all | solution.py:347
  84.1 10.1 %attend.1 = bf16[2560,128]{1,0:T(8,128)(2,1)} custom-call(f32[1,2560]{1,0:T(1,128)S(1)} %reshape.17.bias_ref, bf16[2560,128]{1,0:T(8,128)(2,1)S(1)} %bitcast.14, bf16[2560,256]{1,0:T(8,128)(2,1)S(1)} %bitcast.13), custom_call_target="tpu_custom_call" | custom-call | tf_op jit(solution)/shard_map/attend/pallas_call | solution.py:274
  94.2 8.0 %all-to-all-start.2 = ((bf16[16,160,128]{2,1,0:T(8,128)(2,1)}), bf16[16,160,128]{2,1,0:T(8,128)(2,1)S(1)}, u32[]{:S(2)}, u32[]{:S(2)}) async-start(bf16[16,160,128]{2,1,0:T(8,128)(2,1)} %bitcast.6), calls=%async_computation.2 | async-start | bytes 1310720 | tf_op jit(solution)/shard_map/all_to_all | solution.py:349
  102.3 16.6 %all-to-all-done.2 = bf16[16,160,128]{2,1,0:T(8,128)(2,1)S(1)} async-done(((bf16[16,160,128]{2,1,0:T(8,128)(2,1)}), bf16[16,160,128]{2,1,0:T(8,128)(2,1)S(1)}, u32[]{:S(2)}, u32[]{:S(2)}) %all-to-all-start.2) | async-done | bytes 655392 | tf_op jit(solution)/shard_map/all_to_all | solution.py:349
  118.8 1.0 bitcast_select_fusion
  (1 shorter events, 0.0 us)
Async XLA Ops:
  0.9 3.3 %collective-permute-start = (bf16[16,3,2048]{2,0,1:T(8,128)(2,1)S(1)}, bf16[16,3,2048]{2,0,1:T(8,128)(2,1)S(1)}, u32[]{:S(2)}, u32[]{:S(2)}) collective-permute-start(bf16[16,3,2048]{2,0,1:T(8,128)(2,1)S(1)} %slice.11), channel_id=1, source_target_pairs={{2,0},{4,2},{6,4},{8,6},{10,8},{12,10},{14,12},{16,14},{18,16},{20... | collective-permute-start | bytes 589832 | tf_op jit(solution)/shard_map/ppermute | solution.py:319
  10.1 9.8 %collective-permute-start.1 = (bf16[8,160,128]{2,1,0:T(8,128)(2,1)S(1)}, bf16[8,160,128]{2,1,0:T(8,128)(2,1)S(1)}, u32[]{:S(2)}, u32[]{:S(2)}) collective-permute-start(bf16[8,160,128]{2,1,0:T(8,128)(2,1)S(1)} %patch_states.2.refs_0_), channel_id=1, source_target_pairs={{0,1},{1,0},{2,3},{3,2},{4,5},{5,4},{6,7},{7,6},{8,9},{9,8},{10,11... | collective-permute-start | bytes 983048 | tf_op jit(solution)/shard_map/ppermute | solution.py:334
  19.9 30.8 %all-to-all-start = ((bf16[16,160,128]{2,1,0:T(8,128)(2,1)}), bf16[16,160,128]{2,1,0:T(8,128)(2,1)S(1)}, u32[]{:S(2)}, u32[]{:S(2)}) async-start(bf16[16,160,128]{2,1,0:T(8,128)(2,1)} %get-tuple-element.12.states_ref), calls=%async_computation | async-start | bytes 1310720 | tf_op jit(solution)/shard_map/all_to_all | solution.py:341
  29.8 13.5 %collective-permute-start.2 = (bf16[8,160,128]{2,1,0:T(8,128)(2,1)S(1)}, bf16[8,160,128]{2,1,0:T(8,128)(2,1)S(1)}, u32[]{:S(2)}, u32[]{:S(2)}) collective-permute-start(bf16[8,160,128]{2,1,0:T(8,128)(2,1)S(1)} %get-tuple-element.14), channel_id=1, source_target_pairs={{0,1},{1,0},{2,3},{3,2},{4,5},{5,4},{6,7},{7,6},{8,9},{9,8},{10,11... | collective-permute-start | bytes 983048 | tf_op jit(solution)/shard_map/ppermute | solution.py:334
  43.2 13.5 %copy-start = (s32[16,161]{1,0:T(8,128)S(1)}, s32[16,161]{1,0:T(8,128)}, u32[]{:S(2)}) copy-start(s32[16,161]{1,0:T(8,128)} %bounds_ref.3) | copy-start | bytes 30916
  50.7 33.4 %all-to-all-start.1 = ((bf16[16,160,256]{2,1,0:T(8,128)(2,1)}), bf16[16,160,256]{2,1,0:T(8,128)(2,1)S(1)}, u32[]{:S(2)}, u32[]{:S(2)}) async-start(bf16[16,160,256]{2,1,0:T(8,128)(2,1)} %project_more.1), calls=%async_computation.1 | async-start | bytes 2621440 | tf_op jit(solution)/shard_map/all_to_all | solution.py:347
  94.2 24.6 %all-to-all-start.2 = ((bf16[16,160,128]{2,1,0:T(8,128)(2,1)}), bf16[16,160,128]{2,1,0:T(8,128)(2,1)S(1)}, u32[]{:S(2)}, u32[]{:S(2)}) async-start(bf16[16,160,128]{2,1,0:T(8,128)(2,1)} %bitcast.6), calls=%async_computation.2 | async-start | bytes 1310720 | tf_op jit(solution)/shard_map/all_to_all | solution.py:349

commit v4 on v3

--- a/solution.py
+++ b/solution.py
@@ -13,6 +13,7 @@
 WIN = 16
 HEAD = D // HEADS
 SCALE = 1.0 / math.sqrt(HEAD)
+SCALE_2 = SCALE * math.log2(math.e)
 MASKED = -1e30
 
 
@@ -32,9 +33,10 @@
 
 def patch_body(heads, joins, place_ref, bounds_ref, main_ref, edge_ref, *refs):
     if joins:
-        earlier_ref, out_ref, whole_ref, pens, cuts, inside, pick = refs
+        earlier_ref, out_ref, whole_ref, *refs = refs
     else:
-        out_ref, pens, cuts, inside, pick = refs
+        out_ref, *refs = refs
+    pens, cuts, inside, pick, tops = refs
     byte_rows = main_ref.shape[1]
     slots = out_ref.shape[1]
     rows = byte_rows + WIN
@@ -69,16 +71,19 @@
             pen = pen + pltpu.roll(pen, rows - steps, 0)
             pens[level] = pen
 
-    score_rows = []
     for head in range(heads):
         cols = slice(head * HEAD, (head + 1) * HEAD)
         top = jnp.concatenate([main_ref[0, :, cols], edge_ref[0, :, cols]], axis=0).astype(jnp.float32)
         for level in range(4):
             top = jnp.maximum(top, pltpu.roll(top, rows - (1 << level), 0) + pens[level])
-        query = dot_f32(pick[...], top.astype(jnp.bfloat16)).astype(jnp.bfloat16)
-        spare = jnp.zeros((lanes - rows, HEAD), jnp.bfloat16)
+        tops[:, cols] = top.astype(jnp.bfloat16)
+    queries = dot_f32(pick[...], tops[...]).astype(jnp.bfloat16)
+    spare = jnp.zeros((lanes - rows, HEAD), jnp.bfloat16)
+    score_rows = []
+    for head in range(heads):
+        cols = slice(head * HEAD, (head + 1) * HEAD)
         keys = jnp.concatenate([main_ref[1, :, cols], edge_ref[1, :, cols], spare], axis=0)
-        scores = dot_f32(query, keys, 1) * inside[...]
+        scores = dot_f32(queries[:, cols], keys, 1) * inside[...]
         score_rows.append(jnp.sum(scores, axis=0, keepdims=True))
     scores = jnp.concatenate(score_rows + [jnp.zeros((8 - heads, lanes), jnp.float32)] * (heads < 8), axis=0)
     fore = back = scores
@@ -97,7 +102,6 @@
     weights = terms / (fore + back - terms)
     for head in range(heads):
         cols = slice(head * HEAD, (head + 1) * HEAD)
-        spare = jnp.zeros((lanes - rows, HEAD), jnp.bfloat16)
         values = jnp.concatenate([main_ref[2, :, cols], edge_ref[2, :, cols], spare], axis=0)
         spread = (inside[...] * weights[head : head + 1]).astype(jnp.bfloat16)
         out_ref[head] = dot_f32(spread, values).astype(jnp.bfloat16)
@@ -134,6 +138,7 @@
             pltpu.VMEM((4, 8, lanes), jnp.float32),
             pltpu.VMEM((slots, lanes), jnp.float32),
             pltpu.VMEM((slots, rows), jnp.bfloat16),
+            pltpu.VMEM((rows, width), jnp.bfloat16),
         ],
         compiler_params=params(20),
         name="patch_states",
@@ -141,7 +146,7 @@
 
 
 def column_block(width):
-    return next(c for c in (512, 256, 128) if width % c == 0)
+    return next(c for c in (512, 256, 128) if width % c == 0 and width > c)
 
 
 def spread_states(states_refs, spread):
@@ -162,18 +167,18 @@
 def project_body(half_ref, states_ref, weight_ref, sums_ref, held_ref, spread, blocks, arrived, held_arrived):
     count = states_ref.shape[0] * HEAD
     steps, _, _, block = blocks.shape
-
-    def rows(half):
-        return pl.ds(pl.multiple_of(half * count, count), count)
-
     half = half_ref[0]
     copies = [
         pltpu.make_async_copy(
-            weight_ref.at[rows(half), :, pl.ds(step * block, block)], blocks.at[step], arrived.at[step]
+            weight_ref.at[half_rows(half, count), :, pl.ds(step * block, block)],
+            blocks.at[step],
+            arrived.at[step],
         )
         for step in range(steps)
     ]
-    hold = pltpu.make_async_copy(weight_ref.at[rows(1 - half)], held_ref, held_arrived)
+    hold = pltpu.make_async_copy(
+        weight_ref.at[half_rows(1 - half, count), :, pl.ds(0, held_ref.shape[2])], held_ref, held_arrived
+    )
     for copy in copies:
         copy.start()
     hold.start()
@@ -183,6 +188,10 @@
         weights = blocks.at[step].reshape(2 * count, block)[...]
         sums_ref[:, step * block : (step + 1) * block] = dot_f32(spread[...], weights)
     hold.wait()
+
+
+def half_rows(half, count):
+    return pl.ds(pl.multiple_of(half * count, count), count)
 
 
 def project(half, states, weight):
@@ -197,7 +206,7 @@
         out_specs=[in_vmem, pl.BlockSpec(memory_space=pl.ANY)],
         out_shape=[
             jax.ShapeDtypeStruct((2 * slots, width), jnp.float32),
-            pltpu.VMEM((count, 2, width), weight.dtype),
+            pltpu.VMEM((count, 2, block), weight.dtype),
         ],
         scratch_shapes=[
             pltpu.VMEM((2 * slots, 2 * count), jnp.bfloat16),
@@ -213,59 +222,107 @@
     )(half, states, weight)
 
 
-def project_more_body(parts, *refs):
-    states_refs, (weight_ref, before_ref, out_ref, spread) = refs[:parts], refs[parts:]
+def project_more_body(runs, half_ref, *refs):
+    states_refs, (weight_ref, held_ref, before_ref, out_ref, spread, blocks, arrived) = refs[:runs], refs[runs:]
     slots = out_ref.shape[1]
-    count, _, width = weight_ref.shape
-    block = column_block(width)
+    count = spread.shape[1] // 2
+    later_steps, _, _, block = blocks.shape
+    copies = [
+        pltpu.make_async_copy(
+            weight_ref.at[half_rows(half_ref[0], count), :, pl.ds((step + 1) * block, block)],
+            blocks.at[step],
+            arrived.at[step],
+        )
+        for step in range(later_steps)
+    ]
+    for copy in copies:
+        copy.start()
     spread_states(states_refs, spread)
-    flat = weight_ref.reshape(2 * count, width)
-    for at in range(0, width, block):
-        product = dot_f32(spread[...], flat[:, at : at + block])
-        total = (before_ref[:, at : at + block] + product).astype(jnp.bfloat16)
-        for col in range(0, block, HEAD):
-            head = (at + col) // HEAD
-            out_ref[head, :, :HEAD] = total[:slots, col : col + HEAD]
-            out_ref[head, :, HEAD:] = total[slots:, col : col + HEAD]
-
-
-def project_more(states, weight, before):
+    for step in range(later_steps + 1):
+        if step:
+            copies[step - 1].wait()
+        weights = (blocks.at[step - 1] if step else held_ref).reshape(2 * count, block)[...]
+        before = before_ref[:, step * block : (step + 1) * block]
+        total = (before + dot_f32(spread[...], weights)).astype(jnp.bfloat16)
+        for part in range(block // HEAD):
+            head = step * (block // HEAD) + part
+            cols = slice(part * HEAD, (part + 1) * HEAD)
+            out_ref[head, :, :HEAD] = total[:slots, cols]
+            out_ref[head, :, HEAD:] = total[slots:, cols]
+
+
+def project_more(half, states, weight, held, before):
     slots = states[0].shape[1]
-    count, _, width = weight.shape
+    width = weight.shape[2]
+    block = held.shape[2]
+    later_steps = width // block - 1
+    count = sum(run_states.shape[0] for run_states in states) * HEAD
     in_vmem = pl.BlockSpec(memory_space=pltpu.VMEM)
     return pl.pallas_call(
         functools.partial(project_more_body, len(states)),
-        in_specs=[in_vmem] * (len(states) + 2),
+        in_specs=[pl.BlockSpec(memory_space=pltpu.SMEM)]
+        + [in_vmem] * len(states)
+        + [pl.BlockSpec(memory_space=pl.ANY), in_vmem, in_vmem],
         out_specs=in_vmem,
         out_shape=jax.ShapeDtypeStruct((width // HEAD, slots, 2 * HEAD), jnp.bfloat16),
-        scratch_shapes=[pltpu.VMEM((2 * slots, 2 * count), jnp.bfloat16)],
-        compiler_params=params(24),
+        scratch_shapes=[
+            pltpu.VMEM((2 * slots, 2 * count), jnp.bfloat16),
+            pltpu.VMEM((later_steps, count, 2, block), weight.dtype),
+            pltpu.SemaphoreType.DMA((later_steps,)),
+        ],
+        compiler_params=params(28),
         cost_estimate=pl.CostEstimate(
             flops=8 * slots * count * width, bytes_accessed=4 * count * width, transcendentals=0
         ),
         name="project_more",
-    )(*states, pltpu.with_memory_space_constraint(weight, pltpu.VMEM), before)
-
-
-def attend_body(block, bias_ref, query_ref, kv_ref, out_ref, values):
+    )(half, *states, weight, pltpu.with_memory_space_constraint(held, pltpu.VMEM), before)
+
+
+def attend_body(block, bias_ref, query_ref, kv_ref, out_ref, values, scores, terms):
     slots = kv_ref.shape[0]
+    count = slots // block
     values[:, :HEAD] = kv_ref[:, HEAD:]
     values[:, HEAD:] = jnp.ones((slots, HEAD), jnp.bfloat16)
     row = lax.broadcasted_iota(jnp.int32, (block, block), 0)
     col = lax.broadcasted_iota(jnp.int32, (block, block), 1)
     later = jnp.where(col <= row, 0.0, MASKED)
-    for at in range(0, slots, block):
-        seen = at + block
-        query = query_ref[at:seen]
-        scores = dot_f32(query, kv_ref[:seen, :HEAD], 1) * SCALE + bias_ref[:, :seen]
-        last = scores[:, at:] + later
-        scores = last if at == 0 else jnp.concatenate([scores[:, :at], last], axis=1)
-        terms = jnp.exp(scores - jnp.max(scores, axis=1, keepdims=True))
-        high = terms.astype(jnp.bfloat16)
-        low = (terms - high.astype(jnp.float32)).astype(jnp.bfloat16)
-        summed = dot_f32(high, values[:seen]) + dot_f32(low, values[:seen])
-        mixed = query.astype(jnp.float32) + summed[:, :HEAD] / summed[:, HEAD:]
-        out_ref[at:seen] = mixed.astype(jnp.bfloat16)
+    top = [None] * count
+
+    def tile(index):
+        return slice(index * block, (index + 1) * block)
+
+    def score(at, index):
+        found = dot_f32(query_ref[tile(at)], kv_ref[tile(index), :HEAD], 1) * SCALE_2 + bias_ref[:, tile(index)]
+        if index == at:
+            found = found + later
+        scores[at % 2, :, tile(index)] = found
+        for lane in range(0, block, 128):
+            part = found[:, lane : lane + 128]
+            top[at] = part if top[at] is None else jnp.maximum(top[at], part)
+        if index == at:
+            top[at] = jnp.max(top[at], axis=1, keepdims=True)
+
+    def term(at, index):
+        found = jnp.exp2(scores[at % 2, :, tile(index)] - top[at])
+        high = found.astype(jnp.bfloat16)
+        terms[at % 2, 0, :, tile(index)] = high
+        terms[at % 2, 1, :, tile(index)] = (found - high.astype(jnp.float32)).astype(jnp.bfloat16)
+
+    for at in range(-2, count):
+        total = None
+        for index in range(at + 3):
+            if at + 1 < count and 0 <= at + 1 and index <= at + 1:
+                term(at + 1, index)
+            if 0 <= at and index <= at:
+                part = dot_f32(terms[at % 2, 0, :, tile(index)], values[tile(index)]) + dot_f32(
+                    terms[at % 2, 1, :, tile(index)], values[tile(index)]
+                )
+                total = part if total is None else total + part
+            if at + 2 < count:
+                score(at + 2, index)
+        if 0 <= at:
+            mixed = query_ref[tile(at)].astype(jnp.float32) + total[:, :HEAD] / total[:, HEAD:]
+            out_ref[tile(at)] = mixed.astype(jnp.bfloat16)
 
 
 def attend(bias, query, kv):
@@ -274,8 +331,12 @@
     return pl.pallas_call(
         functools.partial(attend_body, block),
         out_shape=jax.ShapeDtypeStruct((slots, HEAD), jnp.bfloat16),
-        scratch_shapes=[pltpu.VMEM((slots, 2 * HEAD), jnp.bfloat16)],
-        compiler_params=params(24),
+        scratch_shapes=[
+            pltpu.VMEM((slots, 2 * HEAD), jnp.bfloat16),
+            pltpu.VMEM((2, block, slots), jnp.float32),
+            pltpu.VMEM((2, 2, block, slots), jnp.bfloat16),
+        ],
+        compiler_params=params(28),
         name="attend",
     )(bias, query, kv)
 
@@ -333,13 +394,16 @@
     if mp_count == 2:
         others = [lax.ppermute(run_states, "mp", [(0, 1), (1, 0)]) for run_states in (first, second)]
         before, held = project(half[None], states, kv_weight)
+        other_half = 1 - half
     else:
         others = [lax.all_gather(states, "mp", axis=0, tiled=True)]
-        before, held = jnp.zeros((2 * slots, width), jnp.float32), kv_weight
+        before = jnp.zeros((2 * slots, width), jnp.float32)
+        other_half = jnp.zeros_like(half)
+        held = kv_weight[:, :, : column_block(width)]
     if paired:
         sent, others[0] = lax.optimization_barrier((states, others[0]))
         query = lax.all_to_all(sent, "ctx", 0, 0, tiled=True).reshape(ctx_count * slots, HEAD)
-    kv = project_more(others, held, before)
+    kv = project_more(other_half[None], others, kv_weight, held, before)
 
     valid = patch_bounds[:, 1:] > patch_bounds[:, :-1]
     if paired:

time: 120 us -> 116 us (0.967)
  Pallas kernels: 42 us -> 38 us
    pallas_call x1, Pallas kernels: 10.1 us -> 7.47 us  [attend(): pl.pallas_call(functools.partial(attend_body, block), out_shape=jax.Shape...]
    pallas_call x1, Pallas kernels: 11.8 us -> 9.42 us  [project(): pl.pallas_call(project_body, in_specs=[pl.BlockSpec(memory_space=pltpu.SM...]
  transfers between devices with their start and end apart: 6 -> 6, of which waited for: 3 -> 3; matrix products, arithmetic and copies ran while one was open for 0% -> 0% of each run, Pallas kernels for 22% -> 21%
where the time goes in v4:
time: 116 us
  waiting for transfers between devices  45.8 us (39%)
  Pallas kernels  38 us (33%)
  starting transfers between devices  29.8 us (26%)
    all_to_all x1, waiting for transfers between devices, shards(): lax.all_to_all(kv, 'ctx', 0, 0, tiled=True)  27.2 us
    all_to_all x1, waiting for transfers between devices, shards(): mixed = lax.all_to_all(mixed, 'ctx', 0, 0, tiled=True)  16.6 us
    pallas_call x2, Pallas kernels, patch_states(): pl.pallas_call(functools.partial(patch_body, heads, joins), grid=(1,), in...  12.5 us
    all_to_all x1, starting transfers between devices, shards(): lax.all_to_all(sent, 'ctx', 0, 0, tiled=True)  9.88 us
    pallas_call x1, Pallas kernels, project(): pl.pallas_call(project_body, in_specs=[pl.BlockSpec(memory_space=pltpu.SM...  9.42 us
    pallas_call x1, Pallas kernels, project_more(): pl.pallas_call(functools.partial(project_more_body, len(states)), in_spec...  8.59 us
    all_to_all x1, starting transfers between devices, shards(): mixed = lax.all_to_all(mixed, 'ctx', 0, 0, tiled=True)  8.01 us
    pallas_call x1, Pallas kernels, attend(): pl.pallas_call(functools.partial(attend_body, block), out_shape=jax.Shape...  7.47 us
  transfers between devices with their start and end apart: 6, of which 3 were waited for; matrix products, arithmetic and copies ran while one was open for 0% of the time, Pallas kernels for 21%

profile of v4, /device:TPU:0, one launch (start us, length us, event | category | flops | bytes accessed | tf_op | source)
XLA Modules:
  0.0 115.9 jit_solution(3960298783452572345)
XLA Ops:
  0.0 0.9 slice.11
  0.9 1.3 %collective-permute-start = (bf16[16,3,2048]{2,0,1:T(8,128)(2,1)S(1)}, bf16[16,3,2048]{2,0,1:T(8,128)(2,1)S(1)}, u32[]{:S(2)}, u32[]{:S(2)}) collective-permute-start(bf16[16,3,2048]{2,0,1:T(8,128)(2,1)S(1)} %slice.11), channel_id=1, source_target_pairs={{2,0},{4,2},{6,4},{8,6},{10,8},{12,10},{14,12},{16,14},{18,16},{20... | collective-permute-start | bytes 589832 | tf_op jit(solution)/shard_map/ppermute | solution.py:380
  2.2 2.0 %collective-permute-done = bf16[16,3,2048]{2,0,1:T(8,128)(2,1)S(1)} collective-permute-done((bf16[16,3,2048]{2,0,1:T(8,128)(2,1)S(1)}, bf16[16,3,2048]{2,0,1:T(8,128)(2,1)S(1)}, u32[]{:S(2)}, u32[]{:S(2)}) %collective-permute-start) | collective-permute-done | bytes 196640 | tf_op jit(solution)/shard_map/ppermute | solution.py:380
  4.3 5.8 %patch_states.2.refs_0_ = bf16[8,160,128]{2,1,0:T(8,128)(2,1)S(1)} custom-call(s32[1]{0:T(128)} %bitcast.place_ref, s32[16,161]{1,0:T(8,128)} %bounds_ref.3, bf16[3,512,2048]{2,1,0:T(8,128)(2,1)} %bitcast.18, bf16[3,16,2048]{2,1,0:T(8,128)(2,1)S(1)} %bitcast.16), custom_call_target="tpu_custom_call" | custom-call | tf_op jit(solution)/shard_map/patch_states/pallas_call | solution.py:124
  10.1 3.0 %collective-permute-start.1 = (bf16[8,160,128]{2,1,0:T(8,128)(2,1)S(1)}, bf16[8,160,128]{2,1,0:T(8,128)(2,1)S(1)}, u32[]{:S(2)}, u32[]{:S(2)}) collective-permute-start(bf16[8,160,128]{2,1,0:T(8,128)(2,1)S(1)} %patch_states.2.refs_0_), channel_id=1, source_target_pairs={{0,1},{1,0},{2,3},{3,2},{4,5},{5,4},{6,7},{7,6},{8,9},{9,8},{10,11... | collective-permute-start | bytes 983048 | tf_op jit(solution)/shard_map/ppermute | solution.py:395
  13.1 6.7 %patch_states.3 = (bf16[8,160,128]{2,1,0:T(8,128)(2,1)S(1)}, bf16[16,160,128]{2,1,0:T(8,128)(2,1)}) custom-call(s32[1]{0:T(128)} %bitcast.place_ref, s32[16,161]{1,0:T(8,128)} %bounds_ref.3, bf16[3,512,2048]{2,1,0:T(8,128)(2,1)} %bitcast.19, bf16[3,16,2048]{2,1,0:T(8,128)(2,1)S(1)} %bitcast.17, bf16[8,160,128]{2,1,0:T(8,128)(2,1)S(1)} %patch_states.2.refs_0_), custom_call_target="tpu_custom_call" | custom-call | tf_op jit(solution)/shard_map/patch_states/pallas_call | solution.py:124
  19.9 0.0 collective-permute-done.1.refs_0_
  19.9 9.9 %all-to-all-start = ((bf16[16,160,128]{2,1,0:T(8,128)(2,1)}), bf16[16,160,128]{2,1,0:T(8,128)(2,1)S(1)}, u32[]{:S(2)}, u32[]{:S(2)}) async-start(bf16[16,160,128]{2,1,0:T(8,128)(2,1)} %get-tuple-element.12.states_ref), calls=%async_computation | async-start | bytes 1310720 | tf_op jit(solution)/shard_map/all_to_all | solution.py:405
  29.8 1.6 %collective-permute-start.2 = (bf16[8,160,128]{2,1,0:T(8,128)(2,1)S(1)}, bf16[8,160,128]{2,1,0:T(8,128)(2,1)S(1)}, u32[]{:S(2)}, u32[]{:S(2)}) collective-permute-start(bf16[8,160,128]{2,1,0:T(8,128)(2,1)S(1)} %get-tuple-element.14), channel_id=1, source_target_pairs={{0,1},{1,0},{2,3},{3,2},{4,5},{5,4},{6,7},{7,6},{8,9},{9,8},{10,11... | collective-permute-start | bytes 983048 | tf_op jit(solution)/shard_map/ppermute | solution.py:395
  31.4 9.4 %project.1 = (f32[320,2048]{1,0:T(8,128)S(1)}, bf16[2048,2,512]{2,1,0:T(2,128)(2,1)S(1)}) custom-call(s32[1]{0:T(128)} %bitcast.5.half_ref, bf16[16,160,128]{2,1,0:T(8,128)(2,1)} %get-tuple-element.12.states_ref, bf16[4096,2,2048]{2,1,0:T(2,128)(2,1)} %refs_2_.1), custom_call_target="tpu_custom_call" | custom-call | flops 5368709120 | bytes 33554432 | tf_op jit(solution)/shard_map/project/pallas_call | solution.py:203
  40.8 0.0 collective-permute-done.2.refs_1_
  40.8 0.0 copy-start
  40.8 8.6 %project_more.1 = bf16[16,160,256]{2,1,0:T(8,128)(2,1)} custom-call(s32[1]{0:T(128)} %bitcast.4.half_ref, bf16[8,160,128]{2,1,0:T(8,128)(2,1)S(1)} %collective-permute-done.1.refs_0_, bf16[8,160,128]{2,1,0:T(8,128)(2,1)S(1)} %collective-permute-done.2.refs_1_, bf16[4096,2,2048]{2,1,0:T(2,128)(2,1)} %refs_2_.1, ...), custom_call_target="tpu_custom_call" | custom-call | flops 5368709120 | bytes 16777216 | tf_op jit(solution)/shard_map/project_more/pallas_call | solution.py:261
  49.4 0.0 all-to-all-done
  49.4 6.0 %all-to-all-start.1 = ((bf16[16,160,256]{2,1,0:T(8,128)(2,1)}), bf16[16,160,256]{2,1,0:T(8,128)(2,1)S(1)}, u32[]{:S(2)}, u32[]{:S(2)}) async-start(bf16[16,160,256]{2,1,0:T(8,128)(2,1)} %project_more.1), calls=%async_computation.1 | async-start | bytes 2621440 | tf_op jit(solution)/shard_map/all_to_all | solution.py:411
  55.4 0.0 copy-done
  55.4 0.1 broadcast_select_fusion
  55.5 0.1 reshape.17.bias_ref
  55.6 27.2 %all-to-all-done.1 = bf16[16,160,256]{2,1,0:T(8,128)(2,1)S(1)} async-done(((bf16[16,160,256]{2,1,0:T(8,128)(2,1)}), bf16[16,160,256]{2,1,0:T(8,128)(2,1)S(1)}, u32[]{:S(2)}, u32[]{:S(2)}) %all-to-all-start.1) | async-done | bytes 1310752 | tf_op jit(solution)/shard_map/all_to_all | solution.py:411
  82.8 7.5 %attend.1 = bf16[2560,128]{1,0:T(8,128)(2,1)} custom-call(f32[1,2560]{1,0:T(1,128)S(1)} %reshape.17.bias_ref, bf16[2560,128]{1,0:T(8,128)(2,1)S(1)} %bitcast.15, bf16[2560,256]{1,0:T(8,128)(2,1)S(1)} %bitcast.14), custom_call_target="tpu_custom_call" | custom-call | tf_op jit(solution)/shard_map/attend/pallas_call | solution.py:331
  90.3 8.0 %all-to-all-start.2 = ((bf16[16,160,128]{2,1,0:T(8,128)(2,1)}), bf16[16,160,128]{2,1,0:T(8,128)(2,1)S(1)}, u32[]{:S(2)}, u32[]{:S(2)}) async-start(bf16[16,160,128]{2,1,0:T(8,128)(2,1)} %bitcast.7), calls=%async_computation.2 | async-start | bytes 1310720 | tf_op jit(solution)/shard_map/all_to_all | solution.py:413
  98.4 16.6 %all-to-all-done.2 = bf16[16,160,128]{2,1,0:T(8,128)(2,1)S(1)} async-done(((bf16[16,160,128]{2,1,0:T(8,128)(2,1)}), bf16[16,160,128]{2,1,0:T(8,128)(2,1)S(1)}, u32[]{:S(2)}, u32[]{:S(2)}) %all-to-all-start.2) | async-done | bytes 655392 | tf_op jit(solution)/shard_map/all_to_all | solution.py:413
  114.9 1.0 bitcast_select_fusion
  (1 shorter events, 0.0 us)
Async XLA Ops:
  0.9 3.3 %collective-permute-start = (bf16[16,3,2048]{2,0,1:T(8,128)(2,1)S(1)}, bf16[16,3,2048]{2,0,1:T(8,128)(2,1)S(1)}, u32[]{:S(2)}, u32[]{:S(2)}) collective-permute-start(bf16[16,3,2048]{2,0,1:T(8,128)(2,1)S(1)} %slice.11), channel_id=1, source_target_pairs={{2,0},{4,2},{6,4},{8,6},{10,8},{12,10},{14,12},{16,14},{18,16},{20... | collective-permute-start | bytes 589832 | tf_op jit(solution)/shard_map/ppermute | solution.py:380
  10.1 9.8 %collective-permute-start.1 = (bf16[8,160,128]{2,1,0:T(8,128)(2,1)S(1)}, bf16[8,160,128]{2,1,0:T(8,128)(2,1)S(1)}, u32[]{:S(2)}, u32[]{:S(2)}) collective-permute-start(bf16[8,160,128]{2,1,0:T(8,128)(2,1)S(1)} %patch_states.2.refs_0_), channel_id=1, source_target_pairs={{0,1},{1,0},{2,3},{3,2},{4,5},{5,4},{6,7},{7,6},{8,9},{9,8},{10,11... | collective-permute-start | bytes 983048 | tf_op jit(solution)/shard_map/ppermute | solution.py:395
  19.9 29.6 %all-to-all-start = ((bf16[16,160,128]{2,1,0:T(8,128)(2,1)}), bf16[16,160,128]{2,1,0:T(8,128)(2,1)S(1)}, u32[]{:S(2)}, u32[]{:S(2)}) async-start(bf16[16,160,128]{2,1,0:T(8,128)(2,1)} %get-tuple-element.12.states_ref), calls=%async_computation | async-start | bytes 1310720 | tf_op jit(solution)/shard_map/all_to_all | solution.py:405
  29.8 11.0 %collective-permute-start.2 = (bf16[8,160,128]{2,1,0:T(8,128)(2,1)S(1)}, bf16[8,160,128]{2,1,0:T(8,128)(2,1)S(1)}, u32[]{:S(2)}, u32[]{:S(2)}) collective-permute-start(bf16[8,160,128]{2,1,0:T(8,128)(2,1)S(1)} %get-tuple-element.14), channel_id=1, source_target_pairs={{0,1},{1,0},{2,3},{3,2},{4,5},{5,4},{6,7},{7,6},{8,9},{9,8},{10,11... | collective-permute-start | bytes 983048 | tf_op jit(solution)/shard_map/ppermute | solution.py:395
  40.8 14.6 %copy-start = (s32[16,161]{1,0:T(8,128)S(1)}, s32[16,161]{1,0:T(8,128)}, u32[]{:S(2)}) copy-start(s32[16,161]{1,0:T(8,128)} %bounds_ref.3) | copy-start | bytes 30916
  49.4 33.4 %all-to-all-start.1 = ((bf16[16,160,256]{2,1,0:T(8,128)(2,1)}), bf16[16,160,256]{2,1,0:T(8,128)(2,1)S(1)}, u32[]{:S(2)}, u32[]{:S(2)}) async-start(bf16[16,160,256]{2,1,0:T(8,128)(2,1)} %project_more.1), calls=%async_computation.1 | async-start | bytes 2621440 | tf_op jit(solution)/shard_map/all_to_all | solution.py:411
  90.3 24.6 %all-to-all-start.2 = ((bf16[16,160,128]{2,1,0:T(8,128)(2,1)}), bf16[16,160,128]{2,1,0:T(8,128)(2,1)S(1)}, u32[]{:S(2)}, u32[]{:S(2)}) async-start(bf16[16,160,128]{2,1,0:T(8,128)(2,1)} %bitcast.7), calls=%async_computation.2 | async-start | bytes 1310720 | tf_op jit(solution)/shard_map/all_to_all | solution.py:413

commit v5 on v4

--- a/solution.py
+++ b/solution.py
@@ -31,59 +31,89 @@
     return pltpu.roll(row, row.shape[1] - steps, 1)
 
 
-def patch_body(heads, joins, place_ref, bounds_ref, main_ref, edge_ref, *refs):
+def outline_body(place_ref, bounds_ref, parts_ref, held_ref, pens, cuts, inside, pick, arrived):
+    load = pltpu.make_async_copy(parts_ref, held_ref, arrived)
+    load.start()
+    byte_rows = parts_ref.shape[1]
+    slots, lanes = inside.shape
+    rows = pens.shape[1]
+    entries = bounds_ref.shape[1]
+    place = place_ref[0]
+    local = (bounds_ref[pl.ds(place, 1), :] - place * byte_rows).astype(jnp.float32)
+    entry = lax.broadcasted_iota(jnp.int32, (slots, entries), 1)
+    slot = lax.broadcasted_iota(jnp.int32, (slots, entries), 0)
+    first = jnp.sum(jnp.where(entry == slot, local, 0.0), axis=1, keepdims=True)
+    after = jnp.sum(jnp.where(entry == slot + 1, local, 0.0), axis=1, keepdims=True)
+    byte = lax.broadcasted_iota(jnp.int32, (slots, lanes), 1).astype(jnp.float32)
+    member = (byte >= first) & (byte < after)
+    inside[...] = jnp.where(member, 1.0, 0.0)
+    pick[...] = jnp.where(member & (byte == first), 1.0, 0.0)[:, :rows].astype(jnp.bfloat16)
+    edges = jnp.where((byte == first) | (byte == after), 1.0, 0.0)
+    cut = jnp.where(jnp.max(edges, axis=0, keepdims=True) > 0.0, -jnp.inf, 0.0)
+    cut = ahead(jnp.broadcast_to(cut, (8, lanes)), 1)
+    cuts[0] = cut
+    at = lax.broadcasted_iota(jnp.int32, (rows, entries), 0).astype(jnp.float32)
+    begins = jnp.max(jnp.where(at == local, 1.0, 0.0), axis=1, keepdims=True)
+    pen = jnp.broadcast_to(jnp.where(begins > 0.0, -jnp.inf, 0.0), (rows, HEAD))
+    pen = pltpu.roll(pen, rows - 1, 0)
+    pens[0] = pen
+    for level in range(1, 4):
+        steps = 1 << (level - 1)
+        cut = cut + ahead(cut, steps)
+        cuts[level] = cut
+        pen = pen + pltpu.roll(pen, rows - steps, 0)
+        pens[level] = pen
+    load.wait()
+
+
+def outline(place, bounds, parts, slots):
+    rows = parts.shape[1] + WIN
+    lanes = -(-rows // 128) * 128
+    in_vmem = pl.BlockSpec(memory_space=pltpu.VMEM)
+    anywhere = pl.BlockSpec(memory_space=pl.ANY)
+    found = pl.pallas_call(
+        outline_body,
+        in_specs=[pl.BlockSpec(memory_space=pltpu.SMEM), in_vmem, anywhere],
+        out_specs=[anywhere] + [in_vmem] * 4,
+        out_shape=[
+            pltpu.VMEM(parts.shape, parts.dtype),
+            pltpu.VMEM((4, rows, HEAD), jnp.float32),
+            pltpu.VMEM((4, 8, lanes), jnp.float32),
+            pltpu.VMEM((slots, lanes), jnp.float32),
+            pltpu.VMEM((slots, rows), jnp.bfloat16),
+        ],
+        scratch_shapes=[pltpu.SemaphoreType.DMA],
+        compiler_params=params(20),
+        name="outline",
+    )(place, bounds, parts)
+    return [pltpu.with_memory_space_constraint(array, pltpu.VMEM) for array in found]
+
+
+def patch_body(first_head, joins, main_ref, pens, cuts, inside, pick, edge_ref, *refs):
     if joins:
-        earlier_ref, out_ref, whole_ref, *refs = refs
+        earlier_ref, out_ref, whole_ref, tops = refs
     else:
-        out_ref, *refs = refs
-    pens, cuts, inside, pick, tops = refs
-    byte_rows = main_ref.shape[1]
-    slots = out_ref.shape[1]
-    rows = byte_rows + WIN
+        out_ref, tops = refs
+    heads = out_ref.shape[0]
+    rows = pens.shape[1]
     lanes = inside.shape[1]
-    entries = bounds_ref.shape[1]
-
-    @pl.when(pl.program_id(0) == 0)
-    def _():
-        place = place_ref[0]
-        local = (bounds_ref[pl.ds(place, 1), :] - place * byte_rows).astype(jnp.float32)
-        entry = lax.broadcasted_iota(jnp.int32, (slots, entries), 1)
-        slot = lax.broadcasted_iota(jnp.int32, (slots, entries), 0)
-        first = jnp.sum(jnp.where(entry == slot, local, 0.0), axis=1, keepdims=True)
-        after = jnp.sum(jnp.where(entry == slot + 1, local, 0.0), axis=1, keepdims=True)
-        byte = lax.broadcasted_iota(jnp.int32, (slots, lanes), 1).astype(jnp.float32)
-        member = (byte >= first) & (byte < after)
-        inside[...] = jnp.where(member, 1.0, 0.0)
-        pick[...] = jnp.where(member & (byte == first), 1.0, 0.0)[:, :rows].astype(jnp.bfloat16)
-        edges = jnp.where((byte == first) | (byte == after), 1.0, 0.0)
-        cut = jnp.where(jnp.max(edges, axis=0, keepdims=True) > 0.0, -jnp.inf, 0.0)
-        cut = ahead(jnp.broadcast_to(cut, (8, lanes)), 1)
-        cuts[0] = cut
-        at = lax.broadcasted_iota(jnp.int32, (rows, entries), 0).astype(jnp.float32)
-        begins = jnp.max(jnp.where(at == local, 1.0, 0.0), axis=1, keepdims=True)
-        pen = jnp.broadcast_to(jnp.where(begins > 0.0, -jnp.inf, 0.0), (rows, HEAD))
-        pen = pltpu.roll(pen, rows - 1, 0)
-        pens[0] = pen
-        for level in range(1, 4):
-            steps = 1 << (level - 1)
-            cut = cut + ahead(cut, steps)
-            cuts[level] = cut
-            pen = pen + pltpu.roll(pen, rows - steps, 0)
-            pens[level] = pen
+
+    def head_cols(head):
+        return slice((first_head + head) * HEAD, (first_head + head + 1) * HEAD)
 
     for head in range(heads):
-        cols = slice(head * HEAD, (head + 1) * HEAD)
+        cols = head_cols(head)
         top = jnp.concatenate([main_ref[0, :, cols], edge_ref[0, :, cols]], axis=0).astype(jnp.float32)
         for level in range(4):
             top = jnp.maximum(top, pltpu.roll(top, rows - (1 << level), 0) + pens[level])
-        tops[:, cols] = top.astype(jnp.bfloat16)
+        tops[:, head * HEAD : (head + 1) * HEAD] = top.astype(jnp.bfloat16)
     queries = dot_f32(pick[...], tops[...]).astype(jnp.bfloat16)
     spare = jnp.zeros((lanes - rows, HEAD), jnp.bfloat16)
     score_rows = []
     for head in range(heads):
-        cols = slice(head * HEAD, (head + 1) * HEAD)
+        cols = head_cols(head)
         keys = jnp.concatenate([main_ref[1, :, cols], edge_ref[1, :, cols], spare], axis=0)
-        scores = dot_f32(queries[:, cols], keys, 1) * inside[...]
+        scores = dot_f32(queries[:, head * HEAD : (head + 1) * HEAD], keys, 1) * inside[...]
         score_rows.append(jnp.sum(scores, axis=0, keepdims=True))
     scores = jnp.concatenate(score_rows + [jnp.zeros((8 - heads, lanes), jnp.float32)] * (heads < 8), axis=0)
     fore = back = scores
@@ -101,7 +131,7 @@
         back = back + pltpu.roll(back * keep, steps, 1)
     weights = terms / (fore + back - terms)
     for head in range(heads):
-        cols = slice(head * HEAD, (head + 1) * HEAD)
+        cols = head_cols(head)
         values = jnp.concatenate([main_ref[2, :, cols], edge_ref[2, :, cols], spare], axis=0)
         spread = (inside[...] * weights[head : head + 1]).astype(jnp.bfloat16)
         out_ref[head] = dot_f32(spread, values).astype(jnp.bfloat16)
@@ -110,39 +140,21 @@
         whole_ref[heads:] = out_ref[...]
 
 
-def patch_states(place, bounds, parts, edge, slots, first_head, heads, earlier=None):
-    byte_rows = parts.shape[1]
-    rows = byte_rows + WIN
-    lanes = -(-rows // 128) * 128
-    width = heads * HEAD
-    run = first_head // heads
+def patch_states(found, edge, first_head, heads, earlier=None):
+    slots, rows = found[-1].shape
     joins = earlier is not None
     states = jax.ShapeDtypeStruct((heads, slots, HEAD), jnp.bfloat16)
-    states_spec = pl.BlockSpec((heads, slots, HEAD), lambda i: (0, 0, 0))
     whole = jax.ShapeDtypeStruct((2 * heads, slots, HEAD), jnp.bfloat16)
-    whole_spec = pl.BlockSpec((2 * heads, slots, HEAD), lambda i: (0, 0, 0))
+    in_vmem = pl.BlockSpec(memory_space=pltpu.VMEM)
     return pl.pallas_call(
-        functools.partial(patch_body, heads, joins),
-        grid=(1,),
-        in_specs=[
-            pl.BlockSpec(memory_space=pltpu.SMEM),
-            pl.BlockSpec(bounds.shape, lambda i: (0, 0)),
-            pl.BlockSpec((3, byte_rows, width), lambda i: (0, 0, run)),
-            pl.BlockSpec((3, WIN, width), lambda i: (0, 0, run)),
-        ]
-        + [states_spec] * joins,
-        out_specs=[states_spec, whole_spec] if joins else states_spec,
+        functools.partial(patch_body, first_head, joins),
+        in_specs=[in_vmem] * (len(found) + 1 + joins),
+        out_specs=[in_vmem, in_vmem] if joins else in_vmem,
         out_shape=[states, whole] if joins else states,
-        scratch_shapes=[
-            pltpu.VMEM((4, rows, HEAD), jnp.float32),
-            pltpu.VMEM((4, 8, lanes), jnp.float32),
-            pltpu.VMEM((slots, lanes), jnp.float32),
-            pltpu.VMEM((slots, rows), jnp.bfloat16),
-            pltpu.VMEM((rows, width), jnp.bfloat16),
-        ],
+        scratch_shapes=[pltpu.VMEM((rows, heads * HEAD), jnp.bfloat16)],
         compiler_params=params(20),
         name="patch_states",
-    )(place, bounds, parts, edge, *([earlier] if joins else []))
+    )(*found, edge, *([earlier] if joins else []))
 
 
 def column_block(width):
@@ -381,9 +393,8 @@
     parts = byte_qkv.transpose(1, 0, 2)
     edge = edge.transpose(1, 0, 2)
     in_hbm = functools.partial(pltpu.with_memory_space_constraint, memory_space=pltpu.HBM)
-    byte_phase = functools.partial(
-        patch_states, place[None], in_hbm(patch_bounds), in_hbm(parts), edge, slots
-    )
+    found = outline(place[None], in_hbm(patch_bounds), in_hbm(parts), slots)
+    byte_phase = functools.partial(patch_states, found, edge)
     run = max(heads // 2, 1)
     first = byte_phase(0, run)
     states = first

time: 116 us -> 114 us (0.983)
  starting transfers between devices: 29.8 us -> 28 us
    ppermute x2, waiting for transfers between devices: 0.01 us -> 2.63 us  [shards(): lax.ppermute(run_states, 'mp', [(0, 1), (1, 0)])]
    ppermute x1, waiting for transfers between devices: 2.03 us -> 0.01 us  [shards(): lax.ppermute(byte_qkv[:WIN], 'ctx', [(i + 1, i) for i in range(ctx_count...]
    all_to_all x1, starting transfers between devices: 9.88 us -> 8.11 us  [shards(): lax.all_to_all(sent, 'ctx', 0, 0, tiled=True)]
    pallas_call x2 -> x3, Pallas kernels: 12.5 us -> 11.5 us  [the longest x2 7.94 us: patch_states(): pl.pallas_call(functools.partial(patch_body, first_head, joins), in_specs...]
  transfers between devices with their start and end apart: 6 -> 6, of which waited for: 3 -> 3; matrix products, arithmetic and copies ran while one was open for 0% -> 0% of each run, Pallas kernels for 21% -> 23%
where the time goes in v5:
time: 114 us
  waiting for transfers between devices  46.4 us (41%)
  Pallas kernels  36.9 us (32%)
  starting transfers between devices  28 us (25%)
    all_to_all x1, waiting for transfers between devices, shards(): lax.all_to_all(kv, 'ctx', 0, 0, tiled=True)  27.2 us
    all_to_all x1, waiting for transfers between devices, shards(): mixed = lax.all_to_all(mixed, 'ctx', 0, 0, tiled=True)  16.6 us
    pallas_call x1, Pallas kernels, project(): pl.pallas_call(project_body, in_specs=[pl.BlockSpec(memory_space=pltpu.SM...  9.41 us
    pallas_call x1, Pallas kernels, project_more(): pl.pallas_call(functools.partial(project_more_body, len(states)), in_spec...  8.59 us
    all_to_all x1, starting transfers between devices, shards(): lax.all_to_all(sent, 'ctx', 0, 0, tiled=True)  8.11 us
    all_to_all x1, starting transfers between devices, shards(): mixed = lax.all_to_all(mixed, 'ctx', 0, 0, tiled=True)  8.01 us
    pallas_call x2, Pallas kernels, patch_states(): pl.pallas_call(functools.partial(patch_body, first_head, joins), in_specs...  7.94 us
    pallas_call x1, Pallas kernels, attend(): pl.pallas_call(functools.partial(attend_body, block), out_shape=jax.Shape...  7.47 us
  transfers between devices with their start and end apart: 6, of which 3 were waited for; matrix products, arithmetic and copies ran while one was open for 0% of the time, Pallas kernels for 23%

profile of v5, /device:TPU:0, one launch (start us, length us, event | category | flops | bytes accessed | tf_op | source)
XLA Modules:
  0.0 113.7 jit_solution(17823018841538757871)
XLA Ops:
  0.0 0.9 slice.11
  0.9 1.3 %collective-permute-start = (bf16[16,3,2048]{2,0,1:T(8,128)(2,1)S(1)}, bf16[16,3,2048]{2,0,1:T(8,128)(2,1)S(1)}, u32[]{:S(2)}, u32[]{:S(2)}) collective-permute-start(bf16[16,3,2048]{2,0,1:T(8,128)(2,1)S(1)} %slice.11), channel_id=1, source_target_pairs={{2,0},{4,2},{6,4},{8,6},{10,8},{12,10},{14,12},{16,14},{18,16},{20... | collective-permute-start | bytes 589832 | tf_op jit(solution)/shard_map/ppermute | solution.py:392
  2.2 3.5 %outline.1 = (bf16[3,512,2048]{2,1,0:T(8,128)(2,1)S(1)}, f32[4,528,128]{2,1,0:T(8,128)S(1)}, f32[4,8,640]{2,1,0:T(8,128)S(1)}, f32[160,640]{1,0:T(8,128)S(1)}, bf16[160,528]{1,0:T(8,128)(2,1)S(1)}) custom-call(s32[1]{0:T(128)} %bitcast.place_ref, s32[16,161]{1,0:T(8,128)} %bounds_ref.1, bf16[3,512,2048]{2,1,0:T(8,128)(2,1)} %bitcast.18), custom_call_target="tpu_custom_call" | custom-call | tf_op jit(solution)/shard_map/outline/pallas_call | solution.py:74
  5.8 0.0 collective-permute-done
  5.8 3.5 %patch_states.2.refs_0_ = bf16[8,160,128]{2,1,0:T(8,128)(2,1)S(1)} custom-call(bf16[3,512,2048]{2,1,0:T(8,128)(2,1)S(1)} %get-tuple-element.16.main_ref, f32[4,528,128]{2,1,0:T(8,128)S(1)} %get-tuple-element.17.pens, f32[4,8,640]{2,1,0:T(8,128)S(1)} %get-tuple-element.18.cuts, f32[160,640]{1,0:T(8,128)S(1)} %get-tuple-element.19.inside, ...), custom_call_target="tpu_custom_call" | custom-call | tf_op jit(solution)/shard_map/patch_states/pallas_call | solution.py:149
  9.3 3.0 %collective-permute-start.1 = (bf16[8,160,128]{2,1,0:T(8,128)(2,1)S(1)}, bf16[8,160,128]{2,1,0:T(8,128)(2,1)S(1)}, u32[]{:S(2)}, u32[]{:S(2)}) collective-permute-start(bf16[8,160,128]{2,1,0:T(8,128)(2,1)S(1)} %patch_states.2.refs_0_), channel_id=1, source_target_pairs={{0,1},{1,0},{2,3},{3,2},{4,5},{5,4},{6,7},{7,6},{8,9},{9,8},{10,11... | collective-permute-start | bytes 983048 | tf_op jit(solution)/shard_map/ppermute | solution.py:406
  12.3 4.4 %patch_states.3 = (bf16[8,160,128]{2,1,0:T(8,128)(2,1)S(1)}, bf16[16,160,128]{2,1,0:T(8,128)(2,1)}) custom-call(bf16[3,512,2048]{2,1,0:T(8,128)(2,1)S(1)} %get-tuple-element.16.main_ref, f32[4,528,128]{2,1,0:T(8,128)S(1)} %get-tuple-element.17.pens, f32[4,8,640]{2,1,0:T(8,128)S(1)} %get-tuple-element.18.cuts, f32[160,640]{1,0:T(8,128)S(1)} %get-tuple-element.19.inside, ...), custom_call_target="tpu_custom_call" | custom-call | tf_op jit(solution)/shard_map/patch_states/pallas_call | solution.py:149
  16.8 2.6 %collective-permute-done.1.refs_0_ = bf16[8,160,128]{2,1,0:T(8,128)(2,1)S(1)} collective-permute-done((bf16[8,160,128]{2,1,0:T(8,128)(2,1)S(1)}, bf16[8,160,128]{2,1,0:T(8,128)(2,1)S(1)}, u32[]{:S(2)}, u32[]{:S(2)}) %collective-permute-start.1) | collective-permute-done | bytes 327712 | tf_op jit(solution)/shard_map/ppermute | solution.py:406
  19.4 8.1 %all-to-all-start = ((bf16[16,160,128]{2,1,0:T(8,128)(2,1)}), bf16[16,160,128]{2,1,0:T(8,128)(2,1)S(1)}, u32[]{:S(2)}, u32[]{:S(2)}) async-start(bf16[16,160,128]{2,1,0:T(8,128)(2,1)} %get-tuple-element.22.states_ref), calls=%async_computation | async-start | bytes 1310720 | tf_op jit(solution)/shard_map/all_to_all | solution.py:416
  27.5 1.6 %collective-permute-start.2 = (bf16[8,160,128]{2,1,0:T(8,128)(2,1)S(1)}, bf16[8,160,128]{2,1,0:T(8,128)(2,1)S(1)}, u32[]{:S(2)}, u32[]{:S(2)}) collective-permute-start(bf16[8,160,128]{2,1,0:T(8,128)(2,1)S(1)} %get-tuple-element.24), channel_id=1, source_target_pairs={{0,1},{1,0},{2,3},{3,2},{4,5},{5,4},{6,7},{7,6},{8,9},{9,8},{10,11... | collective-permute-start | bytes 983048 | tf_op jit(solution)/shard_map/ppermute | solution.py:406
  29.1 9.4 %project.1 = (f32[320,2048]{1,0:T(8,128)S(1)}, bf16[2048,2,512]{2,1,0:T(2,128)(2,1)S(1)}) custom-call(s32[1]{0:T(128)} %bitcast.5.half_ref, bf16[16,160,128]{2,1,0:T(8,128)(2,1)} %get-tuple-element.22.states_ref, bf16[4096,2,2048]{2,1,0:T(2,128)(2,1)} %refs_2_.1), custom_call_target="tpu_custom_call" | custom-call | flops 5368709120 | bytes 33554432 | tf_op jit(solution)/shard_map/project/pallas_call | solution.py:215
  38.5 0.0 collective-permute-done.2.refs_1_
  38.6 0.0 copy-start
  38.6 8.6 %project_more.1 = bf16[16,160,256]{2,1,0:T(8,128)(2,1)} custom-call(s32[1]{0:T(128)} %bitcast.4.half_ref, bf16[8,160,128]{2,1,0:T(8,128)(2,1)S(1)} %collective-permute-done.1.refs_0_, bf16[8,160,128]{2,1,0:T(8,128)(2,1)S(1)} %collective-permute-done.2.refs_1_, bf16[4096,2,2048]{2,1,0:T(2,128)(2,1)} %refs_2_.1, ...), custom_call_target="tpu_custom_call" | custom-call | flops 5368709120 | bytes 16777216 | tf_op jit(solution)/shard_map/project_more/pallas_call | solution.py:273
  47.2 0.0 all-to-all-done
  47.2 6.0 %all-to-all-start.1 = ((bf16[16,160,256]{2,1,0:T(8,128)(2,1)}), bf16[16,160,256]{2,1,0:T(8,128)(2,1)S(1)}, u32[]{:S(2)}, u32[]{:S(2)}) async-start(bf16[16,160,256]{2,1,0:T(8,128)(2,1)} %project_more.1), calls=%async_computation.1 | async-start | bytes 2621440 | tf_op jit(solution)/shard_map/all_to_all | solution.py:422
  53.2 0.0 copy-done
  53.2 0.1 broadcast_select_fusion
  53.3 0.1 reshape.17.bias_ref
  53.3 27.2 %all-to-all-done.1 = bf16[16,160,256]{2,1,0:T(8,128)(2,1)S(1)} async-done(((bf16[16,160,256]{2,1,0:T(8,128)(2,1)}), bf16[16,160,256]{2,1,0:T(8,128)(2,1)S(1)}, u32[]{:S(2)}, u32[]{:S(2)}) %all-to-all-start.1) | async-done | bytes 1310752 | tf_op jit(solution)/shard_map/all_to_all | solution.py:422
  80.6 7.5 %attend.1 = bf16[2560,128]{1,0:T(8,128)(2,1)} custom-call(f32[1,2560]{1,0:T(1,128)S(1)} %reshape.17.bias_ref, bf16[2560,128]{1,0:T(8,128)(2,1)S(1)} %bitcast.15, bf16[2560,256]{1,0:T(8,128)(2,1)S(1)} %bitcast.14), custom_call_target="tpu_custom_call" | custom-call | tf_op jit(solution)/shard_map/attend/pallas_call | solution.py:343
  88.0 8.0 %all-to-all-start.2 = ((bf16[16,160,128]{2,1,0:T(8,128)(2,1)}), bf16[16,160,128]{2,1,0:T(8,128)(2,1)S(1)}, u32[]{:S(2)}, u32[]{:S(2)}) async-start(bf16[16,160,128]{2,1,0:T(8,128)(2,1)} %bitcast.7), calls=%async_computation.2 | async-start | bytes 1310720 | tf_op jit(solution)/shard_map/all_to_all | solution.py:424
  96.1 16.6 %all-to-all-done.2 = bf16[16,160,128]{2,1,0:T(8,128)(2,1)S(1)} async-done(((bf16[16,160,128]{2,1,0:T(8,128)(2,1)}), bf16[16,160,128]{2,1,0:T(8,128)(2,1)S(1)}, u32[]{:S(2)}, u32[]{:S(2)}) %all-to-all-start.2) | async-done | bytes 655392 | tf_op jit(solution)/shard_map/all_to_all | solution.py:424
  112.7 1.0 bitcast_select_fusion
  (1 shorter events, 0.0 us)
Async XLA Ops:
  0.9 4.8 %collective-permute-start = (bf16[16,3,2048]{2,0,1:T(8,128)(2,1)S(1)}, bf16[16,3,2048]{2,0,1:T(8,128)(2,1)S(1)}, u32[]{:S(2)}, u32[]{:S(2)}) collective-permute-start(bf16[16,3,2048]{2,0,1:T(8,128)(2,1)S(1)} %slice.11), channel_id=1, source_target_pairs={{2,0},{4,2},{6,4},{8,6},{10,8},{12,10},{14,12},{16,14},{18,16},{20... | collective-permute-start | bytes 589832 | tf_op jit(solution)/shard_map/ppermute | solution.py:392
  9.3 10.1 %collective-permute-start.1 = (bf16[8,160,128]{2,1,0:T(8,128)(2,1)S(1)}, bf16[8,160,128]{2,1,0:T(8,128)(2,1)S(1)}, u32[]{:S(2)}, u32[]{:S(2)}) collective-permute-start(bf16[8,160,128]{2,1,0:T(8,128)(2,1)S(1)} %patch_states.2.refs_0_), channel_id=1, source_target_pairs={{0,1},{1,0},{2,3},{3,2},{4,5},{5,4},{6,7},{7,6},{8,9},{9,8},{10,11... | collective-permute-start | bytes 983048 | tf_op jit(solution)/shard_map/ppermute | solution.py:406
  19.4 27.8 %all-to-all-start = ((bf16[16,160,128]{2,1,0:T(8,128)(2,1)}), bf16[16,160,128]{2,1,0:T(8,128)(2,1)S(1)}, u32[]{:S(2)}, u32[]{:S(2)}) async-start(bf16[16,160,128]{2,1,0:T(8,128)(2,1)} %get-tuple-element.22.states_ref), calls=%async_computation | async-start | bytes 1310720 | tf_op jit(solution)/shard_map/all_to_all | solution.py:416
  27.5 11.0 %collective-permute-start.2 = (bf16[8,160,128]{2,1,0:T(8,128)(2,1)S(1)}, bf16[8,160,128]{2,1,0:T(8,128)(2,1)S(1)}, u32[]{:S(2)}, u32[]{:S(2)}) collective-permute-start(bf16[8,160,128]{2,1,0:T(8,128)(2,1)S(1)} %get-tuple-element.24), channel_id=1, source_target_pairs={{0,1},{1,0},{2,3},{3,2},{4,5},{5,4},{6,7},{7,6},{8,9},{9,8},{10,11... | collective-permute-start | bytes 983048 | tf_op jit(solution)/shard_map/ppermute | solution.py:406
  38.6 14.6 %copy-start = (s32[16,161]{1,0:T(8,128)S(1)}, s32[16,161]{1,0:T(8,128)}, u32[]{:S(2)}) copy-start(s32[16,161]{1,0:T(8,128)} %bounds_ref.1) | copy-start | bytes 30916
  47.2 33.4 %all-to-all-start.1 = ((bf16[16,160,256]{2,1,0:T(8,128)(2,1)}), bf16[16,160,256]{2,1,0:T(8,128)(2,1)S(1)}, u32[]{:S(2)}, u32[]{:S(2)}) async-start(bf16[16,160,256]{2,1,0:T(8,128)(2,1)} %project_more.1), calls=%async_computation.1 | async-start | bytes 2621440 | tf_op jit(solution)/shard_map/all_to_all | solution.py:422
  88.0 24.6 %all-to-all-start.2 = ((bf16[16,160,128]{2,1,0:T(8,128)(2,1)}), bf16[16,160,128]{2,1,0:T(8,128)(2,1)S(1)}, u32[]{:S(2)}, u32[]{:S(2)}) async-start(bf16[16,160,128]{2,1,0:T(8,128)(2,1)} %bitcast.7), calls=%async_computation.2 | async-start | bytes 1310720 | tf_op jit(solution)/shard_map/all_to_all | solution.py:424

commit v6 on v5

--- a/solution.py
+++ b/solution.py
@@ -91,10 +91,13 @@
 
 def patch_body(first_head, joins, main_ref, pens, cuts, inside, pick, edge_ref, *refs):
     if joins:
-        earlier_ref, out_ref, whole_ref, tops = refs
+        lead_ref, rest_ref, out_ref, whole_ref, tops = refs
+        held_back = rest_ref.shape[0]
+        heads = out_ref.shape[0] - held_back
     else:
-        out_ref, tops = refs
-    heads = out_ref.shape[0]
+        lead_ref, rest_ref, tops = refs
+        held_back = 0
+        heads = lead_ref.shape[0] + rest_ref.shape[0]
     rows = pens.shape[1]
     lanes = inside.shape[1]
 
@@ -134,27 +137,36 @@
         cols = head_cols(head)
         values = jnp.concatenate([main_ref[2, :, cols], edge_ref[2, :, cols], spare], axis=0)
         spread = (inside[...] * weights[head : head + 1]).astype(jnp.bfloat16)
-        out_ref[head] = dot_f32(spread, values).astype(jnp.bfloat16)
+        states = dot_f32(spread, values).astype(jnp.bfloat16)
+        if joins:
+            out_ref[held_back + head] = states
+        elif head < lead_ref.shape[0]:
+            lead_ref[head] = states
+        else:
+            rest_ref[head - lead_ref.shape[0]] = states
     if joins:
-        whole_ref[: heads] = earlier_ref[...]
-        whole_ref[heads:] = out_ref[...]
-
-
-def patch_states(found, edge, first_head, heads, earlier=None):
+        out_ref[:held_back] = rest_ref[...]
+        whole_ref[: lead_ref.shape[0]] = lead_ref[...]
+        whole_ref[lead_ref.shape[0] :] = out_ref[...]
+
+
+def patch_states(found, edge, first_head, heads, earlier=()):
     slots, rows = found[-1].shape
-    joins = earlier is not None
-    states = jax.ShapeDtypeStruct((heads, slots, HEAD), jnp.bfloat16)
-    whole = jax.ShapeDtypeStruct((2 * heads, slots, HEAD), jnp.bfloat16)
+    if earlier:
+        counts = (earlier[1].shape[0] + heads, first_head + heads)
+    else:
+        lead = max(heads * 5 // 8, 1)
+        counts = (lead, heads - lead)
     in_vmem = pl.BlockSpec(memory_space=pltpu.VMEM)
     return pl.pallas_call(
-        functools.partial(patch_body, first_head, joins),
-        in_specs=[in_vmem] * (len(found) + 1 + joins),
-        out_specs=[in_vmem, in_vmem] if joins else in_vmem,
-        out_shape=[states, whole] if joins else states,
+        functools.partial(patch_body, first_head, bool(earlier)),
+        in_specs=[in_vmem] * (len(found) + 1 + len(earlier)),
+        out_specs=[in_vmem, in_vmem],
+        out_shape=[jax.ShapeDtypeStruct((count, slots, HEAD), jnp.bfloat16) for count in counts],
         scratch_shapes=[pltpu.VMEM((rows, heads * HEAD), jnp.bfloat16)],
         compiler_params=params(20),
         name="patch_states",
-    )(*found, edge, *([earlier] if joins else []))
+    )(*found, edge, *earlier)
 
 
 def column_block(width):
@@ -186,17 +198,31 @@
             blocks.at[step],
             arrived.at[step],
         )
-        for step in range(steps)
+        for step in range(1, steps)
+    ]
+    near = count // 2
+    starts = [
+        pltpu.make_async_copy(
+            weight_ref.at[pl.ds(pl.multiple_of(half * count + part * near, near), near), :, pl.ds(0, block)],
+            blocks.at[0, pl.ds(part * near, near)],
+            arrived.at[part * steps],
+        )
+        for part in range(2)
     ]
     hold = pltpu.make_async_copy(
         weight_ref.at[half_rows(1 - half, count), :, pl.ds(0, held_ref.shape[2])], held_ref, held_arrived
     )
-    for copy in copies:
+    for copy in starts + copies:
         copy.start()
     hold.start()
     spread_states([states_ref], spread)
-    for step in range(steps):
-        copies[step].wait()
+    weights = blocks.at[0].reshape(2 * count, block)
+    starts[0].wait()
+    product = dot_f32(spread[:, :count], weights[:count])
+    starts[1].wait()
+    sums_ref[:, :block] = product + dot_f32(spread[:, count:], weights[count:])
+    for step in range(1, steps):
+        copies[step - 1].wait()
         weights = blocks.at[step].reshape(2 * count, block)[...]
         sums_ref[:, step * block : (step + 1) * block] = dot_f32(spread[...], weights)
     hold.wait()
@@ -223,7 +249,7 @@
         scratch_shapes=[
             pltpu.VMEM((2 * slots, 2 * count), jnp.bfloat16),
             pltpu.VMEM((width // block, count, 2, block), jnp.bfloat16),
-            pltpu.SemaphoreType.DMA((width // block,)),
+            pltpu.SemaphoreType.DMA((width // block + 1,)),
             pltpu.SemaphoreType.DMA,
         ],
         compiler_params=params(28),
@@ -395,15 +421,13 @@
     in_hbm = functools.partial(pltpu.with_memory_space_constraint, memory_space=pltpu.HBM)
     found = outline(place[None], in_hbm(patch_bounds), in_hbm(parts), slots)
     byte_phase = functools.partial(patch_states, found, edge)
-    run = max(heads // 2, 1)
+    run = heads // 2
     first = byte_phase(0, run)
-    states = first
-    if heads > run:
-        second, states = byte_phase(run, run, first)
+    rest, states = byte_phase(run, run, first)
 
     paired = ctx_count == heads
     if mp_count == 2:
-        others = [lax.ppermute(run_states, "mp", [(0, 1), (1, 0)]) for run_states in (first, second)]
+        others = [lax.ppermute(run_states, "mp", [(0, 1), (1, 0)]) for run_states in (first[0], rest)]
         before, held = project(half[None], states, kv_weight)
         other_half = 1 - half
     else:

time: 114 us -> 113 us (level)
  no operation moved by 1% of the time
where the time goes in v6:
time: 113 us; the launch traced here: 112 us
  waiting for transfers between devices  45.4 us (40%)
  Pallas kernels  37 us (33%)
  starting transfers between devices  27.8 us (25%)
    all_to_all x1, waiting for transfers between devices, shards(): lax.all_to_all(kv, 'ctx', 0, 0, tiled=True)  27.2 us
    all_to_all x1, waiting for transfers between devices, shards(): mixed = lax.all_to_all(mixed, 'ctx', 0, 0, tiled=True)  16.6 us
    pallas_call x1, Pallas kernels, project(): pl.pallas_call(project_body, in_specs=[pl.BlockSpec(memory_space=pltpu.SM...  9.48 us
    pallas_call x1, Pallas kernels, project_more(): pl.pallas_call(functools.partial(project_more_body, len(states)), in_spec...  8.59 us
    all_to_all x1, starting transfers between devices, shards(): lax.all_to_all(sent, 'ctx', 0, 0, tiled=True)  8.09 us
    all_to_all x1, starting transfers between devices, shards(): mixed = lax.all_to_all(mixed, 'ctx', 0, 0, tiled=True)  8.01 us
    pallas_call x2, Pallas kernels, patch_states(): pl.pallas_call(functools.partial(patch_body, first_head, bool(earlier)),...  7.93 us
    pallas_call x1, Pallas kernels, attend(): pl.pallas_call(functools.partial(attend_body, block), out_shape=jax.Shape...  7.47 us
  transfers between devices with their start and end apart: 6, of which 3 were waited for; matrix products, arithmetic and copies ran while one was open for 0% of the time, Pallas kernels for 23%

profile of v6, /device:TPU:0, one launch (start us, length us, event | category | flops | bytes accessed | tf_op | source)
XLA Modules:
  0.0 112.5 jit_solution(15314815772412052520)
XLA Ops:
  0.0 0.9 slice.11
  0.9 1.3 %collective-permute-start = (bf16[16,3,2048]{2,0,1:T(8,128)(2,1)S(1)}, bf16[16,3,2048]{2,0,1:T(8,128)(2,1)S(1)}, u32[]{:S(2)}, u32[]{:S(2)}) collective-permute-start(bf16[16,3,2048]{2,0,1:T(8,128)(2,1)S(1)} %slice.11), channel_id=1, source_target_pairs={{2,0},{4,2},{6,4},{8,6},{10,8},{12,10},{14,12},{16,14},{18,16},{20... | collective-permute-start | bytes 589832 | tf_op jit(solution)/shard_map/ppermute | solution.py:418
  2.2 3.5 %outline.1 = (bf16[3,512,2048]{2,1,0:T(8,128)(2,1)S(1)}, f32[4,528,128]{2,1,0:T(8,128)S(1)}, f32[4,8,640]{2,1,0:T(8,128)S(1)}, f32[160,640]{1,0:T(8,128)S(1)}, bf16[160,528]{1,0:T(8,128)(2,1)S(1)}) custom-call(s32[1]{0:T(128)} %bitcast.place_ref, s32[16,161]{1,0:T(8,128)} %bounds_ref.1, bf16[3,512,2048]{2,1,0:T(8,128)(2,1)} %bitcast.18), custom_call_target="tpu_custom_call" | custom-call | tf_op jit(solution)/shard_map/outline/pallas_call | solution.py:74
  5.8 0.0 collective-permute-done
  5.8 3.5 %patch_states.2 = (bf16[5,160,128]{2,1,0:T(8,128)(2,1)S(1)}, bf16[3,160,128]{2,1,0:T(8,128)(2,1)S(1)}) custom-call(bf16[3,512,2048]{2,1,0:T(8,128)(2,1)S(1)} %get-tuple-element.18.main_ref, f32[4,528,128]{2,1,0:T(8,128)S(1)} %get-tuple-element.19.pens, f32[4,8,640]{2,1,0:T(8,128)S(1)} %get-tuple-element.20.cuts, f32[160,640]{1,0:T(8,128)S(1)} %get-tuple-element.21.inside, ...), custom_call_target="tpu_custom_call" | custom-call | tf_op jit(solution)/shard_map/patch_states/pallas_call | solution.py:161
  9.3 3.0 %collective-permute-start.1 = (bf16[5,160,128]{2,1,0:T(8,128)(2,1)S(1)}, bf16[5,160,128]{2,1,0:T(8,128)(2,1)S(1)}, u32[]{:S(2)}, u32[]{:S(2)}) collective-permute-start(bf16[5,160,128]{2,1,0:T(8,128)(2,1)S(1)} %get-tuple-element.23.refs_0_), channel_id=1, source_target_pairs={{0,1},{1,0},{2,3},{3,2},{4,5},{5,4},{6,7},{7,6},{8,9},{9,8},{10,11... | collective-permute-start | bytes 614408 | tf_op jit(solution)/shard_map/ppermute | solution.py:430
  12.3 4.4 %patch_states.3 = (bf16[11,160,128]{2,1,0:T(8,128)(2,1)S(1)}, bf16[16,160,128]{2,1,0:T(8,128)(2,1)}) custom-call(bf16[3,512,2048]{2,1,0:T(8,128)(2,1)S(1)} %get-tuple-element.18.main_ref, f32[4,528,128]{2,1,0:T(8,128)S(1)} %get-tuple-element.19.pens, f32[4,8,640]{2,1,0:T(8,128)S(1)} %get-tuple-element.20.cuts, f32[160,640]{1,0:T(8,128)S(1)} %get-tuple-element.21.inside, ...), custom_call_target="tpu_custom_call" | custom-call | tf_op jit(solution)/shard_map/patch_states/pallas_call | solution.py:161
  16.8 0.0 collective-permute-done.1.refs_0_
  16.8 8.1 %all-to-all-start = ((bf16[16,160,128]{2,1,0:T(8,128)(2,1)}), bf16[16,160,128]{2,1,0:T(8,128)(2,1)S(1)}, u32[]{:S(2)}, u32[]{:S(2)}) async-start(bf16[16,160,128]{2,1,0:T(8,128)(2,1)} %get-tuple-element.26.states_ref), calls=%async_computation | async-start | bytes 1310720 | tf_op jit(solution)/shard_map/all_to_all | solution.py:440
  24.9 1.6 %collective-permute-start.2 = (bf16[11,160,128]{2,1,0:T(8,128)(2,1)S(1)}, bf16[11,160,128]{2,1,0:T(8,128)(2,1)S(1)}, u32[]{:S(2)}, u32[]{:S(2)}) collective-permute-start(bf16[11,160,128]{2,1,0:T(8,128)(2,1)S(1)} %get-tuple-element.28), channel_id=1, source_target_pairs={{0,1},{1,0},{2,3},{3,2},{4,5},{5,4},{6,7},{7,6},{8,9},{9,8},{10,11... | collective-permute-start | bytes 1351688 | tf_op jit(solution)/shard_map/ppermute | solution.py:430
  26.5 9.5 %project.1 = (f32[320,2048]{1,0:T(8,128)S(1)}, bf16[2048,2,512]{2,1,0:T(2,128)(2,1)S(1)}) custom-call(s32[1]{0:T(128)} %bitcast.5.half_ref, bf16[16,160,128]{2,1,0:T(8,128)(2,1)} %get-tuple-element.26.states_ref, bf16[4096,2,2048]{2,1,0:T(2,128)(2,1)} %refs_2_.1), custom_call_target="tpu_custom_call" | custom-call | flops 5368709120 | bytes 33554432 | tf_op jit(solution)/shard_map/project/pallas_call | solution.py:241
  36.0 1.6 %collective-permute-done.2.refs_1_ = bf16[11,160,128]{2,1,0:T(8,128)(2,1)S(1)} collective-permute-done((bf16[11,160,128]{2,1,0:T(8,128)(2,1)S(1)}, bf16[11,160,128]{2,1,0:T(8,128)(2,1)S(1)}, u32[]{:S(2)}, u32[]{:S(2)}) %collective-permute-start.2) | collective-permute-done | bytes 450592 | tf_op jit(solution)/shard_map/ppermute | solution.py:430
  37.6 0.0 copy-start
  37.6 8.6 %project_more.1 = bf16[16,160,256]{2,1,0:T(8,128)(2,1)} custom-call(s32[1]{0:T(128)} %bitcast.4.half_ref, bf16[5,160,128]{2,1,0:T(8,128)(2,1)S(1)} %collective-permute-done.1.refs_0_, bf16[11,160,128]{2,1,0:T(8,128)(2,1)S(1)} %collective-permute-done.2.refs_1_, bf16[4096,2,2048]{2,1,0:T(2,128)(2,1)} %refs_2_.1, ...), custom_call_target="tpu_custom_call" | custom-call | flops 5368709120 | bytes 16777216 | tf_op jit(solution)/shard_map/project_more/pallas_call | solution.py:299
  46.2 0.0 all-to-all-done
  46.2 5.8 %all-to-all-start.1 = ((bf16[16,160,256]{2,1,0:T(8,128)(2,1)}), bf16[16,160,256]{2,1,0:T(8,128)(2,1)S(1)}, u32[]{:S(2)}, u32[]{:S(2)}) async-start(bf16[16,160,256]{2,1,0:T(8,128)(2,1)} %project_more.1), calls=%async_computation.1 | async-start | bytes 2621440 | tf_op jit(solution)/shard_map/all_to_all | solution.py:446
  52.0 0.0 copy-done
  52.0 0.1 broadcast_select_fusion
  52.0 0.1 reshape.17.bias_ref
  52.1 27.2 %all-to-all-done.1 = bf16[16,160,256]{2,1,0:T(8,128)(2,1)S(1)} async-done(((bf16[16,160,256]{2,1,0:T(8,128)(2,1)}), bf16[16,160,256]{2,1,0:T(8,128)(2,1)S(1)}, u32[]{:S(2)}, u32[]{:S(2)}) %all-to-all-start.1) | async-done | bytes 1310752 | tf_op jit(solution)/shard_map/all_to_all | solution.py:446
  79.4 7.5 %attend.1 = bf16[2560,128]{1,0:T(8,128)(2,1)} custom-call(f32[1,2560]{1,0:T(1,128)S(1)} %reshape.17.bias_ref, bf16[2560,128]{1,0:T(8,128)(2,1)S(1)} %bitcast.15, bf16[2560,256]{1,0:T(8,128)(2,1)S(1)} %bitcast.14), custom_call_target="tpu_custom_call" | custom-call | tf_op jit(solution)/shard_map/attend/pallas_call | solution.py:369
  86.8 8.0 %all-to-all-start.2 = ((bf16[16,160,128]{2,1,0:T(8,128)(2,1)}), bf16[16,160,128]{2,1,0:T(8,128)(2,1)S(1)}, u32[]{:S(2)}, u32[]{:S(2)}) async-start(bf16[16,160,128]{2,1,0:T(8,128)(2,1)} %bitcast.7), calls=%async_computation.2 | async-start | bytes 1310720 | tf_op jit(solution)/shard_map/all_to_all | solution.py:448
  94.9 16.6 %all-to-all-done.2 = bf16[16,160,128]{2,1,0:T(8,128)(2,1)S(1)} async-done(((bf16[16,160,128]{2,1,0:T(8,128)(2,1)}), bf16[16,160,128]{2,1,0:T(8,128)(2,1)S(1)}, u32[]{:S(2)}, u32[]{:S(2)}) %all-to-all-start.2) | async-done | bytes 655392 | tf_op jit(solution)/shard_map/all_to_all | solution.py:448
  111.5 1.0 bitcast_select_fusion
  (1 shorter events, 0.0 us)
Async XLA Ops:
  0.9 4.8 %collective-permute-start = (bf16[16,3,2048]{2,0,1:T(8,128)(2,1)S(1)}, bf16[16,3,2048]{2,0,1:T(8,128)(2,1)S(1)}, u32[]{:S(2)}, u32[]{:S(2)}) collective-permute-start(bf16[16,3,2048]{2,0,1:T(8,128)(2,1)S(1)} %slice.11), channel_id=1, source_target_pairs={{2,0},{4,2},{6,4},{8,6},{10,8},{12,10},{14,12},{16,14},{18,16},{20... | collective-permute-start | bytes 589832 | tf_op jit(solution)/shard_map/ppermute | solution.py:418
  9.3 7.5 %collective-permute-start.1 = (bf16[5,160,128]{2,1,0:T(8,128)(2,1)S(1)}, bf16[5,160,128]{2,1,0:T(8,128)(2,1)S(1)}, u32[]{:S(2)}, u32[]{:S(2)}) collective-permute-start(bf16[5,160,128]{2,1,0:T(8,128)(2,1)S(1)} %get-tuple-element.23.refs_0_), channel_id=1, source_target_pairs={{0,1},{1,0},{2,3},{3,2},{4,5},{5,4},{6,7},{7,6},{8,9},{9,8},{10,11... | collective-permute-start | bytes 614408 | tf_op jit(solution)/shard_map/ppermute | solution.py:430
  16.8 29.4 %all-to-all-start = ((bf16[16,160,128]{2,1,0:T(8,128)(2,1)}), bf16[16,160,128]{2,1,0:T(8,128)(2,1)S(1)}, u32[]{:S(2)}, u32[]{:S(2)}) async-start(bf16[16,160,128]{2,1,0:T(8,128)(2,1)} %get-tuple-element.26.states_ref), calls=%async_computation | async-start | bytes 1310720 | tf_op jit(solution)/shard_map/all_to_all | solution.py:440
  24.9 12.7 %collective-permute-start.2 = (bf16[11,160,128]{2,1,0:T(8,128)(2,1)S(1)}, bf16[11,160,128]{2,1,0:T(8,128)(2,1)S(1)}, u32[]{:S(2)}, u32[]{:S(2)}) collective-permute-start(bf16[11,160,128]{2,1,0:T(8,128)(2,1)S(1)} %get-tuple-element.28), channel_id=1, source_target_pairs={{0,1},{1,0},{2,3},{3,2},{4,5},{5,4},{6,7},{7,6},{8,9},{9,8},{10,11... | collective-permute-start | bytes 1351688 | tf_op jit(solution)/shard_map/ppermute | solution.py:430
  37.6 14.4 %copy-start = (s32[16,161]{1,0:T(8,128)S(1)}, s32[16,161]{1,0:T(8,128)}, u32[]{:S(2)}) copy-start(s32[16,161]{1,0:T(8,128)} %bounds_ref.1) | copy-start | bytes 30916
  46.2 33.2 %all-to-all-start.1 = ((bf16[16,160,256]{2,1,0:T(8,128)(2,1)}), bf16[16,160,256]{2,1,0:T(8,128)(2,1)S(1)}, u32[]{:S(2)}, u32[]{:S(2)}) async-start(bf16[16,160,256]{2,1,0:T(8,128)(2,1)} %project_more.1), calls=%async_computation.1 | async-start | bytes 2621440 | tf_op jit(solution)/shard_map/all_to_all | solution.py:446
  86.8 24.6 %all-to-all-start.2 = ((bf16[16,160,128]{2,1,0:T(8,128)(2,1)}), bf16[16,160,128]{2,1,0:T(8,128)(2,1)S(1)}, u32[]{:S(2)}, u32[]{:S(2)}) async-start(bf16[16,160,128]{2,1,0:T(8,128)(2,1)} %bitcast.7), calls=%async_computation.2 | async-start | bytes 1310720 | tf_op jit(solution)/shard_map/all_to_all | solution.py:448

commit v7 on v6

--- a/solution.py
+++ b/solution.py
@@ -32,7 +32,7 @@
 
 
 def outline_body(place_ref, bounds_ref, parts_ref, held_ref, pens, cuts, inside, pick, arrived):
-    load = pltpu.make_async_copy(parts_ref, held_ref, arrived)
+    load = pltpu.make_async_copy(parts_ref.at[:, :, pl.ds(0, held_ref.shape[2])], held_ref, arrived)
     load.start()
     byte_rows = parts_ref.shape[1]
     slots, lanes = inside.shape
@@ -76,7 +76,7 @@
         in_specs=[pl.BlockSpec(memory_space=pltpu.SMEM), in_vmem, anywhere],
         out_specs=[anywhere] + [in_vmem] * 4,
         out_shape=[
-            pltpu.VMEM(parts.shape, parts.dtype),
+            pltpu.VMEM((*parts.shape[:2], parts.shape[2] // 2), parts.dtype),
             pltpu.VMEM((4, rows, HEAD), jnp.float32),
             pltpu.VMEM((4, 8, lanes), jnp.float32),
             pltpu.VMEM((slots, lanes), jnp.float32),
@@ -95,18 +95,24 @@
         held_back = rest_ref.shape[0]
         heads = out_ref.shape[0] - held_back
     else:
-        lead_ref, rest_ref, tops = refs
+        parts_ref, lead_ref, rest_ref, next_ref, tops, arrived = refs
+        run = pl.ds(next_ref.shape[2], next_ref.shape[2])
+        load = pltpu.make_async_copy(parts_ref.at[:, :, run], next_ref, arrived)
+        load.start()
         held_back = 0
         heads = lead_ref.shape[0] + rest_ref.shape[0]
     rows = pens.shape[1]
     lanes = inside.shape[1]
 
     def head_cols(head):
-        return slice((first_head + head) * HEAD, (first_head + head + 1) * HEAD)
+        return slice(head * HEAD, (head + 1) * HEAD)
+
+    def edge_cols(head):
+        return head_cols(first_head + head)
 
     for head in range(heads):
         cols = head_cols(head)
-        top = jnp.concatenate([main_ref[0, :, cols], edge_ref[0, :, cols]], axis=0).astype(jnp.float32)
+        top = jnp.concatenate([main_ref[0, :, cols], edge_ref[0, :, edge_cols(head)]], axis=0).astype(jnp.float32)
         for level in range(4):
             top = jnp.maximum(top, pltpu.roll(top, rows - (1 << level), 0) + pens[level])
         tops[:, head * HEAD : (head + 1) * HEAD] = top.astype(jnp.bfloat16)
@@ -115,7 +121,7 @@
     score_rows = []
     for head in range(heads):
         cols = head_cols(head)
-        keys = jnp.concatenate([main_ref[1, :, cols], edge_ref[1, :, cols], spare], axis=0)
+        keys = jnp.concatenate([main_ref[1, :, cols], edge_ref[1, :, edge_cols(head)], spare], axis=0)
         scores = dot_f32(queries[:, head * HEAD : (head + 1) * HEAD], keys, 1) * inside[...]
         score_rows.append(jnp.sum(scores, axis=0, keepdims=True))
     scores = jnp.concatenate(score_rows + [jnp.zeros((8 - heads, lanes), jnp.float32)] * (heads < 8), axis=0)
@@ -135,7 +141,7 @@
     weights = terms / (fore + back - terms)
     for head in range(heads):
         cols = head_cols(head)
-        values = jnp.concatenate([main_ref[2, :, cols], edge_ref[2, :, cols], spare], axis=0)
+        values = jnp.concatenate([main_ref[2, :, cols], edge_ref[2, :, edge_cols(head)], spare], axis=0)
         spread = (inside[...] * weights[head : head + 1]).astype(jnp.bfloat16)
         states = dot_f32(spread, values).astype(jnp.bfloat16)
         if joins:
@@ -148,9 +154,11 @@
         out_ref[:held_back] = rest_ref[...]
         whole_ref[: lead_ref.shape[0]] = lead_ref[...]
         whole_ref[lead_ref.shape[0] :] = out_ref[...]
-
-
-def patch_states(found, edge, first_head, heads, earlier=()):
+    else:
+        load.wait()
+
+
+def patch_states(found, edge, first_head, heads, parts, earlier=()):
     slots, rows = found[-1].shape
     if earlier:
         counts = (earlier[1].shape[0] + heads, first_head + heads)
@@ -158,15 +166,18 @@
         lead = max(heads * 5 // 8, 1)
         counts = (lead, heads - lead)
     in_vmem = pl.BlockSpec(memory_space=pltpu.VMEM)
+    anywhere = pl.BlockSpec(memory_space=pl.ANY)
+    loads = not earlier
+    out_shape = [jax.ShapeDtypeStruct((count, slots, HEAD), jnp.bfloat16) for count in counts]
     return pl.pallas_call(
         functools.partial(patch_body, first_head, bool(earlier)),
-        in_specs=[in_vmem] * (len(found) + 1 + len(earlier)),
-        out_specs=[in_vmem, in_vmem],
-        out_shape=[jax.ShapeDtypeStruct((count, slots, HEAD), jnp.bfloat16) for count in counts],
-        scratch_shapes=[pltpu.VMEM((rows, heads * HEAD), jnp.bfloat16)],
+        in_specs=[in_vmem] * (len(found) + 1 + len(earlier)) + [anywhere] * loads,
+        out_specs=[in_vmem, in_vmem] + [anywhere] * loads,
+        out_shape=out_shape + [pltpu.VMEM(found[0].shape, found[0].dtype)] * loads,
+        scratch_shapes=[pltpu.VMEM((rows, heads * HEAD), jnp.bfloat16)] + [pltpu.SemaphoreType.DMA] * loads,
         compiler_params=params(20),
         name="patch_states",
-    )(*found, edge, *earlier)
+    )(*found, edge, *earlier, *([parts] if loads else []))
 
 
 def column_block(width):
@@ -420,14 +431,14 @@
     edge = edge.transpose(1, 0, 2)
     in_hbm = functools.partial(pltpu.with_memory_space_constraint, memory_space=pltpu.HBM)
     found = outline(place[None], in_hbm(patch_bounds), in_hbm(parts), slots)
-    byte_phase = functools.partial(patch_states, found, edge)
     run = heads // 2
-    first = byte_phase(0, run)
-    rest, states = byte_phase(run, run, first)
+    lead, held_back, second = patch_states(found, edge, 0, run, in_hbm(parts))
+    found[0] = pltpu.with_memory_space_constraint(second, pltpu.VMEM)
+    rest, states = patch_states(found, edge, run, run, None, (lead, held_back))
 
     paired = ctx_count == heads
     if mp_count == 2:
-        others = [lax.ppermute(run_states, "mp", [(0, 1), (1, 0)]) for run_states in (first[0], rest)]
+        others = [lax.ppermute(run_states, "mp", [(0, 1), (1, 0)]) for run_states in (lead, rest)]
         before, held = project(half[None], states, kv_weight)
         other_half = 1 - half
     else:

time: 113 us -> 115 us (1.018)
    pallas_call x2, Pallas kernels: 7.93 us -> 9.63 us  [patch_states(): pl.pallas_call(functools.partial(patch_body, first_head, bool(earlier)),...]
  transfers between devices with their start and end apart: 6 -> 6, of which waited for: 3 -> 3; matrix products, arithmetic and copies ran while one was open for 0% -> 0% of each run, Pallas kernels for 23% -> 22%
where the time goes in v7:
time: 115 us; the launch traced here: 114 us
  waiting for transfers between devices  45.4 us (39%)
  Pallas kernels  37.8 us (33%)
  starting transfers between devices  28.7 us (25%)
    all_to_all x1, waiting for transfers between devices, shards(): lax.all_to_all(kv, 'ctx', 0, 0, tiled=True)  27.2 us
    all_to_all x1, waiting for transfers between devices, shards(): mixed = lax.all_to_all(mixed, 'ctx', 0, 0, tiled=True)  16.6 us
    pallas_call x2, Pallas kernels, patch_states(): pl.pallas_call(functools.partial(patch_body, first_head, bool(earlier)),...  9.63 us
    pallas_call x1, Pallas kernels, project(): pl.pallas_call(project_body, in_specs=[pl.BlockSpec(memory_space=pltpu.SM...  9.48 us
    all_to_all x1, starting transfers between devices, shards(): lax.all_to_all(sent, 'ctx', 0, 0, tiled=True)  8.98 us
    pallas_call x1, Pallas kernels, project_more(): pl.pallas_call(functools.partial(project_more_body, len(states)), in_spec...  8.59 us
    all_to_all x1, starting transfers between devices, shards(): mixed = lax.all_to_all(mixed, 'ctx', 0, 0, tiled=True)  8.01 us
    pallas_call x1, Pallas kernels, attend(): pl.pallas_call(functools.partial(attend_body, block), out_shape=jax.Shape...  7.47 us
  transfers between devices with their start and end apart: 6, of which 3 were waited for; matrix products, arithmetic and copies ran while one was open for 0% of the time, Pallas kernels for 22%

profile of v7, /device:TPU:0, one launch (start us, length us, event | category | flops | bytes accessed | tf_op | source)
XLA Modules:
  0.0 114.2 jit_solution(3292635348152012774)
XLA Ops:
  0.0 0.9 slice.11
  0.9 1.3 %collective-permute-start = (bf16[16,3,2048]{2,0,1:T(8,128)(2,1)S(1)}, bf16[16,3,2048]{2,0,1:T(8,128)(2,1)S(1)}, u32[]{:S(2)}, u32[]{:S(2)}) collective-permute-start(bf16[16,3,2048]{2,0,1:T(8,128)(2,1)S(1)} %slice.11), channel_id=1, source_target_pairs={{2,0},{4,2},{6,4},{8,6},{10,8},{12,10},{14,12},{16,14},{18,16},{20... | collective-permute-start | bytes 589832 | tf_op jit(solution)/shard_map/ppermute | solution.py:429
  2.2 2.6 %outline.1 = (bf16[3,512,1024]{2,1,0:T(8,128)(2,1)S(1)}, f32[4,528,128]{2,1,0:T(8,128)S(1)}, f32[4,8,640]{2,1,0:T(8,128)S(1)}, f32[160,640]{1,0:T(8,128)S(1)}, bf16[160,528]{1,0:T(8,128)(2,1)S(1)}) custom-call(s32[1]{0:T(128)} %bitcast.place_ref, s32[16,161]{1,0:T(8,128)} %bounds_ref.1, bf16[3,512,2048]{2,1,0:T(8,128)(2,1)} %bitcast.18), custom_call_target="tpu_custom_call" | custom-call | tf_op jit(solution)/shard_map/outline/pallas_call | solution.py:74
  4.9 0.0 collective-permute-done
  4.9 5.2 %patch_states.2 = (bf16[5,160,128]{2,1,0:T(8,128)(2,1)S(1)}, bf16[3,160,128]{2,1,0:T(8,128)(2,1)S(1)}, bf16[3,512,1024]{2,1,0:T(8,128)(2,1)S(1)}) custom-call(bf16[3,512,1024]{2,1,0:T(8,128)(2,1)S(1)} %get-tuple-element.19.main_ref, f32[4,528,128]{2,1,0:T(8,128)S(1)} %get-tuple-element.20.pens, f32[4,8,640]{2,1,0:T(8,128)S(1)} %get-tuple-element.21.cuts, ...), custom_call_target="tpu_custom_call" | custom-call | tf_op jit(solution)/shard_map/patch_states/pallas_call | solution.py:172
  10.1 3.0 %collective-permute-start.1 = (bf16[5,160,128]{2,1,0:T(8,128)(2,1)S(1)}, bf16[5,160,128]{2,1,0:T(8,128)(2,1)S(1)}, u32[]{:S(2)}, u32[]{:S(2)}) collective-permute-start(bf16[5,160,128]{2,1,0:T(8,128)(2,1)S(1)} %get-tuple-element.25.refs_0_), channel_id=1, source_target_pairs={{0,1},{1,0},{2,3},{3,2},{4,5},{5,4},{6,7},{7,6},{8,9},{9,8},{10,11... | collective-permute-start | bytes 614408 | tf_op jit(solution)/shard_map/ppermute | solution.py:441
  13.2 4.4 %patch_states.3 = (bf16[11,160,128]{2,1,0:T(8,128)(2,1)S(1)}, bf16[16,160,128]{2,1,0:T(8,128)(2,1)}) custom-call(bf16[3,512,1024]{2,1,0:T(8,128)(2,1)S(1)} %get-tuple-element.24.main_ref, f32[4,528,128]{2,1,0:T(8,128)S(1)} %get-tuple-element.20.pens, f32[4,8,640]{2,1,0:T(8,128)S(1)} %get-tuple-element.21.cuts, f32[160,640]{1,0:T(8,128)S(1)} %get-tuple-element.22.inside, ...), custom_call_target="tpu_custom_call" | custom-call | tf_op jit(solution)/shard_map/patch_states/pallas_call | solution.py:172
  17.6 0.0 collective-permute-done.1.refs_0_
  17.6 9.0 %all-to-all-start = ((bf16[16,160,128]{2,1,0:T(8,128)(2,1)}), bf16[16,160,128]{2,1,0:T(8,128)(2,1)S(1)}, u32[]{:S(2)}, u32[]{:S(2)}) async-start(bf16[16,160,128]{2,1,0:T(8,128)(2,1)} %get-tuple-element.28.states_ref), calls=%async_computation | async-start | bytes 1310720 | tf_op jit(solution)/shard_map/all_to_all | solution.py:451
  26.6 1.6 %collective-permute-start.2 = (bf16[11,160,128]{2,1,0:T(8,128)(2,1)S(1)}, bf16[11,160,128]{2,1,0:T(8,128)(2,1)S(1)}, u32[]{:S(2)}, u32[]{:S(2)}) collective-permute-start(bf16[11,160,128]{2,1,0:T(8,128)(2,1)S(1)} %get-tuple-element.30), channel_id=1, source_target_pairs={{0,1},{1,0},{2,3},{3,2},{4,5},{5,4},{6,7},{7,6},{8,9},{9,8},{10,11... | collective-permute-start | bytes 1351688 | tf_op jit(solution)/shard_map/ppermute | solution.py:441
  28.2 9.5 %project.1 = (f32[320,2048]{1,0:T(8,128)S(1)}, bf16[2048,2,512]{2,1,0:T(2,128)(2,1)S(1)}) custom-call(s32[1]{0:T(128)} %bitcast.5.half_ref, bf16[16,160,128]{2,1,0:T(8,128)(2,1)} %get-tuple-element.28.states_ref, bf16[4096,2,2048]{2,1,0:T(2,128)(2,1)} %refs_2_.1), custom_call_target="tpu_custom_call" | custom-call | flops 5368709120 | bytes 33554432 | tf_op jit(solution)/shard_map/project/pallas_call | solution.py:252
  37.7 1.6 %collective-permute-done.2.refs_1_ = bf16[11,160,128]{2,1,0:T(8,128)(2,1)S(1)} collective-permute-done((bf16[11,160,128]{2,1,0:T(8,128)(2,1)S(1)}, bf16[11,160,128]{2,1,0:T(8,128)(2,1)S(1)}, u32[]{:S(2)}, u32[]{:S(2)}) %collective-permute-start.2) | collective-permute-done | bytes 450592 | tf_op jit(solution)/shard_map/ppermute | solution.py:441
  39.3 0.0 copy-start
  39.3 8.6 %project_more.1 = bf16[16,160,256]{2,1,0:T(8,128)(2,1)} custom-call(s32[1]{0:T(128)} %bitcast.4.half_ref, bf16[5,160,128]{2,1,0:T(8,128)(2,1)S(1)} %collective-permute-done.1.refs_0_, bf16[11,160,128]{2,1,0:T(8,128)(2,1)S(1)} %collective-permute-done.2.refs_1_, bf16[4096,2,2048]{2,1,0:T(2,128)(2,1)} %refs_2_.1, ...), custom_call_target="tpu_custom_call" | custom-call | flops 5368709120 | bytes 16777216 | tf_op jit(solution)/shard_map/project_more/pallas_call | solution.py:310
  47.9 0.0 all-to-all-done
  47.9 5.8 %all-to-all-start.1 = ((bf16[16,160,256]{2,1,0:T(8,128)(2,1)}), bf16[16,160,256]{2,1,0:T(8,128)(2,1)S(1)}, u32[]{:S(2)}, u32[]{:S(2)}) async-start(bf16[16,160,256]{2,1,0:T(8,128)(2,1)} %project_more.1), calls=%async_computation.1 | async-start | bytes 2621440 | tf_op jit(solution)/shard_map/all_to_all | solution.py:457
  53.6 0.0 copy-done
  53.7 0.1 broadcast_select_fusion
  53.7 0.1 reshape.17.bias_ref
  53.8 27.2 %all-to-all-done.1 = bf16[16,160,256]{2,1,0:T(8,128)(2,1)S(1)} async-done(((bf16[16,160,256]{2,1,0:T(8,128)(2,1)}), bf16[16,160,256]{2,1,0:T(8,128)(2,1)S(1)}, u32[]{:S(2)}, u32[]{:S(2)}) %all-to-all-start.1) | async-done | bytes 1310752 | tf_op jit(solution)/shard_map/all_to_all | solution.py:457
  81.1 7.5 %attend.1 = bf16[2560,128]{1,0:T(8,128)(2,1)} custom-call(f32[1,2560]{1,0:T(1,128)S(1)} %reshape.17.bias_ref, bf16[2560,128]{1,0:T(8,128)(2,1)S(1)} %bitcast.15, bf16[2560,256]{1,0:T(8,128)(2,1)S(1)} %bitcast.14), custom_call_target="tpu_custom_call" | custom-call | tf_op jit(solution)/shard_map/attend/pallas_call | solution.py:380
  88.5 8.0 %all-to-all-start.2 = ((bf16[16,160,128]{2,1,0:T(8,128)(2,1)}), bf16[16,160,128]{2,1,0:T(8,128)(2,1)S(1)}, u32[]{:S(2)}, u32[]{:S(2)}) async-start(bf16[16,160,128]{2,1,0:T(8,128)(2,1)} %bitcast.7), calls=%async_computation.2 | async-start | bytes 1310720 | tf_op jit(solution)/shard_map/all_to_all | solution.py:459
  96.6 16.6 %all-to-all-done.2 = bf16[16,160,128]{2,1,0:T(8,128)(2,1)S(1)} async-done(((bf16[16,160,128]{2,1,0:T(8,128)(2,1)}), bf16[16,160,128]{2,1,0:T(8,128)(2,1)S(1)}, u32[]{:S(2)}, u32[]{:S(2)}) %all-to-all-start.2) | async-done | bytes 655392 | tf_op jit(solution)/shard_map/all_to_all | solution.py:459
  113.1 1.0 bitcast_select_fusion
  (1 shorter events, 0.0 us)
Async XLA Ops:
  0.9 3.9 %collective-permute-start = (bf16[16,3,2048]{2,0,1:T(8,128)(2,1)S(1)}, bf16[16,3,2048]{2,0,1:T(8,128)(2,1)S(1)}, u32[]{:S(2)}, u32[]{:S(2)}) collective-permute-start(bf16[16,3,2048]{2,0,1:T(8,128)(2,1)S(1)} %slice.11), channel_id=1, source_target_pairs={{2,0},{4,2},{6,4},{8,6},{10,8},{12,10},{14,12},{16,14},{18,16},{20... | collective-permute-start | bytes 589832 | tf_op jit(solution)/shard_map/ppermute | solution.py:429
  10.1 7.4 %collective-permute-start.1 = (bf16[5,160,128]{2,1,0:T(8,128)(2,1)S(1)}, bf16[5,160,128]{2,1,0:T(8,128)(2,1)S(1)}, u32[]{:S(2)}, u32[]{:S(2)}) collective-permute-start(bf16[5,160,128]{2,1,0:T(8,128)(2,1)S(1)} %get-tuple-element.25.refs_0_), channel_id=1, source_target_pairs={{0,1},{1,0},{2,3},{3,2},{4,5},{5,4},{6,7},{7,6},{8,9},{9,8},{10,11... | collective-permute-start | bytes 614408 | tf_op jit(solution)/shard_map/ppermute | solution.py:441
  17.6 30.3 %all-to-all-start = ((bf16[16,160,128]{2,1,0:T(8,128)(2,1)}), bf16[16,160,128]{2,1,0:T(8,128)(2,1)S(1)}, u32[]{:S(2)}, u32[]{:S(2)}) async-start(bf16[16,160,128]{2,1,0:T(8,128)(2,1)} %get-tuple-element.28.states_ref), calls=%async_computation | async-start | bytes 1310720 | tf_op jit(solution)/shard_map/all_to_all | solution.py:451
  26.6 12.7 %collective-permute-start.2 = (bf16[11,160,128]{2,1,0:T(8,128)(2,1)S(1)}, bf16[11,160,128]{2,1,0:T(8,128)(2,1)S(1)}, u32[]{:S(2)}, u32[]{:S(2)}) collective-permute-start(bf16[11,160,128]{2,1,0:T(8,128)(2,1)S(1)} %get-tuple-element.30), channel_id=1, source_target_pairs={{0,1},{1,0},{2,3},{3,2},{4,5},{5,4},{6,7},{7,6},{8,9},{9,8},{10,11... | collective-permute-start | bytes 1351688 | tf_op jit(solution)/shard_map/ppermute | solution.py:441
  39.3 14.4 %copy-start = (s32[16,161]{1,0:T(8,128)S(1)}, s32[16,161]{1,0:T(8,128)}, u32[]{:S(2)}) copy-start(s32[16,161]{1,0:T(8,128)} %bounds_ref.1) | copy-start | bytes 30916
  47.9 33.2 %all-to-all-start.1 = ((bf16[16,160,256]{2,1,0:T(8,128)(2,1)}), bf16[16,160,256]{2,1,0:T(8,128)(2,1)S(1)}, u32[]{:S(2)}, u32[]{:S(2)}) async-start(bf16[16,160,256]{2,1,0:T(8,128)(2,1)} %project_more.1), calls=%async_computation.1 | async-start | bytes 2621440 | tf_op jit(solution)/shard_map/all_to_all | solution.py:457
  88.5 24.6 %all-to-all-start.2 = ((bf16[16,160,128]{2,1,0:T(8,128)(2,1)}), bf16[16,160,128]{2,1,0:T(8,128)(2,1)S(1)}, u32[]{:S(2)}, u32[]{:S(2)}) async-start(bf16[16,160,128]{2,1,0:T(8,128)(2,1)} %bitcast.7), calls=%async_computation.2 | async-start | bytes 1310720 | tf_op jit(solution)/shard_map/all_to_all | solution.py:459
